TPU v7x, 32 devices: a whole 2x2x4 slice. The times are simulated.
32 devices in a mesh: ctx: 8 (over z, x), head: 4 (over y, core).
Axes of the slice: x: 2, y: 2, z: 4, core: 2. Of those that a mesh axis runs over, the one named last changes fastest.
Arguments:
- queries: float32 [2048, 4096], P('ctx', 'head'), may hold values from -48 to 48
- keys: float32 [2048, 4096], P('ctx', 'head'), may hold values from -48 to 48
- values: float32 [2048, 4096], P('ctx', 'head'), may hold values from -8 to 8
- query_map: float32 [32, 128, 128], P('head'), may hold values from -2 to 2
- key_map: float32 [32, 128, 128], P('head'), may hold values from -2 to 2
- out_weight: float32 [4096, 4096], P(None, ('ctx', 'head')), may hold values from -0.09375 to 0.09375
- residual: float32 [2048, 4096], P('ctx', 'head'), may hold values from -1.5 to 1.5
Outputs:
- layer_out: float32 [2048, 4096], P('ctx', 'head')
All inputs are finite; a program needn't handle non-finite values.
Results may differ from a plain program's by a relative error of at most 0.0001.
Values sent between devices are 32-bit elements; how exact they have to be, the bound alone decides.
No kernel may reach another device: no remote copies, remote signals or barrier semaphores. Data moves between devices by JAX's collectives and lax.ppermute only.
A program may use at most 192 MiB of HBM per device.

v0:
```python
import functools

import numpy as np

import jax
import jax.numpy as jnp
from jax import lax
from jax.experimental import pallas as pl
from jax.experimental.pallas import tpu as pltpu
from jax.sharding import PartitionSpec as P

HIGH = lax.Precision.HIGHEST
together = lax.optimization_barrier
AXES = ("ctx", "head")
PAIR = 2
EXTRA = 8
MIB = 1024 * 1024


def split(x):
    high = x.astype(jnp.bfloat16)
    return high, (x - high.astype(jnp.float32)).astype(jnp.bfloat16)


def dot3(a, b, dims=(((1,), (0,)), ((), ()))):
    a_high, a_low = split(a)
    b_high, b_low = split(b)
    dot = functools.partial(lax.dot_general, dimension_numbers=dims, preferred_element_type=jnp.float32)
    return dot(a_high, b_high) + (dot(a_high, b_low) + dot(a_low, b_high))


def features(rows, weights):
    scores = jnp.dot(rows, weights, precision=HIGH, preferred_element_type=jnp.float32)
    up = jnp.exp(scores - jnp.max(scores, axis=-1, keepdims=True))
    down = jnp.exp(jnp.min(scores, axis=-1, keepdims=True) - scores)
    up = up / jnp.sum(up, axis=-1, keepdims=True)
    down = down / jnp.sum(down, axis=-1, keepdims=True)
    return jnp.concatenate([up, down], axis=-1)


def key_kernel(first, k_ref, map_ref, v_ref, state_ref, feat_ref):
    heads, head_size, feat_half = map_ref.shape
    size = 2 * feat_half
    row = lax.broadcasted_iota(jnp.int32, (EXTRA, feat_half), 0)
    for i in range(heads):
        columns = slice(i * head_size, (i + 1) * head_size)
        feat = features(k_ref[:, columns], map_ref[i])
        feat_ref[i] = feat
        state_ref[i, :size, :] = dot3(feat, v_ref[:, columns], (((0,), (0,)), ((), ())))
        norm = jnp.sum(feat, axis=0, keepdims=True)
        state_ref[i, size:, :] = jnp.where(row < EXTRA // 2, norm[:, :feat_half], norm[:, feat_half:])


def attend(feat, key_feat, values, numer_ref, denom_ref):
    weights = dot3(feat, key_feat, (((1,), (1,)), ((), ())))
    row = lax.broadcasted_iota(jnp.int32, weights.shape, 0)
    column = lax.broadcasted_iota(jnp.int32, weights.shape, 1)
    weights = jnp.where(column <= row, weights, 0.0)
    numer_ref[0] = dot3(weights, values)
    denom_ref[0] = jnp.broadcast_to(jnp.sum(weights, axis=-1, keepdims=True), denom_ref.shape[1:])


def rest_kernel(first, *refs):
    k_ref, k_map_ref, q_ref, q_map_ref, v_ref, other_q_ref, other_q_map_ref, other_v_ref, other_feat_ref = refs[:9]
    state_ref, feat_ref, numer_ref, denom_ref, other_out_ref, other_numer_ref, other_denom_ref = refs[9:]
    heads, head_size, feat_half = k_map_ref.shape
    size = 2 * feat_half
    row = lax.broadcasted_iota(jnp.int32, (EXTRA, feat_half), 0)
    key_feat = features(k_ref[...], k_map_ref[0])
    state_ref[0, :size, :] = dot3(key_feat, v_ref[...], (((0,), (0,)), ((), ())))
    norm = jnp.sum(key_feat, axis=0, keepdims=True)
    state_ref[0, size:, :] = jnp.where(row < EXTRA // 2, norm[:, :feat_half], norm[:, feat_half:])
    feat = features(q_ref[...], q_map_ref[0])
    feat_ref[0] = feat
    attend(feat, key_feat, v_ref[...], numer_ref, denom_ref)
    feat = features(other_q_ref[...], other_q_map_ref[0])
    other_out_ref[0] = feat
    attend(feat, other_feat_ref[0], other_v_ref[...], other_numer_ref, other_denom_ref)


def mix_kernel(qfeat_ref, numer_ref, denom_ref, prior_ref, out_ref):
    feat = qfeat_ref[0]
    size = feat.shape[1]
    norm = jnp.concatenate(
        [prior_ref[0, size : size + 1, :], prior_ref[0, size + EXTRA // 2 : size + EXTRA // 2 + 1, :]], axis=1
    )
    denom = denom_ref[0] + jnp.sum(feat * norm, axis=-1, keepdims=True)
    out_ref[...] = (numer_ref[0] + dot3(feat, prior_ref[0, :size, :])) / denom


def project_kernel(terms, units, *refs):
    rows_refs, refs = refs[: 2 * units], refs[2 * units :]
    count = sum(stop - start for _, start, stop in terms)
    w_refs, rest, out_ref = refs[:count], refs[count:-1], refs[-1]
    out_ref[...] = rest[0][...] if rest else jnp.zeros_like(out_ref)
    lanes = w_refs[0].shape[1]
    for unit, start, stop in terms:
        a = jnp.concatenate([rows_refs[2 * unit][...], rows_refs[2 * unit + 1][...]], axis=0)
        w = jnp.concatenate([ref[...] for ref in w_refs[: stop - start]], axis=1)
        w_refs = w_refs[stop - start :]
        out_ref[:, start * lanes : stop * lanes] += dot3(a, w)


def pieces_of(product, groups, width):
    rows = product.shape[0] // 2
    return [
        jnp.concatenate([product[d * rows : (d + 1) * rows, b * width : (b + 1) * width] for b in group], axis=1)
        for d in range(2)
        for group in groups
    ]


def route_kernel(groups, width, send, mine_ref, other_ref, *refs):
    out_refs, pieces_ref = refs[:-1], refs[-1]
    product = mine_ref[...] + other_ref[...]
    for j, piece in enumerate(pieces_of(product, groups, width)):
        pieces_ref[j] = piece
    for k, out_ref in enumerate(out_refs):
        out_ref[...] = pieces_ref[send[k]]


def assemble_kernel(size, place, *refs):
    arrived, (residual_ref, out_ref, blocks_ref) = refs[:-3], refs[-3:]
    width = blocks_ref.shape[2]
    for k, ref in enumerate(arrived):
        for b in range(size):
            blocks_ref[k * size + b] = ref[:, b * width : (b + 1) * width]
    for p in range(blocks_ref.shape[0]):
        columns = slice(p * width, (p + 1) * width)
        out_ref[:, columns] = residual_ref[:, columns] + blocks_ref[place[p]]


def route_tables(ctx, heads, rels):
    groups = {}
    for column, rel in enumerate(rels):
        groups.setdefault(rel * heads // ctx, []).append(column)
    groups = [groups[key] for key in sorted(groups)]
    size = len(groups[0])
    targets = {}
    for c in range(ctx):
        for h in range(heads):
            found = {}
            for d, step in enumerate((0, PAIR)):
                for g, columns in enumerate(groups):
                    to = (c ^ step) * heads + (c ^ rels[columns[0]]) * heads // ctx
                    found[to] = d * len(groups) + g
            targets[c * heads + h] = found
    classes = {}
    for device in sorted(targets):
        classes.setdefault(tuple(sorted(targets[device])), []).append(device)
    steps = 2 * len(groups)
    perms = [[] for _ in range(steps)]
    send = np.zeros((ctx * heads, steps), np.int32)
    arrives = {}
    for ends, sources in classes.items():
        for i, source in enumerate(sources):
            for k in range(steps):
                to = ends[i ^ k]
                perms[k].append((source, to))
                send[source, k] = targets[source][to]
                arrives[to, source] = k
    place = np.zeros((ctx * heads, ctx), np.int32)
    for c in range(ctx):
        for h in range(heads):
            for p in range(ctx):
                column_ctx, source_h = divmod(h * ctx + p, heads)
                source_c = (c & ~PAIR) | (column_ctx & PAIR)
                k = arrives[c * heads + h, source_c * heads + source_h]
                rel = source_c ^ column_ctx
                group = [g for g in groups if rels.index(rel) in g][0]
                place[c * heads + h, p] = k * size + group.index(rels.index(rel))
    return groups, perms, send, place


def body(ctx, heads, queries, keys, values, query_map, key_map, out_weight, residual):
    rows = queries.shape[0]
    heads_here, head_size, feat_half = query_map.shape
    feat_size = 2 * feat_half
    half = heads_here // 2
    wide = half * head_size
    depth = out_weight.shape[0] // heads
    strip_width = out_weight.shape[1]
    c = lax.axis_index("ctx")
    h = lax.axis_index("head")
    me = c * heads + h
    odd = c & 1

    def swap(x, by_ctx, by_head=0, keep=lambda c: True):
        pairs = [
            (i * heads + j, (i ^ by_ctx) * heads + (j ^ by_head))
            for i in range(ctx)
            for j in range(heads)
            if keep(i)
        ]
        return lax.ppermute(x, AXES, pairs)

    def of(*shape):
        return jax.ShapeDtypeStruct(shape, jnp.float32)

    def cost(products, count, exps=0):
        return pl.CostEstimate(flops=2 * products, bytes_accessed=4 * count, transcendentals=exps)

    def params(mib):
        return pltpu.CompilerParams(vmem_limit_bytes=mib * MIB)

    def head_block(size, lanes):
        return pl.BlockSpec((1, size, lanes), lambda i, *_: (i, 0, 0))

    def key_part(first):
        columns = pl.BlockSpec((rows, wide), lambda i, first: (0, first[0]))
        maps = pl.BlockSpec((half, head_size, feat_half), lambda i, first: (first[0], 0, 0))
        shapes = [of(half, feat_size + EXTRA, head_size), of(half, rows, feat_size)]
        return pl.pallas_call(
            key_kernel,
            grid_spec=pltpu.PrefetchScalarGridSpec(
                num_scalar_prefetch=1,
                grid=(1,),
                in_specs=[columns, maps, columns],
                out_specs=[pl.BlockSpec(s.shape, lambda i, first: (0, 0, 0)) for s in shapes],
            ),
            out_shape=shapes,
            compiler_params=params(60),
            name="key_part",
            cost_estimate=cost(
                6 * half * rows * head_size * (feat_half + feat_size),
                half * rows * (2 * head_size + 2 * feat_size),
                half * rows * feat_size,
            ),
        )(first, keys, key_map, values)

    def rest_part(firsts, other_feat):
        def columns(which):
            return pl.BlockSpec((rows, head_size), lambda i, first: (0, first[which] * half + i))

        def maps(which):
            return pl.BlockSpec((1, head_size, feat_half), lambda i, first: (first[which] * half + i, 0, 0))

        query_shapes = [of(half, rows, feat_size), of(half, rows, head_size), of(half, rows, head_size)]
        shapes = [of(half, feat_size + EXTRA, head_size), *query_shapes, *query_shapes]
        outs = pl.pallas_call(
            rest_kernel,
            grid_spec=pltpu.PrefetchScalarGridSpec(
                num_scalar_prefetch=1,
                grid=(half,),
                in_specs=[columns(0), maps(0), columns(0), maps(0), columns(0)]
                + [columns(1), maps(1), columns(1), head_block(rows, feat_size)],
                out_specs=[head_block(*shape.shape[1:]) for shape in shapes],
            ),
            out_shape=shapes,
            compiler_params=params(40),
            name="rest_part",
            cost_estimate=cost(
                6 * half * rows * (head_size * (3 * feat_half + feat_size) + 2 * rows * (feat_size + head_size)),
                half * rows * (8 * head_size + 4 * feat_size),
                3 * half * rows * feat_size,
            ),
        )(firsts, keys, key_map, queries, query_map, values, queries, query_map, values, other_feat)
        return outs[0], outs[1:4], outs[4:]

    def mix(qfeat, numer, denom, prior):
        return pl.pallas_call(
            mix_kernel,
            grid=(half,),
            in_specs=[
                head_block(rows, feat_size),
                head_block(rows, head_size),
                head_block(rows, head_size),
                head_block(feat_size + EXTRA, head_size),
            ],
            out_specs=pl.BlockSpec((rows, head_size), lambda i: (0, i)),
            out_shape=of(rows, wide),
            compiler_params=params(12),
            name="mix",
            cost_estimate=cost(
                3 * half * rows * feat_size * head_size, half * rows * (3 * head_size + 2 * feat_size)
            ),
        )(qfeat, numer, denom, prior)

    even = range(0, heads, 2)
    blocks = heads // 2
    quarter = 2 * blocks // 4 * wide
    bits = [1 << b for b in reversed(range(ctx.bit_length() - 1)) if 1 << b != PAIR]
    far, near = bits[-2:]
    rels = [0]
    for bit in bits[:-2]:
        rels = rels + [r | bit for r in rels]
    rels = [r | s for s in (0, near, far, far | near) for r in rels]

    def rows_of(weight, flip, some):
        starts = [(h ^ flip ^ d) * depth + which * wide for which, d in some]
        return jnp.concatenate([lax.dynamic_slice_in_dim(weight, start, wide, 0) for start in starts])

    def widen(x):
        for bit in bits[:-2]:
            x = jnp.concatenate([x, swap(x, bit)], axis=1)
        return x

    def quarters(x):
        return [x[i : i + quarter] for i in range(0, x.shape[0], quarter)]

    order = [(which, d) for which in (odd, 1 - odd) for d in even]
    part = len(order) // 4
    own, other = odd.reshape(1), (1 - odd).reshape(1)
    kept_first = widen(rows_of(out_weight, 0, order[:part]))
    far_1 = swap(kept_first, far)
    other_state, other_feat = key_part(other)
    out_weight, other_state = together((out_weight, other_state))
    kept_rest = widen(rows_of(out_weight, 0, order[part:]))
    from_neighbour = swap(other_state, 1)
    own_state, own_query, other_query = rest_part(jnp.concatenate([own, other]), other_feat)
    groups, perms, send, place = route_tables(ctx, heads, rels)
    steps, size = len(perms), len(groups[0])
    send_here = jnp.asarray(send)[me]
    place_here = jnp.asarray(place)[me]

    from_neighbour, own_state, far_1, kept_first, kept_rest, out_weight = together(
        (from_neighbour, own_state, far_1, kept_first, kept_rest, out_weight)
    )
    far_2 = swap(kept_rest[: 2 * quarter], far)
    kept = jnp.concatenate([kept_first, kept_rest])
    kept_near = swap(kept, near)
    taken = widen(swap(rows_of(out_weight, 1, order), 0, 1))
    earlier = jnp.where(odd == 0, own_state, from_neighbour)
    total = own_state + from_neighbour
    before = jnp.zeros_like(total)
    bit = 2
    while 2 * bit < ctx:
        got = swap(total, bit)
        before = before + jnp.where((c & bit) != 0, got, 0.0)
        total = total + got
        bit *= 2
    total, before, far_2, kept_near, taken = together((total, before, far_2, kept_near, taken))
    taken_near = swap(taken, near)
    second = (c & PAIR) != 0
    got = swap(jnp.where(second, total[half // 2 :], total[: half // 2]), bit, keep=lambda i: not i & bit)
    taken_parts = quarters(taken)
    got, taken_parts[0] = together((got, taken_parts[0]))
    met = swap(got, PAIR, keep=lambda i: i & bit)
    far_3 = swap(taken_parts[0], far)
    got = jnp.concatenate([jnp.where(second, met, got), jnp.where(second, got, met)])
    got, far_3, taken_near, taken_parts[1], send_here, place_here = together(
        (got, far_3, taken_near, taken_parts[1], send_here, place_here)
    )
    before = before + got

    other_prior = swap(before + jnp.where(odd == 0, earlier, 0.0), 1)
    own_mixed = mix(*own_query, before + jnp.where(odd == 1, earlier, 0.0))
    head_bits = [1 << b for b in range(1, heads.bit_length() - 1)]

    def spread(own, met, across, last):
        pieces = {(0, 0): own, (PAIR, 0): met, (0, head_bits[0]): across, (PAIR, head_bits[0]): last}
        for bit in head_bits[1:]:
            pieces.update({(d, j | bit): swap(pieces[d, j], 0, bit) for d, j in list(pieces)})
        return [pieces[d, j] for d in (0, PAIR) for j in even]

    met, across = swap(own_mixed, PAIR), swap(own_mixed, 0, head_bits[0])
    far_4 = swap(taken_parts[1], far)
    next_part = taken[2 * quarter :]
    other_prior, far_1, far_2, far_3, far_4, met, across, next_part = together(
        (other_prior, far_1, far_2, far_3, far_4, met, across, next_part)
    )
    own_pieces = spread(own_mixed, met, across, swap(met, 0, head_bits[0]))
    other_mixed = mix(*other_query, other_prior)
    met, across = swap(other_mixed, PAIR), swap(other_mixed, 0, head_bits[0])
    far_5 = swap(next_part, far)
    both_1 = swap(jnp.concatenate([far_1, far_2, far_3, far_4]), near)
    met, across, far_5, both_1, kept_rest = together((met, across, far_5, both_1, kept_rest))
    far_6 = swap(kept_rest[2 * quarter :], far)
    both_2 = swap(far_5, near)
    other_pieces = spread(other_mixed, met, across, swap(met, 0, head_bits[0]))

    lanes = kept.shape[1]

    def strip(parts, crossed=False):
        places = [(x, start * part + i) for x, start, stop in parts for i in range((stop - start) * part)]
        return places[blocks:] + places[:blocks] if crossed else places

    def strips_of(last_far, last_both):
        theirs = [
            strip([(taken, 0, 4)]),
            strip([(taken_near, 0, 4)], True),
            strip([(far_3, 0, 1), (far_4, 0, 1), (far_5, 0, 2)]),
            strip([(both_1, 3, 5), (both_2, 0, 2)], True),
        ]
        mine = [
            strip([(kept, 0, 4)]),
            strip([(kept_near, 0, 4)], True),
            strip([(far_1, 0, 1), (far_2, 0, 2), (last_far, 0, 1)]),
            strip([(both_1, 0, 3), (last_both, 0, 1)], True),
        ]
        return theirs, mine

    def project(pieces, strips, runs, total=None, column=0):
        runs = [(u, start, stop) for q, start, stop in runs for u in range(q * part, (q + 1) * part)]
        used = sorted({u for u, _, _ in runs})
        weights = [strips[s][u] for u, start, stop in runs for s in range(start, stop)]
        shape = (2 * rows, len(strips) * lanes)
        extra = [] if total is None else [total]
        terms = [(used.index(u), start, stop) for u, start, stop in runs]
        return pl.pallas_call(
            functools.partial(project_kernel, terms, len(used)),
            grid=(1,),
            in_specs=[pl.BlockSpec((rows, wide), lambda i: (0, 0))] * (2 * len(used))
            + [pl.BlockSpec((wide, lanes), lambda i, unit=unit: (unit, 0)) for _, unit in weights]
            + [pl.BlockSpec(shape, lambda i: (0, column))] * len(extra),
            out_specs=pl.BlockSpec(shape, lambda i: (0, 0)),
            out_shape=of(*shape),
            compiler_params=params(24),
            name="project",
            cost_estimate=cost(6 * rows * wide * len(weights) * lanes, wide * lanes * len(weights) + 2 * rows * shape[1]),
        )(*[x for u in used for x in pieces[u]], *[x for x, _ in weights], *extra)

    def by_unit(pieces):
        return [(pieces[j], pieces[blocks + j]) for j in range(blocks)]

    theirs, mine = strips_of(None, None)
    pieces = by_unit(own_pieces) + by_unit(other_pieces)
    product = project(pieces, theirs + mine, [(0, 0, 3), (0, 4, 8), (1, 0, 3), (1, 4, 7)])
    product = project(pieces, theirs + mine, [(2, 0, 8)], product)
    product, other_pieces, far_6 = together((product, other_pieces, far_6))
    theirs, mine = strips_of(far_6, swap(far_6, near))
    pieces = by_unit(own_pieces) + by_unit(other_pieces)
    from_them = swap(project(pieces, theirs, [(3, 0, 4), (0, 3, 4), (1, 3, 4)], product, 0), 0, 1)
    product = project(pieces, mine, [(3, 0, 4), (1, 3, 4)], product, 1)

    if strip_width % 128 == 0:
        parts = pl.pallas_call(
            functools.partial(route_kernel, groups, strip_width),
            grid_spec=pltpu.PrefetchScalarGridSpec(
                num_scalar_prefetch=1,
                grid=(1,),
                in_specs=[pl.BlockSpec(x.shape, lambda i, send: (0, 0)) for x in (product, from_them)],
                out_specs=[pl.BlockSpec((rows, size * strip_width), lambda i, send: (0, 0))] * steps,
                scratch_shapes=[pltpu.VMEM((steps, rows, size * strip_width), jnp.float32)],
            ),
            out_shape=[of(rows, size * strip_width)] * steps,
            compiler_params=params(12),
            name="route",
            cost_estimate=cost(0, 6 * rows * steps * size * strip_width),
        )(send_here, product, from_them)
    else:
        parts = jnp.stack(pieces_of(product + from_them, groups, strip_width))
        parts = [lax.dynamic_index_in_dim(parts, send_here[k], 0, False) for k in range(steps)]
    arrived = [lax.ppermute(part, AXES, perm) for part, perm in zip(parts, perms)]
    if strip_width % 128 == 0:
        return pl.pallas_call(
            functools.partial(assemble_kernel, size),
            grid_spec=pltpu.PrefetchScalarGridSpec(
                num_scalar_prefetch=1,
                grid=(1,),
                in_specs=[pl.BlockSpec(x.shape, lambda i, place: (0, 0)) for x in (*arrived, residual)],
                out_specs=pl.BlockSpec(residual.shape, lambda i, place: (0, 0)),
                scratch_shapes=[pltpu.VMEM((ctx, rows, strip_width), jnp.float32)],
            ),
            out_shape=of(*residual.shape),
            compiler_params=params(12),
            name="assemble",
            cost_estimate=cost(0, 3 * residual.size),
        )(place_here, *arrived, residual)
    blocks = jnp.stack([a[:, b * strip_width : (b + 1) * strip_width] for a in arrived for b in range(size)])
    projected = [lax.dynamic_index_in_dim(blocks, place_here[p], 0, False) for p in range(ctx)]
    return residual + jnp.concatenate(projected, axis=1)


def solution(mesh):
    placed = (
        P("ctx", "head"),
        P("ctx", "head"),
        P("ctx", "head"),
        P("head", None, None),
        P("head", None, None),
        P(None, ("ctx", "head")),
        P("ctx", "head"),
    )
    return jax.shard_map(
        functools.partial(body, mesh.shape["ctx"], mesh.shape["head"]),
        mesh=mesh,
        in_specs=placed,
        out_specs=P("ctx", "head"),
        check_vma=False,
    )
```

profile of v0, /device:TPU:0, one launch (start us, length us, event | category | flops | bytes accessed | tf_op | source)
XLA Modules:
  0.0 198.9 jit_solution(13934592972923232421)
XLA Ops:
  0.0 4.0 %key_part.1 = (f32[4,264,128]{2,1,0:T(8,128)}, f32[4,256,256]{2,1,0:T(8,128)}) custom-call(s32[1]{0:T(128)} %bitcast.first, f32[256,1024]{1,0:T(8,128)} %refs_0_.1, f32[8,128,128]{2,1,0:T(8,128)} %refs_1_.1, f32[256,1024]{1,0:T(8,128)} %refs_7_.1), custom_call_target="tpu_custom_call" | custom-call | flops 603979776 | bytes 3145728 | tf_op jit(solution)/shard_map/key_part/pallas_call | solution.py:213
  4.0 2.9 %collective-permute-start = (f32[4,264,128]{2,1,0:T(8,128)}, f32[4,264,128]{2,1,0:T(8,128)}, u32[]{:S(2)}, u32[]{:S(2)}) collective-permute-start(f32[4,264,128]{2,1,0:T(8,128)} %get-tuple-element.57), channel_id=1, source_target_pairs={{0,4},{1,5},{2,6},{3,7},{4,0},{5,1},{6,2},{7,3},{8,12},{9,13},{10,... | collective-permute-start | bytes 1622024 | tf_op jit(solution)/shard_map/ppermute | solution.py:195
  8.7 2.6 %collective-permute-start.1 = (f32[512,128]{1,0:T(8,128)}, f32[512,128]{1,0:T(8,128)S(1)}, u32[]{:S(2)}, u32[]{:S(2)}) collective-permute-start(f32[512,128]{1,0:T(8,128)} %constant_dynamic-slice_fusion.9), channel_id=1, source_target_pairs={{0,16},{1,17},{2,18},{3,19},{4,20},{5,21},{6,22},{7,23},{8,24},{9,... | collective-permute-start | bytes 786440 | tf_op jit(solution)/shard_map/ppermute | solution.py:195
  14.8 9.6 %rest_part.1 = (f32[4,264,128]{2,1,0:T(8,128)S(1)}, f32[4,256,256]{2,1,0:T(8,128)S(1)}, f32[4,256,128]{2,1,0:T(8,128)S(1)}, f32[4,256,128]{2,1,0:T(8,128)S(1)}, ...) custom-call(s32[2]{0:T(128)S(1)} %pad_add_fusion.first, ...), custom_call_target="tpu_custom_call" | custom-call | flops 3422552064 | bytes 8388608 | tf_op jit(solution)/shard_map/rest_part/pallas_call | solution.py:240
  39.2 20.4 %collective-permute-done.2 = f32[4,264,128]{2,1,0:T(8,128)} collective-permute-done((f32[4,264,128]{2,1,0:T(8,128)}, f32[4,264,128]{2,1,0:T(8,128)}, u32[]{:S(2)}, u32[]{:S(2)}) %collective-permute-start.2) | collective-permute-done | bytes 540704 | tf_op jit(solution)/shard_map/ppermute | solution.py:195
  61.7 3.6 %collective-permute-done.3.refs_16_.refs_8_ = f32[1024,128]{1,0:T(8,128)} collective-permute-done((f32[1024,128]{1,0:T(8,128)}, f32[1024,128]{1,0:T(8,128)}, u32[]{:S(2)}, u32[]{:S(2)}) %collective-permute-start.3) | collective-permute-done | bytes 524320 | tf_op jit(solution)/shard_map/ppermute | solution.py:195
  66.8 2.3 %collective-permute-start.6 = (f32[2,264,128]{2,1,0:T(8,128)S(1)}, f32[2,264,128]{2,1,0:T(8,128)}, u32[]{:S(2)}, u32[]{:S(2)}) collective-permute-start(f32[2,264,128]{2,1,0:T(8,128)S(1)} %slice_select_fusion), channel_id=1, source_target_pairs={{0,16},{1,17},{2,18},{3,19},{4,20},{5,21},{6,22},{7,23},{8,24},{9,... | collective-permute-start | bytes 811016 | tf_op jit(solution)/shard_map/ppermute | solution.py:195
  69.9 3.6 %collective-permute-done.6 = f32[2,264,128]{2,1,0:T(8,128)} collective-permute-done((f32[2,264,128]{2,1,0:T(8,128)S(1)}, f32[2,264,128]{2,1,0:T(8,128)}, u32[]{:S(2)}, u32[]{:S(2)}) %collective-permute-start.6) | collective-permute-done | bytes 270368 | tf_op jit(solution)/shard_map/ppermute | solution.py:195
  76.4 11.4 %collective-permute-start.8 = (f32[512,128]{1,0:T(8,128)}, f32[512,128]{1,0:T(8,128)S(1)}, u32[]{:S(2)}, u32[]{:S(2)}) collective-permute-start(f32[512,128]{1,0:T(8,128)} %get-tuple-element.69), channel_id=1, source_target_pairs={{0,16},{1,17},{2,18},{3,19},{4,20},{5,21},{6,22},{7,23},{8,24},{9,... | collective-permute-start | bytes 786440 | tf_op jit(solution)/shard_map/ppermute | solution.py:195
  89.0 10.9 %collective-permute-done.8.refs_6_ = f32[512,128]{1,0:T(8,128)S(1)} collective-permute-done((f32[512,128]{1,0:T(8,128)}, f32[512,128]{1,0:T(8,128)S(1)}, u32[]{:S(2)}, u32[]{:S(2)}) %collective-permute-start.8) | collective-permute-done | bytes 262176 | tf_op jit(solution)/shard_map/ppermute | solution.py:195
  104.8 2.9 %collective-permute-start.11 = (f32[512,128]{1,0:T(8,128)S(1)}, f32[512,128]{1,0:T(8,128)S(1)}, u32[]{:S(2)}, u32[]{:S(2)}) collective-permute-start(f32[512,128]{1,0:T(8,128)S(1)} %copy-done.25), channel_id=1, source_target_pairs={{0,16},{1,17},{2,18},{3,19},{4,20},{5,21},{6,22},{7,23},{8,24},{9,... | collective-permute-start | bytes 786440 | tf_op jit(solution)/shard_map/ppermute | solution.py:195
  107.8 11.6 %collective-permute-done.11.refs_13_ = f32[512,128]{1,0:T(8,128)S(1)} collective-permute-done((f32[512,128]{1,0:T(8,128)S(1)}, f32[512,128]{1,0:T(8,128)S(1)}, u32[]{:S(2)}, u32[]{:S(2)}) %collective-permute-start.11) | collective-permute-done | bytes 262176 | tf_op jit(solution)/shard_map/ppermute | solution.py:195
  119.3 2.2 %collective-permute-done.12.refs_1_ = f32[256,512]{1,0:T(8,128)S(1)} collective-permute-done((f32[256,512]{1,0:T(8,128)S(1)}, f32[256,512]{1,0:T(8,128)S(1)}, u32[]{:S(2)}, u32[]{:S(2)}) %collective-permute-start.12) | collective-permute-done | bytes 524320 | tf_op jit(solution)/shard_map/ppermute | solution.py:195
  129.4 15.5 %collective-permute-done.15.refs_1_ = f32[256,512]{1,0:T(8,128)S(1)} collective-permute-done((f32[256,512]{1,0:T(8,128)S(1)}, f32[256,512]{1,0:T(8,128)S(1)}, u32[]{:S(2)}, u32[]{:S(2)}) %collective-permute-start.15) | collective-permute-done | bytes 524320 | tf_op jit(solution)/shard_map/ppermute | solution.py:195
  144.9 5.8 %collective-permute-done.17.refs_4_.refs_8_ = f32[1024,128]{1,0:T(8,128)S(1)} collective-permute-done((f32[1024,128]{1,0:T(8,128)S(1)}, f32[1024,128]{1,0:T(8,128)S(1)}, u32[]{:S(2)}, u32[]{:S(2)}) %collective-permute-start.17) | collective-permute-done | bytes 524320 | tf_op jit(solution)/shard_map/ppermute | solution.py:195
  151.4 2.3 %collective-permute-start.19 = (f32[256,512]{1,0:T(8,128)S(1)}, f32[256,512]{1,0:T(8,128)S(1)}, u32[]{:S(2)}, u32[]{:S(2)}) collective-permute-start(f32[256,512]{1,0:T(8,128)S(1)} %collective-permute-done.15.refs_1_), channel_id=1, source_target_pairs={{0,2},{1,3},{2,0},{3,1},{4,6},{5,7},{6,4},{7,5},{8,10},{9,11},{10,... | collective-permute-start | bytes 1572872 | tf_op jit(solution)/shard_map/ppermute | solution.py:195
  156.0 4.6 %project.4.refs_10_ = f32[512,1024]{1,0:T(8,128)S(1)} custom-call(f32[256,512]{1,0:T(8,128)S(1)} %mix.2.refs_0_, f32[256,512]{1,0:T(8,128)S(1)} %collective-permute-done.12.refs_1_, f32[256,512]{1,0:T(8,128)S(1)} %collective-permute-done.13.refs_2_.refs_0_, f32[256,512]{1,0:T(8,128)S(1)} %collective-permute-done.14.refs_3_.refs_1_, ...), custom_call_target="tpu_custom_call" | custom-call | flops 2617245696 | bytes 5505024 | tf_op jit(solution)/shard_map/project/pallas_call | solution.py:400
  160.6 2.9 %project.5.refs_9_.refs_12_ = f32[512,1024]{1,0:T(8,128)S(1)} custom-call(f32[256,512]{1,0:T(8,128)S(1)} %mix.3.refs_0_, f32[256,512]{1,0:T(8,128)S(1)} %collective-permute-done.15.refs_1_, f32[2048,128]{1,0:T(8,128)S(1)} %collective-permute-done.5.refs_4_.refs_11_.refs_2_.refs_6_, f32[2048,128]{1,0:T(8,128)} %collective-permute-done.9.refs_5_.refs_12_.refs_3_.refs_7_, ...), custom_call_target="tpu_custom_call" | custom-call | flops 1610612736 | bytes 4194304 | tf_op jit(solution)/shard_map/project/pallas_call | solution.py:400
  163.5 3.6 %collective-permute-done.20.refs_6_ = f32[512,128]{1,0:T(8,128)S(1)} collective-permute-done((f32[512,128]{1,0:T(8,128)S(1)}, f32[512,128]{1,0:T(8,128)S(1)}, u32[]{:S(2)}, u32[]{:S(2)}) %collective-permute-start.20) | collective-permute-done | bytes 262176 | tf_op jit(solution)/shard_map/ppermute | solution.py:195
  167.1 2.9 %project.7 = f32[512,512]{1,0:T(8,128)S(1)} custom-call(f32[256,512]{1,0:T(8,128)S(1)} %mix.2.refs_0_, f32[256,512]{1,0:T(8,128)S(1)} %collective-permute-done.12.refs_1_, f32[256,512]{1,0:T(8,128)S(1)} %collective-permute-done.13.refs_2_.refs_0_, f32[256,512]{1,0:T(8,128)S(1)} %collective-permute-done.14.refs_3_.refs_1_, ...), custom_call_target="tpu_custom_call" | custom-call | flops 1207959552 | bytes 2621440 | tf_op jit(solution)/shard_map/project/pallas_call | solution.py:400
  171.5 7.3 %collective-permute-done.21.refs_8_ = f32[512,128]{1,0:T(8,128)S(1)} collective-permute-done((f32[512,128]{1,0:T(8,128)S(1)}, f32[512,128]{1,0:T(8,128)S(1)}, u32[]{:S(2)}, u32[]{:S(2)}) %collective-permute-start.21) | collective-permute-done | bytes 262176 | tf_op jit(solution)/shard_map/ppermute | solution.py:195
  184.4 3.5 %collective-permute-start.27 = (f32[256,256]{1,0:T(8,128)S(1)}, f32[256,256]{1,0:T(8,128)S(1)}, u32[]{:S(2)}, u32[]{:S(2)}) collective-permute-start(f32[256,256]{1,0:T(8,128)S(1)} %get-tuple-element.106), channel_id=1, source_target_pairs={{0,10},{1,8},{2,2},{3,0},{4,14},{5,12},{6,6},{7,4},{8,11},{9,9},{1... | collective-permute-start | bytes 786440 | tf_op jit(solution)/shard_map/ppermute | solution.py:444
  188.0 5.9 %collective-permute-done.25.refs_1_ = f32[256,256]{1,0:T(8,128)S(1)} collective-permute-done((f32[256,256]{1,0:T(8,128)S(1)}, f32[256,256]{1,0:T(8,128)S(1)}, u32[]{:S(2)}, u32[]{:S(2)}) %collective-permute-start.25) | collective-permute-done | bytes 262176 | tf_op jit(solution)/shard_map/ppermute | solution.py:444
  194.3 2.9 %collective-permute-done.27.refs_3_ = f32[256,256]{1,0:T(8,128)S(1)} collective-permute-done((f32[256,256]{1,0:T(8,128)S(1)}, f32[256,256]{1,0:T(8,128)S(1)}, u32[]{:S(2)}, u32[]{:S(2)}) %collective-permute-start.27) | collective-permute-done | bytes 262176 | tf_op jit(solution)/shard_map/ppermute | solution.py:444
  (115 shorter events, 53.2 us)
Async XLA Ops:
  4.0 27.1 %collective-permute-start = (f32[4,264,128]{2,1,0:T(8,128)}, f32[4,264,128]{2,1,0:T(8,128)}, u32[]{:S(2)}, u32[]{:S(2)}) collective-permute-start(f32[4,264,128]{2,1,0:T(8,128)} %get-tuple-element.57), channel_id=1, source_target_pairs={{0,4},{1,5},{2,6},{3,7},{4,0},{5,1},{6,2},{7,3},{8,12},{9,13},{10,... | collective-permute-start | bytes 1622024 | tf_op jit(solution)/shard_map/ppermute | solution.py:195
  8.7 22.5 %collective-permute-start.1 = (f32[512,128]{1,0:T(8,128)}, f32[512,128]{1,0:T(8,128)S(1)}, u32[]{:S(2)}, u32[]{:S(2)}) collective-permute-start(f32[512,128]{1,0:T(8,128)} %constant_dynamic-slice_fusion.9), channel_id=1, source_target_pairs={{0,16},{1,17},{2,18},{3,19},{4,20},{5,21},{6,22},{7,23},{8,24},{9,... | collective-permute-start | bytes 786440 | tf_op jit(solution)/shard_map/ppermute | solution.py:195
  32.5 32.7 %collective-permute-start.4 = (f32[2048,128]{1,0:T(8,128)S(1)}, f32[2048,128]{1,0:T(8,128)S(1)}, u32[]{:S(2)}, u32[]{:S(2)}) collective-permute-start(f32[2048,128]{1,0:T(8,128)S(1)} %constant_dynamic-update-slice_fusion.refs_7_.refs_14_.refs_6_.refs_4_), channel_id=1, source_target_pairs={{0,4},{1,5},{2,6},{3,7},{4,0},{5,1},{6,2},{7,3},{8,12},{9,13},{10,... | collective-permute-start | bytes 3145736 | tf_op jit(solution)/shard_map/ppermute | solution.py:195
  34.3 31.0 %collective-permute-start.5 = (f32[2048,128]{1,0:T(8,128)}, f32[2048,128]{1,0:T(8,128)S(1)}, u32[]{:S(2)}, u32[]{:S(2)}) collective-permute-start(f32[2048,128]{1,0:T(8,128)} %pad_maximum_fusion.1), channel_id=1, source_target_pairs={{0,1},{1,0},{2,3},{3,2},{4,5},{5,4},{6,7},{7,6},{8,9},{9,8},{10,11... | collective-permute-start | bytes 3145736 | tf_op jit(solution)/shard_map/ppermute | solution.py:195
  36.4 23.2 %collective-permute-start.2 = (f32[4,264,128]{2,1,0:T(8,128)}, f32[4,264,128]{2,1,0:T(8,128)}, u32[]{:S(2)}, u32[]{:S(2)}) collective-permute-start(f32[4,264,128]{2,1,0:T(8,128)} %add.78), channel_id=1, source_target_pairs={{0,8},{1,9},{2,10},{3,11},{4,12},{5,13},{6,14},{7,15},{8,0},{9,1},... | collective-permute-start | bytes 1622024 | tf_op jit(solution)/shard_map/ppermute | solution.py:195
  38.8 26.4 %collective-permute-start.3 = (f32[1024,128]{1,0:T(8,128)}, f32[1024,128]{1,0:T(8,128)}, u32[]{:S(2)}, u32[]{:S(2)}) collective-permute-start(f32[1024,128]{1,0:T(8,128)} %slice.21), channel_id=1, source_target_pairs={{0,16},{1,17},{2,18},{3,19},{4,20},{5,21},{6,22},{7,23},{8,24},{9,... | collective-permute-start | bytes 1572872 | tf_op jit(solution)/shard_map/ppermute | solution.py:195
  65.2 34.7 %collective-permute-start.9 = (f32[2048,128]{1,0:T(8,128)S(1)}, f32[2048,128]{1,0:T(8,128)}, u32[]{:S(2)}, u32[]{:S(2)}) collective-permute-start(f32[2048,128]{1,0:T(8,128)S(1)} %collective-permute-done.5.refs_4_.refs_11_.refs_2_.refs_6_), channel_id=1, source_target_pairs={{0,4},{1,5},{2,6},{3,7},{4,0},{5,1},{6,2},{7,3},{8,12},{9,13},{10,... | collective-permute-start | bytes 3145736 | tf_op jit(solution)/shard_map/ppermute | solution.py:195
  73.6 14.3 %collective-permute-start.7 = (f32[2,264,128]{2,1,0:T(8,128)}, f32[2,264,128]{2,1,0:T(8,128)}, u32[]{:S(2)}, u32[]{:S(2)}) collective-permute-start(f32[2,264,128]{2,1,0:T(8,128)} %collective-permute-done.6), channel_id=1, source_target_pairs={{16,24},{17,25},{18,26},{19,27},{20,28},{21,29},{22,30},{23,31},{2... | collective-permute-start | bytes 811016 | tf_op jit(solution)/shard_map/ppermute | solution.py:195
  76.4 23.5 %collective-permute-start.8 = (f32[512,128]{1,0:T(8,128)}, f32[512,128]{1,0:T(8,128)S(1)}, u32[]{:S(2)}, u32[]{:S(2)}) collective-permute-start(f32[512,128]{1,0:T(8,128)} %get-tuple-element.69), channel_id=1, source_target_pairs={{0,16},{1,17},{2,18},{3,19},{4,20},{5,21},{6,22},{7,23},{8,24},{9,... | collective-permute-start | bytes 786440 | tf_op jit(solution)/shard_map/ppermute | solution.py:195
  100.1 21.4 %collective-permute-start.10 = (f32[4,264,128]{2,1,0:T(8,128)S(1)}, f32[4,264,128]{2,1,0:T(8,128)S(1)}, u32[]{:S(2)}, u32[]{:S(2)}) collective-permute-start(f32[4,264,128]{2,1,0:T(8,128)S(1)} %get-tuple-element.108), channel_id=1, source_target_pairs={{0,4},{1,5},{2,6},{3,7},{4,0},{5,1},{6,2},{7,3},{8,12},{9,13},{10,... | collective-permute-start | bytes 1622024 | tf_op jit(solution)/shard_map/ppermute | solution.py:195
  103.1 18.4 %collective-permute-start.12 = (f32[256,512]{1,0:T(8,128)S(1)}, f32[256,512]{1,0:T(8,128)S(1)}, u32[]{:S(2)}, u32[]{:S(2)}) collective-permute-start(f32[256,512]{1,0:T(8,128)S(1)} %mix.2.refs_0_), channel_id=1, source_target_pairs={{0,8},{1,9},{2,10},{3,11},{4,12},{5,13},{6,14},{7,15},{8,0},{9,1},... | collective-permute-start | bytes 1572872 | tf_op jit(solution)/shard_map/ppermute | solution.py:195
  103.2 18.3 %collective-permute-start.13 = (f32[256,512]{1,0:T(8,128)S(1)}, f32[256,512]{1,0:T(8,128)S(1)}, u32[]{:S(2)}, u32[]{:S(2)}) collective-permute-start(f32[256,512]{1,0:T(8,128)S(1)} %mix.2.refs_0_), channel_id=1, source_target_pairs={{0,2},{1,3},{2,0},{3,1},{4,6},{5,7},{6,4},{7,5},{8,10},{9,11},{10,... | collective-permute-start | bytes 1572872 | tf_op jit(solution)/shard_map/ppermute | solution.py:195
  104.8 14.5 %collective-permute-start.11 = (f32[512,128]{1,0:T(8,128)S(1)}, f32[512,128]{1,0:T(8,128)S(1)}, u32[]{:S(2)}, u32[]{:S(2)}) collective-permute-start(f32[512,128]{1,0:T(8,128)S(1)} %copy-done.25), channel_id=1, source_target_pairs={{0,16},{1,17},{2,18},{3,19},{4,20},{5,21},{6,22},{7,23},{8,24},{9,... | collective-permute-start | bytes 786440 | tf_op jit(solution)/shard_map/ppermute | solution.py:195
  122.7 28.7 %collective-permute-start.18 = (f32[2560,128]{1,0:T(8,128)S(1)}, f32[2560,128]{1,0:T(8,128)S(1)}, u32[]{:S(2)}, u32[]{:S(2)}) collective-permute-start(f32[2560,128]{1,0:T(8,128)S(1)} %pad_maximum_fusion), channel_id=1, source_target_pairs={{0,4},{1,5},{2,6},{3,7},{4,0},{5,1},{6,2},{7,3},{8,12},{9,13},{10,... | collective-permute-start | bytes 3932168 | tf_op jit(solution)/shard_map/ppermute | solution.py:195
  124.4 20.6 %collective-permute-start.15 = (f32[256,512]{1,0:T(8,128)S(1)}, f32[256,512]{1,0:T(8,128)S(1)}, u32[]{:S(2)}, u32[]{:S(2)}) collective-permute-start(f32[256,512]{1,0:T(8,128)S(1)} %mix.3.refs_0_), channel_id=1, source_target_pairs={{0,8},{1,9},{2,10},{3,11},{4,12},{5,13},{6,14},{7,15},{8,0},{9,1},... | collective-permute-start | bytes 1572872 | tf_op jit(solution)/shard_map/ppermute | solution.py:195
  125.7 19.2 %collective-permute-start.16 = (f32[256,512]{1,0:T(8,128)S(1)}, f32[256,512]{1,0:T(8,128)S(1)}, u32[]{:S(2)}, u32[]{:S(2)}) collective-permute-start(f32[256,512]{1,0:T(8,128)S(1)} %mix.3.refs_0_), channel_id=1, source_target_pairs={{0,2},{1,3},{2,0},{3,1},{4,6},{5,7},{6,4},{7,5},{8,10},{9,11},{10,... | collective-permute-start | bytes 1572872 | tf_op jit(solution)/shard_map/ppermute | solution.py:195
  127.2 23.6 %collective-permute-start.17 = (f32[1024,128]{1,0:T(8,128)S(1)}, f32[1024,128]{1,0:T(8,128)S(1)}, u32[]{:S(2)}, u32[]{:S(2)}) collective-permute-start(f32[1024,128]{1,0:T(8,128)S(1)} %slice.26), channel_id=1, source_target_pairs={{0,16},{1,17},{2,18},{3,19},{4,20},{5,21},{6,22},{7,23},{8,24},{9,... | collective-permute-start | bytes 1572872 | tf_op jit(solution)/shard_map/ppermute | solution.py:195
  128.9 27.1 %collective-permute-start.14 = (f32[256,512]{1,0:T(8,128)S(1)}, f32[256,512]{1,0:T(8,128)S(1)}, u32[]{:S(2)}, u32[]{:S(2)}) collective-permute-start(f32[256,512]{1,0:T(8,128)S(1)} %collective-permute-done.12.refs_1_), channel_id=1, source_target_pairs={{0,2},{1,3},{2,0},{3,1},{4,6},{5,7},{6,4},{7,5},{8,10},{9,11},{10,... | collective-permute-start | bytes 1572872 | tf_op jit(solution)/shard_map/ppermute | solution.py:195
  151.4 15.7 %collective-permute-start.19 = (f32[256,512]{1,0:T(8,128)S(1)}, f32[256,512]{1,0:T(8,128)S(1)}, u32[]{:S(2)}, u32[]{:S(2)}) collective-permute-start(f32[256,512]{1,0:T(8,128)S(1)} %collective-permute-done.15.refs_1_), channel_id=1, source_target_pairs={{0,2},{1,3},{2,0},{3,1},{4,6},{5,7},{6,4},{7,5},{8,10},{9,11},{10,... | collective-permute-start | bytes 1572872 | tf_op jit(solution)/shard_map/ppermute | solution.py:195
  153.7 13.5 %collective-permute-start.22 = (f32[1024,128]{1,0:T(8,128)S(1)}, f32[1024,128]{1,0:T(8,128)S(1)}, u32[]{:S(2)}, u32[]{:S(2)}) collective-permute-start(f32[1024,128]{1,0:T(8,128)S(1)} %collective-permute-done.17.refs_4_.refs_8_), channel_id=1, source_target_pairs={{0,4},{1,5},{2,6},{3,7},{4,0},{5,1},{6,2},{7,3},{8,12},{9,13},{10,... | collective-permute-start | bytes 1572872 | tf_op jit(solution)/shard_map/ppermute | solution.py:195
  155.1 12.0 %collective-permute-start.20 = (f32[512,128]{1,0:T(8,128)S(1)}, f32[512,128]{1,0:T(8,128)S(1)}, u32[]{:S(2)}, u32[]{:S(2)}) collective-permute-start(f32[512,128]{1,0:T(8,128)S(1)} %slice.27), channel_id=1, source_target_pairs={{0,16},{1,17},{2,18},{3,19},{4,20},{5,21},{6,22},{7,23},{8,24},{9,... | collective-permute-start | bytes 786440 | tf_op jit(solution)/shard_map/ppermute | solution.py:195
  181.8 12.1 %collective-permute-start.25 = (f32[256,256]{1,0:T(8,128)S(1)}, f32[256,256]{1,0:T(8,128)S(1)}, u32[]{:S(2)}, u32[]{:S(2)}) collective-permute-start(f32[256,256]{1,0:T(8,128)S(1)} %get-tuple-element.104), channel_id=1, source_target_pairs={{0,2},{1,0},{2,10},{3,8},{4,6},{5,4},{6,14},{7,12},{8,3},{9,1},{10... | collective-permute-start | bytes 786440 | tf_op jit(solution)/shard_map/ppermute | solution.py:444
  183.3 10.9 %collective-permute-start.26 = (f32[256,256]{1,0:T(8,128)S(1)}, f32[256,256]{1,0:T(8,128)S(1)}, u32[]{:S(2)}, u32[]{:S(2)}) collective-permute-start(f32[256,256]{1,0:T(8,128)S(1)} %get-tuple-element.105), channel_id=1, source_target_pairs={{0,8},{1,10},{2,0},{3,2},{4,12},{5,14},{6,4},{7,6},{8,9},{9,11},{1... | collective-permute-start | bytes 786440 | tf_op jit(solution)/shard_map/ppermute | solution.py:444
  184.4 12.8 %collective-permute-start.27 = (f32[256,256]{1,0:T(8,128)S(1)}, f32[256,256]{1,0:T(8,128)S(1)}, u32[]{:S(2)}, u32[]{:S(2)}) collective-permute-start(f32[256,256]{1,0:T(8,128)S(1)} %get-tuple-element.106), channel_id=1, source_target_pairs={{0,10},{1,8},{2,2},{3,0},{4,14},{5,12},{6,6},{7,4},{8,11},{9,9},{1... | collective-permute-start | bytes 786440 | tf_op jit(solution)/shard_map/ppermute | solution.py:444
  (30 other events, 208.8 us)
where the time goes:
time: 201 us; the launch traced here: 199 us
  waiting for transfers between devices  94.4 us (47%)
  starting transfers between devices  48.6 us (24%)
  Pallas kernels  30.3 us (15%)
  local copies, waits for them, and re-layouts  17.5 us (9%)
  other arithmetic  7.71 us (4%)
    ppermute x24, waiting for transfers between devices, swap(): return lax.ppermute(x, AXES, pairs)  85.2 us
    ppermute x24, starting transfers between devices, swap(): return lax.ppermute(x, AXES, pairs)  41.8 us
    pallas_call x4, Pallas kernels, project(): pl.pallas_call(functools.partial(project_kernel, terms, len(used)), grid=...  11.9 us
    unnamed x53, local copies, waits for them, and re-layouts  10.2 us
    pallas_call x1, Pallas kernels, rest_part(): pl.pallas_call(rest_kernel, grid_spec=pltpu.PrefetchScalarGridSpec(num_sc...  9.61 us
    ppermute x4, waiting for transfers between devices, body(): lax.ppermute(part, AXES, perm)  9.22 us
    ppermute x4, starting transfers between devices, body(): lax.ppermute(part, AXES, perm)  6.85 us
    pallas_call x1, Pallas kernels, key_part(): pl.pallas_call(key_kernel, grid_spec=pltpu.PrefetchScalarGridSpec(num_sca...  4.04 us
  transfers between devices with their start and end apart: 28, of which 14 were waited for; matrix products, arithmetic and copies ran while one was open for 7% of the time, Pallas kernels for 11%

commit v1 on v0

--- a/solution.py
+++ b/solution.py
@@ -36,6 +36,18 @@
     up = up / jnp.sum(up, axis=-1, keepdims=True)
     down = down / jnp.sum(down, axis=-1, keepdims=True)
     return jnp.concatenate([up, down], axis=-1)
+
+
+def arrange_kernel(plan, wide, starts, weight_ref, *refs):
+    out_refs, sems = refs[:-1], refs[-1]
+    copies = []
+    for out_ref, picks in zip(out_refs, plan):
+        for i, pick in enumerate(picks):
+            source = weight_ref.at[pl.ds(pl.multiple_of(starts[pick], wide), wide), :]
+            copies.append(pltpu.make_async_copy(source, out_ref.at[pl.ds(i * wide, wide), :], sems.at[len(copies)]))
+            copies[-1].start()
+    for copy in copies:
+        copy.wait()
 
 
 def key_kernel(first, k_ref, map_ref, v_ref, state_ref, feat_ref):
@@ -78,14 +90,20 @@
     attend(feat, other_feat_ref[0], other_v_ref[...], other_numer_ref, other_denom_ref)
 
 
-def mix_kernel(qfeat_ref, numer_ref, denom_ref, prior_ref, out_ref):
+def mix_kernel(qfeat_ref, numer_ref, denom_ref, prior_ref, *refs):
     feat = qfeat_ref[0]
     size = feat.shape[1]
     norm = jnp.concatenate(
         [prior_ref[0, size : size + 1, :], prior_ref[0, size + EXTRA // 2 : size + EXTRA // 2 + 1, :]], axis=1
     )
     denom = denom_ref[0] + jnp.sum(feat * norm, axis=-1, keepdims=True)
-    out_ref[...] = (numer_ref[0] + dot3(feat, prior_ref[0, :size, :])) / denom
+    mixed = (numer_ref[0] + dot3(feat, prior_ref[0, :size, :])) / denom
+    if len(refs) == 1:
+        refs[0][...] = mixed
+    else:
+        below_ref, out_ref, both_ref = refs
+        out_ref[...] = mixed
+        both_ref[...] = jnp.concatenate([mixed, below_ref[...]], axis=0)
 
 
 def project_kernel(terms, units, *refs):
@@ -257,7 +275,12 @@
         )(firsts, keys, key_map, queries, query_map, values, queries, query_map, values, other_feat)
         return outs[0], outs[1:4], outs[4:]
 
-    def mix(qfeat, numer, denom, prior):
+    def mix(qfeat, numer, denom, prior, below=None):
+        columns = pl.BlockSpec((rows, head_size), lambda i: (0, i))
+        out_specs, shapes = columns, of(rows, wide)
+        if below is not None:
+            out_specs = [columns, pl.BlockSpec((2 * rows, head_size), lambda i: (0, i))]
+            shapes = [shapes, of(2 * rows, wide)]
         return pl.pallas_call(
             mix_kernel,
             grid=(half,),
@@ -266,19 +289,19 @@
                 head_block(rows, head_size),
                 head_block(rows, head_size),
                 head_block(feat_size + EXTRA, head_size),
-            ],
-            out_specs=pl.BlockSpec((rows, head_size), lambda i: (0, i)),
-            out_shape=of(rows, wide),
+            ]
+            + [columns] * (below is not None),
+            out_specs=out_specs,
+            out_shape=shapes,
             compiler_params=params(12),
             name="mix",
             cost_estimate=cost(
                 3 * half * rows * feat_size * head_size, half * rows * (3 * head_size + 2 * feat_size)
             ),
-        )(qfeat, numer, denom, prior)
+        )(qfeat, numer, denom, prior, *([] if below is None else [below]))
 
     even = range(0, heads, 2)
     blocks = heads // 2
-    quarter = 2 * blocks // 4 * wide
     bits = [1 << b for b in reversed(range(ctx.bit_length() - 1)) if 1 << b != PAIR]
     far, near = bits[-2:]
     rels = [0]
@@ -286,26 +309,42 @@
         rels = rels + [r | bit for r in rels]
     rels = [r | s for s in (0, near, far, far | near) for r in rels]
 
-    def rows_of(weight, flip, some):
-        starts = [(h ^ flip ^ d) * depth + which * wide for which, d in some]
-        return jnp.concatenate([lax.dynamic_slice_in_dim(weight, start, wide, 0) for start in starts])
+    def arranged(weight, starts, plan):
+        shapes = [of(len(picks) * wide, strip_width) for picks in plan]
+        count = sum(len(picks) for picks in plan)
+        return pl.pallas_call(
+            functools.partial(arrange_kernel, plan, wide),
+            grid_spec=pltpu.PrefetchScalarGridSpec(
+                num_scalar_prefetch=1,
+                grid=(1,),
+                in_specs=[pl.BlockSpec(memory_space=pl.ANY)],
+                out_specs=[pl.BlockSpec(memory_space=pl.ANY)] * len(plan),
+                scratch_shapes=[pltpu.SemaphoreType.DMA((count,))],
+            ),
+            out_shape=shapes,
+            compiler_params=params(12),
+            name="arrange",
+            cost_estimate=cost(0, 2 * count * wide * strip_width),
+        )(starts, weight)
 
     def widen(x):
         for bit in bits[:-2]:
             x = jnp.concatenate([x, swap(x, bit)], axis=1)
         return x
 
-    def quarters(x):
-        return [x[i : i + quarter] for i in range(0, x.shape[0], quarter)]
-
     order = [(which, d) for which in (odd, 1 - odd) for d in even]
     part = len(order) // 4
     own, other = odd.reshape(1), (1 - odd).reshape(1)
-    kept_first = widen(rows_of(out_weight, 0, order[:part]))
-    far_1 = swap(kept_first, far)
     other_state, other_feat = key_part(other)
     out_weight, other_state = together((out_weight, other_state))
-    kept_rest = widen(rows_of(out_weight, 0, order[part:]))
+    starts = jnp.stack([(h ^ flip ^ d) * depth + which * wide for flip in (0, 1) for which, d in order])
+    count = len(order)
+    spans = [(0, part), (part, 3 * part), (3 * part, count), (0, count)]
+    plan = [list(range(*span)) for span in spans]
+    plan += [list(range(count + start, count + stop)) for start, stop in ((0, 2 * part), (2 * part, count), (0, count))]
+    *kept_parts, kept, given_1, given_2, given = arranged(out_weight, starts, plan)
+    kept_parts, kept = [widen(x) for x in kept_parts], widen(kept)
+    far_1 = swap(kept_parts[0], far)
     from_neighbour = swap(other_state, 1)
     own_state, own_query, other_query = rest_part(jnp.concatenate([own, other]), other_feat)
     groups, perms, send, place = route_tables(ctx, heads, rels)
@@ -313,13 +352,12 @@
     send_here = jnp.asarray(send)[me]
     place_here = jnp.asarray(place)[me]
 
-    from_neighbour, own_state, far_1, kept_first, kept_rest, out_weight = together(
-        (from_neighbour, own_state, far_1, kept_first, kept_rest, out_weight)
-    )
-    far_2 = swap(kept_rest[: 2 * quarter], far)
-    kept = jnp.concatenate([kept_first, kept_rest])
+    from_neighbour, own_state, far_1, kept_parts, kept, given_1, given_2, given = together(
+        (from_neighbour, own_state, far_1, kept_parts, kept, given_1, given_2, given)
+    )
+    far_2 = swap(kept_parts[1], far)
     kept_near = swap(kept, near)
-    taken = widen(swap(rows_of(out_weight, 1, order), 0, 1))
+    taken, taken_1, taken_2 = [widen(swap(x, 0, 1)) for x in (given, given_1, given_2)]
     earlier = jnp.where(odd == 0, own_state, from_neighbour)
     total = own_state + from_neighbour
     before = jnp.zeros_like(total)
@@ -329,66 +367,58 @@
         before = before + jnp.where((c & bit) != 0, got, 0.0)
         total = total + got
         bit *= 2
-    total, before, far_2, kept_near, taken = together((total, before, far_2, kept_near, taken))
+    total, before, far_2, kept_near, taken, taken_1, taken_2, send_here, place_here, far_1 = together(
+        (total, before, far_2, kept_near, taken, taken_1, taken_2, send_here, place_here, far_1)
+    )
     taken_near = swap(taken, near)
+    both_1 = swap(far_1, near)
     second = (c & PAIR) != 0
     got = swap(jnp.where(second, total[half // 2 :], total[: half // 2]), bit, keep=lambda i: not i & bit)
-    taken_parts = quarters(taken)
-    got, taken_parts[0] = together((got, taken_parts[0]))
+    got, kept_parts[2] = together((got, kept_parts[2]))
     met = swap(got, PAIR, keep=lambda i: i & bit)
-    far_3 = swap(taken_parts[0], far)
+    far_3 = swap(kept_parts[2], far)
     got = jnp.concatenate([jnp.where(second, met, got), jnp.where(second, got, met)])
-    got, far_3, taken_near, taken_parts[1], send_here, place_here = together(
-        (got, far_3, taken_near, taken_parts[1], send_here, place_here)
-    )
+    got, far_3, taken_near, both_1, taken_1 = together((got, far_3, taken_near, both_1, taken_1))
     before = before + got
 
     other_prior = swap(before + jnp.where(odd == 0, earlier, 0.0), 1)
     own_mixed = mix(*own_query, before + jnp.where(odd == 1, earlier, 0.0))
     head_bits = [1 << b for b in range(1, heads.bit_length() - 1)]
 
-    def spread(own, met, across, last):
-        pieces = {(0, 0): own, (PAIR, 0): met, (0, head_bits[0]): across, (PAIR, head_bits[0]): last}
+    def spread(pieces):
         for bit in head_bits[1:]:
-            pieces.update({(d, j | bit): swap(pieces[d, j], 0, bit) for d, j in list(pieces)})
-        return [pieces[d, j] for d in (0, PAIR) for j in even]
+            for (d, j), (x, i) in list(pieces.items()):
+                pieces[d, j | bit] = (swap(x[i * rows : (i + 1) * rows], 0, bit), 0)
+        return [(pieces[0, j], pieces[PAIR, j]) for j in even]
 
     met, across = swap(own_mixed, PAIR), swap(own_mixed, 0, head_bits[0])
-    far_4 = swap(taken_parts[1], far)
-    next_part = taken[2 * quarter :]
-    other_prior, far_1, far_2, far_3, far_4, met, across, next_part = together(
-        (other_prior, far_1, far_2, far_3, far_4, met, across, next_part)
-    )
-    own_pieces = spread(own_mixed, met, across, swap(met, 0, head_bits[0]))
-    other_mixed = mix(*other_query, other_prior)
-    met, across = swap(other_mixed, PAIR), swap(other_mixed, 0, head_bits[0])
-    far_5 = swap(next_part, far)
-    both_1 = swap(jnp.concatenate([far_1, far_2, far_3, far_4]), near)
-    met, across, far_5, both_1, kept_rest = together((met, across, far_5, both_1, kept_rest))
-    far_6 = swap(kept_rest[2 * quarter :], far)
-    both_2 = swap(far_5, near)
-    other_pieces = spread(other_mixed, met, across, swap(met, 0, head_bits[0]))
+    far_4 = swap(taken_1, far)
+    both_3 = swap(far_3, near)
+    other_prior, far_2, far_4, both_3, met, across, taken_2 = together(
+        (other_prior, far_2, far_4, both_3, met, across, taken_2)
+    )
+    other_mixed, both = mix(*other_query, other_prior, met)
+    other_met = swap(other_mixed, PAIR)
+    both = swap(both, 0, head_bits[0])
+    far_5 = swap(taken_2, far)
+    both_2 = swap(far_2, near)
+    both_4 = swap(far_4, near)
+    other_met, both, far_5, both_2, both_4 = together((other_met, both, far_5, both_2, both_4))
+    both_5 = swap(far_5, near)
+    last = swap(other_met, 0, head_bits[0])
+    own_pieces = spread(
+        {(0, 0): (own_mixed, 0), (PAIR, 0): (met, 0), (0, head_bits[0]): (across, 0), (PAIR, head_bits[0]): (both, 1)}
+    )
+
+    def other_pieces(last):
+        pieces = {(0, 0): (other_mixed, 0), (PAIR, 0): (other_met, 0), (0, head_bits[0]): (both, 0)}
+        return spread({**pieces, (PAIR, head_bits[0]): (last, 0)})
 
     lanes = kept.shape[1]
 
     def strip(parts, crossed=False):
         places = [(x, start * part + i) for x, start, stop in parts for i in range((stop - start) * part)]
         return places[blocks:] + places[:blocks] if crossed else places
-
-    def strips_of(last_far, last_both):
-        theirs = [
-            strip([(taken, 0, 4)]),
-            strip([(taken_near, 0, 4)], True),
-            strip([(far_3, 0, 1), (far_4, 0, 1), (far_5, 0, 2)]),
-            strip([(both_1, 3, 5), (both_2, 0, 2)], True),
-        ]
-        mine = [
-            strip([(kept, 0, 4)]),
-            strip([(kept_near, 0, 4)], True),
-            strip([(far_1, 0, 1), (far_2, 0, 2), (last_far, 0, 1)]),
-            strip([(both_1, 0, 3), (last_both, 0, 1)], True),
-        ]
-        return theirs, mine
 
     def project(pieces, strips, runs, total=None, column=0):
         runs = [(u, start, stop) for q, start, stop in runs for u in range(q * part, (q + 1) * part)]
@@ -400,7 +430,7 @@
         return pl.pallas_call(
             functools.partial(project_kernel, terms, len(used)),
             grid=(1,),
-            in_specs=[pl.BlockSpec((rows, wide), lambda i: (0, 0))] * (2 * len(used))
+            in_specs=[pl.BlockSpec((rows, wide), lambda i, block=block: (block, 0)) for u in used for _, block in pieces[u]]
             + [pl.BlockSpec((wide, lanes), lambda i, unit=unit: (unit, 0)) for _, unit in weights]
             + [pl.BlockSpec(shape, lambda i: (0, column))] * len(extra),
             out_specs=pl.BlockSpec(shape, lambda i: (0, 0)),
@@ -408,20 +438,27 @@
             compiler_params=params(24),
             name="project",
             cost_estimate=cost(6 * rows * wide * len(weights) * lanes, wide * lanes * len(weights) + 2 * rows * shape[1]),
-        )(*[x for u in used for x in pieces[u]], *[x for x, _ in weights], *extra)
-
-    def by_unit(pieces):
-        return [(pieces[j], pieces[blocks + j]) for j in range(blocks)]
-
-    theirs, mine = strips_of(None, None)
-    pieces = by_unit(own_pieces) + by_unit(other_pieces)
-    product = project(pieces, theirs + mine, [(0, 0, 3), (0, 4, 8), (1, 0, 3), (1, 4, 7)])
+        )(*[x for u in used for x, _ in pieces[u]], *[x for x, _ in weights], *extra)
+
+    theirs = [
+        strip([(taken, 0, 4)]),
+        strip([(taken_near, 0, 4)], True),
+        strip([(far_4, 0, 2), (far_5, 0, 2)]),
+        strip([(both_4, 0, 2), (both_5, 0, 2)], True),
+    ]
+    mine = [
+        strip([(kept, 0, 4)]),
+        strip([(kept_near, 0, 4)], True),
+        strip([(far_1, 0, 1), (far_2, 0, 2), (far_3, 0, 1)]),
+        strip([(both_1, 0, 1), (both_2, 0, 2), (both_3, 0, 1)], True),
+    ]
+    pieces = own_pieces + other_pieces(last)
+    product = project(pieces, theirs + mine, [(0, 0, 3), (0, 4, 8), (1, 0, 3), (1, 4, 8)])
     product = project(pieces, theirs + mine, [(2, 0, 8)], product)
-    product, other_pieces, far_6 = together((product, other_pieces, far_6))
-    theirs, mine = strips_of(far_6, swap(far_6, near))
-    pieces = by_unit(own_pieces) + by_unit(other_pieces)
+    product, last = together((product, last))
+    pieces = own_pieces + other_pieces(last)
     from_them = swap(project(pieces, theirs, [(3, 0, 4), (0, 3, 4), (1, 3, 4)], product, 0), 0, 1)
-    product = project(pieces, mine, [(3, 0, 4), (1, 3, 4)], product, 1)
+    product = project(pieces, mine, [(3, 0, 4)], product, 1)
 
     if strip_width % 128 == 0:
         parts = pl.pallas_call(

time: 201 us -> 190 us (0.945)
  local copies, waits for them, and re-layouts: 17.5 us -> 13 us
  waiting for transfers between devices: 94.4 us -> 91.5 us
  other arithmetic: 7.71 us -> 4.98 us
    ppermute x24 -> x26, waiting for transfers between devices: 85.2 us -> 80.8 us  [swap(): return lax.ppermute(x, AXES, pairs)]
    dynamic_slice x3 -> x0, local copies, waits for them, and re-layouts: 3.08 us -> none  [rows_of(): lax.dynamic_slice_in_dim(weight, start, wide, 0)]
    slice x4 -> x0, local copies, waits for them, and re-layouts: 2.73 us -> none  [the longest x1 0.97 us: body(): far_6 = swap(kept_rest[2 * quarter:], far)]
    concatenate x3 -> x0, other arithmetic: 2.24 us -> none  [the longest x1 1.13 us: body(): both_1 = swap(jnp.concatenate([far_1, far_2, far_3, far_4]), near)]
    pallas_call x0 -> x1, Pallas kernels: none -> 2.22 us  [arranged(): pl.pallas_call(functools.partial(arrange_kernel, plan, wide), grid_spec=p...]
    ppermute x24 -> x26, starting transfers between devices: 41.8 us -> 39.8 us  [swap(): return lax.ppermute(x, AXES, pairs)]
    unnamed x53 -> x52, local copies, waits for them, and re-layouts: 10.2 us -> 11.6 us
  transfers between devices with their start and end apart: 28 -> 30, of which waited for: 14 -> 17; matrix products, arithmetic and copies ran while one was open for 7% -> 3% of each run, Pallas kernels for 11% -> 11%
where the time goes in v1:
time: 190 us; the launch traced here: 189 us
  waiting for transfers between devices  91.5 us (48%)
  starting transfers between devices  47.4 us (25%)
  Pallas kernels  32.3 us (17%)
  local copies, waits for them, and re-layouts  13 us (7%)
  other arithmetic  4.98 us (3%)
    ppermute x26, waiting for transfers between devices, swap(): return lax.ppermute(x, AXES, pairs)  80.8 us
    ppermute x26, starting transfers between devices, swap(): return lax.ppermute(x, AXES, pairs)  39.8 us
    unnamed x52, local copies, waits for them, and re-layouts  11.6 us
    pallas_call x4, Pallas kernels, project(): pl.pallas_call(functools.partial(project_kernel, terms, len(used)), grid=...  11.3 us
    ppermute x4, waiting for transfers between devices, body(): lax.ppermute(part, AXES, perm)  10.7 us
    pallas_call x1, Pallas kernels, rest_part(): pl.pallas_call(rest_kernel, grid_spec=pltpu.PrefetchScalarGridSpec(num_sc...  9.61 us
    ppermute x4, starting transfers between devices, body(): lax.ppermute(part, AXES, perm)  7.56 us
    pallas_call x1, Pallas kernels, key_part(): pl.pallas_call(key_kernel, grid_spec=pltpu.PrefetchScalarGridSpec(num_sca...  4.04 us
  transfers between devices with their start and end apart: 30, of which 17 were waited for; matrix products, arithmetic and copies ran while one was open for 3% of the time, Pallas kernels for 11%

profile of v1, /device:TPU:0, one launch (start us, length us, event | category | flops | bytes accessed | tf_op | source)
XLA Modules:
  0.0 189.5 jit_solution(12322542557377471266)
XLA Ops:
  0.0 4.0 %key_part.1 = (f32[4,264,128]{2,1,0:T(8,128)}, f32[4,256,256]{2,1,0:T(8,128)}) custom-call(s32[1]{0:T(128)} %bitcast.first, f32[256,1024]{1,0:T(8,128)} %refs_0_.1, f32[8,128,128]{2,1,0:T(8,128)} %refs_1_.1, f32[256,1024]{1,0:T(8,128)} %refs_7_.1), custom_call_target="tpu_custom_call" | custom-call | flops 603979776 | bytes 3145728 | tf_op jit(solution)/shard_map/key_part/pallas_call | solution.py:231
  4.0 2.9 %collective-permute-start = (f32[4,264,128]{2,1,0:T(8,128)}, f32[4,264,128]{2,1,0:T(8,128)}, u32[]{:S(2)}, u32[]{:S(2)}) collective-permute-start(f32[4,264,128]{2,1,0:T(8,128)} %get-tuple-element.70), channel_id=1, source_target_pairs={{0,4},{1,5},{2,6},{3,7},{4,0},{5,1},{6,2},{7,3},{8,12},{9,13},{10,... | collective-permute-start | bytes 1622024 | tf_op jit(solution)/shard_map/ppermute | solution.py:213
  10.0 2.6 %collective-permute-start.1 = (f32[512,128]{1,0:T(8,128)S(1)}, f32[512,128]{1,0:T(8,128)S(1)}, u32[]{:S(2)}, u32[]{:S(2)}) collective-permute-start(f32[512,128]{1,0:T(8,128)S(1)} %get-tuple-element.74), channel_id=1, source_target_pairs={{0,16},{1,17},{2,18},{3,19},{4,20},{5,21},{6,22},{7,23},{8,24},{9,... | collective-permute-start | bytes 786440 | tf_op jit(solution)/shard_map/ppermute | solution.py:213
  18.4 9.6 %rest_part.1 = (f32[4,264,128]{2,1,0:T(8,128)S(1)}, f32[4,256,256]{2,1,0:T(8,128)S(1)}, f32[4,256,128]{2,1,0:T(8,128)S(1)}, f32[4,256,128]{2,1,0:T(8,128)S(1)}, ...) custom-call(s32[2]{0:T(128)S(1)} %pad_add_fusion.first, ...), custom_call_target="tpu_custom_call" | custom-call | flops 3422552064 | bytes 8388608 | tf_op jit(solution)/shard_map/rest_part/pallas_call | solution.py:258
  36.6 17.7 %collective-permute-done.2 = f32[4,264,128]{2,1,0:T(8,128)S(1)} collective-permute-done((f32[4,264,128]{2,1,0:T(8,128)S(1)}, f32[4,264,128]{2,1,0:T(8,128)S(1)}, u32[]{:S(2)}, u32[]{:S(2)}) %collective-permute-start.2) | collective-permute-done | bytes 540704 | tf_op jit(solution)/shard_map/ppermute | solution.py:213
  58.6 4.2 %collective-permute-done.3.refs_16_.refs_8_ = f32[1024,128]{1,0:T(8,128)} collective-permute-done((f32[1024,128]{1,0:T(8,128)}, f32[1024,128]{1,0:T(8,128)}, u32[]{:S(2)}, u32[]{:S(2)}) %collective-permute-start.3) | collective-permute-done | bytes 524320 | tf_op jit(solution)/shard_map/ppermute | solution.py:213
  66.6 4.7 %collective-permute-done.8 = f32[2,264,128]{2,1,0:T(8,128)} collective-permute-done((f32[2,264,128]{2,1,0:T(8,128)S(1)}, f32[2,264,128]{2,1,0:T(8,128)}, u32[]{:S(2)}, u32[]{:S(2)}) %collective-permute-start.8) | collective-permute-done | bytes 270368 | tf_op jit(solution)/shard_map/ppermute | solution.py:213
  73.3 11.5 %collective-permute-start.10 = (f32[512,128]{1,0:T(8,128)}, f32[512,128]{1,0:T(8,128)S(1)}, u32[]{:S(2)}, u32[]{:S(2)}) collective-permute-start(f32[512,128]{1,0:T(8,128)} %copy-done.22), channel_id=1, source_target_pairs={{0,16},{1,17},{2,18},{3,19},{4,20},{5,21},{6,22},{7,23},{8,24},{9,... | collective-permute-start | bytes 786440 | tf_op jit(solution)/shard_map/ppermute | solution.py:213
  85.9 7.4 %collective-permute-done.12.refs_9_ = f32[512,128]{1,0:T(8,128)S(1)} collective-permute-done((f32[512,128]{1,0:T(8,128)S(1)}, f32[512,128]{1,0:T(8,128)S(1)}, u32[]{:S(2)}, u32[]{:S(2)}) %collective-permute-start.12) | collective-permute-done | bytes 262176 | tf_op jit(solution)/shard_map/ppermute | solution.py:213
  93.3 3.3 %collective-permute-done.10.refs_4_ = f32[512,128]{1,0:T(8,128)S(1)} collective-permute-done((f32[512,128]{1,0:T(8,128)}, f32[512,128]{1,0:T(8,128)S(1)}, u32[]{:S(2)}, u32[]{:S(2)}) %collective-permute-start.10) | collective-permute-done | bytes 262176 | tf_op jit(solution)/shard_map/ppermute | solution.py:213
  99.8 3.0 %collective-permute-start.16 = (f32[256,512]{1,0:T(8,128)S(1)}, f32[256,512]{1,0:T(8,128)S(1)}, u32[]{:S(2)}, u32[]{:S(2)}) collective-permute-start(f32[256,512]{1,0:T(8,128)S(1)} %mix.2.refs_0_), channel_id=1, source_target_pairs={{0,8},{1,9},{2,10},{3,11},{4,12},{5,13},{6,14},{7,15},{8,0},{9,1},... | collective-permute-start | bytes 1572872 | tf_op jit(solution)/shard_map/ppermute | solution.py:213
  104.6 10.9 %collective-permute-done.15.refs_17_ = f32[512,128]{1,0:T(8,128)S(1)} collective-permute-done((f32[512,128]{1,0:T(8,128)S(1)}, f32[512,128]{1,0:T(8,128)S(1)}, u32[]{:S(2)}, u32[]{:S(2)}) %collective-permute-start.15) | collective-permute-done | bytes 262176 | tf_op jit(solution)/shard_map/ppermute | solution.py:213
  115.5 6.6 %collective-permute-done.14.refs_6_.refs_13_ = f32[1024,128]{1,0:T(8,128)S(1)} collective-permute-done((f32[1024,128]{1,0:T(8,128)}, f32[1024,128]{1,0:T(8,128)S(1)}, u32[]{:S(2)}, u32[]{:S(2)}) %collective-permute-start.14) | collective-permute-done | bytes 524320 | tf_op jit(solution)/shard_map/ppermute | solution.py:213
  126.0 3.5 %collective-permute-start.20 = (f32[1024,128]{1,0:T(8,128)}, f32[1024,128]{1,0:T(8,128)S(1)}, u32[]{:S(2)}, u32[]{:S(2)}) collective-permute-start(f32[1024,128]{1,0:T(8,128)} %collective-permute-done.7), channel_id=1, source_target_pairs={{0,16},{1,17},{2,18},{3,19},{4,20},{5,21},{6,22},{7,23},{8,24},{9,... | collective-permute-start | bytes 1572872 | tf_op jit(solution)/shard_map/ppermute | solution.py:213
  131.6 16.5 %collective-permute-done.18.refs_1_ = f32[256,512]{1,0:T(8,128)S(1)} collective-permute-done((f32[256,512]{1,0:T(8,128)S(1)}, f32[256,512]{1,0:T(8,128)S(1)}, u32[]{:S(2)}, u32[]{:S(2)}) %collective-permute-start.18) | collective-permute-done | bytes 524320 | tf_op jit(solution)/shard_map/ppermute | solution.py:213
  148.0 2.3 %collective-permute-done.20.refs_4_.refs_8_ = f32[1024,128]{1,0:T(8,128)S(1)} collective-permute-done((f32[1024,128]{1,0:T(8,128)}, f32[1024,128]{1,0:T(8,128)S(1)}, u32[]{:S(2)}, u32[]{:S(2)}) %collective-permute-start.20) | collective-permute-done | bytes 524320 | tf_op jit(solution)/shard_map/ppermute | solution.py:213
  150.4 2.4 %collective-permute-done.22.refs_5_.refs_9_ = f32[1024,128]{1,0:T(8,128)S(1)} collective-permute-done((f32[1024,128]{1,0:T(8,128)S(1)}, f32[1024,128]{1,0:T(8,128)S(1)}, u32[]{:S(2)}, u32[]{:S(2)}) %collective-permute-start.22) | collective-permute-done | bytes 524320 | tf_op jit(solution)/shard_map/ppermute | solution.py:213
  153.4 4.6 %project.4.refs_10_ = f32[512,1024]{1,0:T(8,128)S(1)} custom-call(f32[256,512]{1,0:T(8,128)S(1)} %mix.2.refs_0_, f32[256,512]{1,0:T(8,128)S(1)} %collective-permute-done.16.refs_0_.refs_1_, f32[256,512]{1,0:T(8,128)S(1)} %collective-permute-done.17.refs_2_, f32[512,512]{1,0:T(8,128)S(1)} %collective-permute-done.19.refs_3_.refs_0_.refs_4_, ...), custom_call_target="tpu_custom_call" | custom-call | flops 2818572288 | bytes 5767168 | tf_op jit(solution)/shard_map/project/pallas_call | solution.py:430
  158.0 2.9 %project.5.refs_6_.refs_12_ = f32[512,1024]{1,0:T(8,128)S(1)} custom-call(f32[256,512]{1,0:T(8,128)S(1)} %get-tuple-element.112.refs_0_, f32[256,512]{1,0:T(8,128)S(1)} %collective-permute-done.18.refs_1_, f32[2048,128]{1,0:T(8,128)S(1)} %collective-permute-done.5.refs_4_.refs_11_.refs_2_.refs_6_, ...), custom_call_target="tpu_custom_call" | custom-call | flops 1610612736 | bytes 4194304 | tf_op jit(solution)/shard_map/project/pallas_call | solution.py:430
  163.0 2.9 %project.7 = f32[512,512]{1,0:T(8,128)S(1)} custom-call(f32[256,512]{1,0:T(8,128)S(1)} %mix.2.refs_0_, f32[256,512]{1,0:T(8,128)S(1)} %collective-permute-done.16.refs_0_.refs_1_, f32[256,512]{1,0:T(8,128)S(1)} %collective-permute-done.17.refs_2_, f32[512,512]{1,0:T(8,128)S(1)} %collective-permute-done.19.refs_3_.refs_0_.refs_4_, ...), custom_call_target="tpu_custom_call" | custom-call | flops 1207959552 | bytes 2621440 | tf_op jit(solution)/shard_map/project/pallas_call | solution.py:430
  170.1 3.0 %collective-permute-start.27 = (f32[256,256]{1,0:T(8,128)S(1)}, f32[256,256]{1,0:T(8,128)S(1)}, u32[]{:S(2)}, u32[]{:S(2)}) collective-permute-start(f32[256,256]{1,0:T(8,128)S(1)} %get-tuple-element.130), channel_id=1, source_target_pairs={{0,2},{1,0},{2,10},{3,8},{4,6},{5,4},{6,14},{7,12},{8,3},{9,1},{10... | collective-permute-start | bytes 786440 | tf_op jit(solution)/shard_map/ppermute | solution.py:481
  174.0 2.9 %collective-permute-start.29 = (f32[256,256]{1,0:T(8,128)S(1)}, f32[256,256]{1,0:T(8,128)S(1)}, u32[]{:S(2)}, u32[]{:S(2)}) collective-permute-start(f32[256,256]{1,0:T(8,128)S(1)} %get-tuple-element.132), channel_id=1, source_target_pairs={{0,10},{1,8},{2,2},{3,0},{4,14},{5,12},{6,6},{7,4},{8,11},{9,9},{1... | collective-permute-start | bytes 786440 | tf_op jit(solution)/shard_map/ppermute | solution.py:481
  177.0 6.1 %collective-permute-done.27.refs_1_ = f32[256,256]{1,0:T(8,128)S(1)} collective-permute-done((f32[256,256]{1,0:T(8,128)S(1)}, f32[256,256]{1,0:T(8,128)S(1)}, u32[]{:S(2)}, u32[]{:S(2)}) %collective-permute-start.27) | collective-permute-done | bytes 262176 | tf_op jit(solution)/shard_map/ppermute | solution.py:481
  183.1 2.3 %collective-permute-done.28.refs_2_ = f32[256,256]{1,0:T(8,128)S(1)} collective-permute-done((f32[256,256]{1,0:T(8,128)S(1)}, f32[256,256]{1,0:T(8,128)S(1)}, u32[]{:S(2)}, u32[]{:S(2)}) %collective-permute-start.28) | collective-permute-done | bytes 262176 | tf_op jit(solution)/shard_map/ppermute | solution.py:481
  (109 shorter events, 51.3 us)
Async XLA Ops:
  4.0 28.3 %collective-permute-start = (f32[4,264,128]{2,1,0:T(8,128)}, f32[4,264,128]{2,1,0:T(8,128)}, u32[]{:S(2)}, u32[]{:S(2)}) collective-permute-start(f32[4,264,128]{2,1,0:T(8,128)} %get-tuple-element.70), channel_id=1, source_target_pairs={{0,4},{1,5},{2,6},{3,7},{4,0},{5,1},{6,2},{7,3},{8,12},{9,13},{10,... | collective-permute-start | bytes 1622024 | tf_op jit(solution)/shard_map/ppermute | solution.py:213
  10.0 22.3 %collective-permute-start.1 = (f32[512,128]{1,0:T(8,128)S(1)}, f32[512,128]{1,0:T(8,128)S(1)}, u32[]{:S(2)}, u32[]{:S(2)}) collective-permute-start(f32[512,128]{1,0:T(8,128)S(1)} %get-tuple-element.74), channel_id=1, source_target_pairs={{0,16},{1,17},{2,18},{3,19},{4,20},{5,21},{6,22},{7,23},{8,24},{9,... | collective-permute-start | bytes 786440 | tf_op jit(solution)/shard_map/ppermute | solution.py:213
  33.8 20.5 %collective-permute-start.2 = (f32[4,264,128]{2,1,0:T(8,128)S(1)}, f32[4,264,128]{2,1,0:T(8,128)S(1)}, u32[]{:S(2)}, u32[]{:S(2)}) collective-permute-start(f32[4,264,128]{2,1,0:T(8,128)S(1)} %add.54), channel_id=1, source_target_pairs={{0,8},{1,9},{2,10},{3,11},{4,12},{5,13},{6,14},{7,15},{8,0},{9,1},... | collective-permute-start | bytes 1622024 | tf_op jit(solution)/shard_map/ppermute | solution.py:213
  35.5 27.4 %collective-permute-start.4 = (f32[2048,128]{1,0:T(8,128)S(1)}, f32[2048,128]{1,0:T(8,128)S(1)}, u32[]{:S(2)}, u32[]{:S(2)}) collective-permute-start(f32[2048,128]{1,0:T(8,128)S(1)} %get-tuple-element.84.refs_7_.refs_14_.refs_6_.refs_2_), channel_id=1, source_target_pairs={{0,4},{1,5},{2,6},{3,7},{4,0},{5,1},{6,2},{7,3},{8,12},{9,13},{10,... | collective-permute-start | bytes 3145736 | tf_op jit(solution)/shard_map/ppermute | solution.py:213
  36.0 26.9 %collective-permute-start.5 = (f32[2048,128]{1,0:T(8,128)}, f32[2048,128]{1,0:T(8,128)S(1)}, u32[]{:S(2)}, u32[]{:S(2)}) collective-permute-start(f32[2048,128]{1,0:T(8,128)} %get-tuple-element.85), channel_id=1, source_target_pairs={{0,1},{1,0},{2,3},{3,2},{4,5},{5,4},{6,7},{7,6},{8,9},{9,8},{10,11... | collective-permute-start | bytes 3145736 | tf_op jit(solution)/shard_map/ppermute | solution.py:213
  36.0 26.8 %collective-permute-start.3 = (f32[1024,128]{1,0:T(8,128)}, f32[1024,128]{1,0:T(8,128)}, u32[]{:S(2)}, u32[]{:S(2)}) collective-permute-start(f32[1024,128]{1,0:T(8,128)} %get-tuple-element.83), channel_id=1, source_target_pairs={{0,16},{1,17},{2,18},{3,19},{4,20},{5,21},{6,22},{7,23},{8,24},{9,... | collective-permute-start | bytes 1572872 | tf_op jit(solution)/shard_map/ppermute | solution.py:213
  36.4 26.4 %collective-permute-start.6 = (f32[1024,128]{1,0:T(8,128)}, f32[1024,128]{1,0:T(8,128)}, u32[]{:S(2)}, u32[]{:S(2)}) collective-permute-start(f32[1024,128]{1,0:T(8,128)} %get-tuple-element.86), channel_id=1, source_target_pairs={{0,1},{1,0},{2,3},{3,2},{4,5},{5,4},{6,7},{7,6},{8,9},{9,8},{10,11... | collective-permute-start | bytes 1572872 | tf_op jit(solution)/shard_map/ppermute | solution.py:213
  62.9 33.7 %collective-permute-start.11 = (f32[2048,128]{1,0:T(8,128)S(1)}, f32[2048,128]{1,0:T(8,128)}, u32[]{:S(2)}, u32[]{:S(2)}) collective-permute-start(f32[2048,128]{1,0:T(8,128)S(1)} %collective-permute-done.5.refs_4_.refs_11_.refs_2_.refs_6_), channel_id=1, source_target_pairs={{0,4},{1,5},{2,6},{3,7},{4,0},{5,1},{6,2},{7,3},{8,12},{9,13},{10,... | collective-permute-start | bytes 3145736 | tf_op jit(solution)/shard_map/ppermute | solution.py:213
  71.4 13.4 %collective-permute-start.9 = (f32[2,264,128]{2,1,0:T(8,128)}, f32[2,264,128]{2,1,0:T(8,128)}, u32[]{:S(2)}, u32[]{:S(2)}) collective-permute-start(f32[2,264,128]{2,1,0:T(8,128)} %collective-permute-done.8), channel_id=1, source_target_pairs={{16,24},{17,25},{18,26},{19,27},{20,28},{21,29},{22,30},{23,31},{2... | collective-permute-start | bytes 811016 | tf_op jit(solution)/shard_map/ppermute | solution.py:213
  72.7 20.5 %collective-permute-start.12 = (f32[512,128]{1,0:T(8,128)S(1)}, f32[512,128]{1,0:T(8,128)S(1)}, u32[]{:S(2)}, u32[]{:S(2)}) collective-permute-start(f32[512,128]{1,0:T(8,128)S(1)} %collective-permute-done.1.refs_9_), channel_id=1, source_target_pairs={{0,4},{1,5},{2,6},{3,7},{4,0},{5,1},{6,2},{7,3},{8,12},{9,13},{10,... | collective-permute-start | bytes 786440 | tf_op jit(solution)/shard_map/ppermute | solution.py:213
  73.3 23.3 %collective-permute-start.10 = (f32[512,128]{1,0:T(8,128)}, f32[512,128]{1,0:T(8,128)S(1)}, u32[]{:S(2)}, u32[]{:S(2)}) collective-permute-start(f32[512,128]{1,0:T(8,128)} %copy-done.22), channel_id=1, source_target_pairs={{0,16},{1,17},{2,18},{3,19},{4,20},{5,21},{6,22},{7,23},{8,24},{9,... | collective-permute-start | bytes 786440 | tf_op jit(solution)/shard_map/ppermute | solution.py:213
  96.8 26.3 %collective-permute-start.13 = (f32[4,264,128]{2,1,0:T(8,128)S(1)}, f32[4,264,128]{2,1,0:T(8,128)S(1)}, u32[]{:S(2)}, u32[]{:S(2)}) collective-permute-start(f32[4,264,128]{2,1,0:T(8,128)S(1)} %get-tuple-element.134), channel_id=1, source_target_pairs={{0,4},{1,5},{2,6},{3,7},{4,0},{5,1},{6,2},{7,3},{8,12},{9,13},{10,... | collective-permute-start | bytes 1622024 | tf_op jit(solution)/shard_map/ppermute | solution.py:213
  98.6 23.5 %collective-permute-start.14 = (f32[1024,128]{1,0:T(8,128)}, f32[1024,128]{1,0:T(8,128)S(1)}, u32[]{:S(2)}, u32[]{:S(2)}) collective-permute-start(f32[1024,128]{1,0:T(8,128)} %collective-permute-done.6), channel_id=1, source_target_pairs={{0,16},{1,17},{2,18},{3,19},{4,20},{5,21},{6,22},{7,23},{8,24},{9,... | collective-permute-start | bytes 1572872 | tf_op jit(solution)/shard_map/ppermute | solution.py:213
  99.8 23.3 %collective-permute-start.16 = (f32[256,512]{1,0:T(8,128)S(1)}, f32[256,512]{1,0:T(8,128)S(1)}, u32[]{:S(2)}, u32[]{:S(2)}) collective-permute-start(f32[256,512]{1,0:T(8,128)S(1)} %mix.2.refs_0_), channel_id=1, source_target_pairs={{0,8},{1,9},{2,10},{3,11},{4,12},{5,13},{6,14},{7,15},{8,0},{9,1},... | collective-permute-start | bytes 1572872 | tf_op jit(solution)/shard_map/ppermute | solution.py:213
  102.8 20.2 %collective-permute-start.17 = (f32[256,512]{1,0:T(8,128)S(1)}, f32[256,512]{1,0:T(8,128)S(1)}, u32[]{:S(2)}, u32[]{:S(2)}) collective-permute-start(f32[256,512]{1,0:T(8,128)S(1)} %mix.2.refs_0_), channel_id=1, source_target_pairs={{0,2},{1,3},{2,0},{3,1},{4,6},{5,7},{6,4},{7,5},{8,10},{9,11},{10,... | collective-permute-start | bytes 1572872 | tf_op jit(solution)/shard_map/ppermute | solution.py:213
  104.3 11.2 %collective-permute-start.15 = (f32[512,128]{1,0:T(8,128)S(1)}, f32[512,128]{1,0:T(8,128)S(1)}, u32[]{:S(2)}, u32[]{:S(2)}) collective-permute-start(f32[512,128]{1,0:T(8,128)S(1)} %collective-permute-done.10.refs_4_), channel_id=1, source_target_pairs={{0,4},{1,5},{2,6},{3,7},{4,0},{5,1},{6,2},{7,3},{8,12},{9,13},{10,... | collective-permute-start | bytes 786440 | tf_op jit(solution)/shard_map/ppermute | solution.py:213
  124.4 28.4 %collective-permute-start.19 = (f32[512,512]{1,0:T(8,128)S(1)}, f32[512,512]{1,0:T(8,128)S(1)}, u32[]{:S(2)}, u32[]{:S(2)}) collective-permute-start(f32[512,512]{1,0:T(8,128)S(1)} %get-tuple-element.113), channel_id=1, source_target_pairs={{0,2},{1,3},{2,0},{3,1},{4,6},{5,7},{6,4},{7,5},{8,10},{9,11},{10,... | collective-permute-start | bytes 3145736 | tf_op jit(solution)/shard_map/ppermute | solution.py:213
  126.0 22.0 %collective-permute-start.18 = (f32[256,512]{1,0:T(8,128)S(1)}, f32[256,512]{1,0:T(8,128)S(1)}, u32[]{:S(2)}, u32[]{:S(2)}) collective-permute-start(f32[256,512]{1,0:T(8,128)S(1)} %get-tuple-element.112.refs_0_), channel_id=1, source_target_pairs={{0,8},{1,9},{2,10},{3,11},{4,12},{5,13},{6,14},{7,15},{8,0},{9,1},... | collective-permute-start | bytes 1572872 | tf_op jit(solution)/shard_map/ppermute | solution.py:213
  126.0 24.4 %collective-permute-start.20 = (f32[1024,128]{1,0:T(8,128)}, f32[1024,128]{1,0:T(8,128)S(1)}, u32[]{:S(2)}, u32[]{:S(2)}) collective-permute-start(f32[1024,128]{1,0:T(8,128)} %collective-permute-done.7), channel_id=1, source_target_pairs={{0,16},{1,17},{2,18},{3,19},{4,20},{5,21},{6,22},{7,23},{8,24},{9,... | collective-permute-start | bytes 1572872 | tf_op jit(solution)/shard_map/ppermute | solution.py:213
  129.5 20.8 %collective-permute-start.21 = (f32[1024,128]{1,0:T(8,128)}, f32[1024,128]{1,0:T(8,128)S(1)}, u32[]{:S(2)}, u32[]{:S(2)}) collective-permute-start(f32[1024,128]{1,0:T(8,128)} %collective-permute-done.3.refs_16_.refs_8_), channel_id=1, source_target_pairs={{0,4},{1,5},{2,6},{3,7},{4,0},{5,1},{6,2},{7,3},{8,12},{9,13},{10,... | collective-permute-start | bytes 1572872 | tf_op jit(solution)/shard_map/ppermute | solution.py:213
  129.9 22.9 %collective-permute-start.22 = (f32[1024,128]{1,0:T(8,128)S(1)}, f32[1024,128]{1,0:T(8,128)S(1)}, u32[]{:S(2)}, u32[]{:S(2)}) collective-permute-start(f32[1024,128]{1,0:T(8,128)S(1)} %collective-permute-done.14.refs_6_.refs_13_), channel_id=1, source_target_pairs={{0,4},{1,5},{2,6},{3,7},{4,0},{5,1},{6,2},{7,3},{8,12},{9,13},{10,... | collective-permute-start | bytes 1572872 | tf_op jit(solution)/shard_map/ppermute | solution.py:213
  170.1 13.0 %collective-permute-start.27 = (f32[256,256]{1,0:T(8,128)S(1)}, f32[256,256]{1,0:T(8,128)S(1)}, u32[]{:S(2)}, u32[]{:S(2)}) collective-permute-start(f32[256,256]{1,0:T(8,128)S(1)} %get-tuple-element.130), channel_id=1, source_target_pairs={{0,2},{1,0},{2,10},{3,8},{4,6},{5,4},{6,14},{7,12},{8,3},{9,1},{10... | collective-permute-start | bytes 786440 | tf_op jit(solution)/shard_map/ppermute | solution.py:481
  173.1 12.3 %collective-permute-start.28 = (f32[256,256]{1,0:T(8,128)S(1)}, f32[256,256]{1,0:T(8,128)S(1)}, u32[]{:S(2)}, u32[]{:S(2)}) collective-permute-start(f32[256,256]{1,0:T(8,128)S(1)} %get-tuple-element.131), channel_id=1, source_target_pairs={{0,8},{1,10},{2,0},{3,2},{4,12},{5,14},{6,4},{7,6},{8,9},{9,11},{1... | collective-permute-start | bytes 786440 | tf_op jit(solution)/shard_map/ppermute | solution.py:481
  174.0 13.7 %collective-permute-start.29 = (f32[256,256]{1,0:T(8,128)S(1)}, f32[256,256]{1,0:T(8,128)S(1)}, u32[]{:S(2)}, u32[]{:S(2)}) collective-permute-start(f32[256,256]{1,0:T(8,128)S(1)} %get-tuple-element.132), channel_id=1, source_target_pairs={{0,10},{1,8},{2,2},{3,0},{4,14},{5,12},{6,6},{7,4},{8,11},{9,9},{1... | collective-permute-start | bytes 786440 | tf_op jit(solution)/shard_map/ppermute | solution.py:481
  (32 other events, 263.1 us)

commit v2 on v1

--- a/solution.py
+++ b/solution.py
@@ -203,7 +203,7 @@
     me = c * heads + h
     odd = c & 1
 
-    def swap(x, by_ctx, by_head=0, keep=lambda c: True):
+    def swap(x, by_ctx, by_head=0, keep=lambda source: True):
         pairs = [
             (i * heads + j, (i ^ by_ctx) * heads + (j ^ by_head))
             for i in range(ctx)
@@ -265,7 +265,7 @@
                 out_specs=[head_block(*shape.shape[1:]) for shape in shapes],
             ),
             out_shape=shapes,
-            compiler_params=params(40),
+            compiler_params=params(48),
             name="rest_part",
             cost_estimate=cost(
                 6 * half * rows * (head_size * (3 * feat_half + feat_size) + 2 * rows * (feat_size + head_size)),
@@ -322,7 +322,7 @@
                 scratch_shapes=[pltpu.SemaphoreType.DMA((count,))],
             ),
             out_shape=shapes,
-            compiler_params=params(12),
+            compiler_params=params(16),
             name="arrange",
             cost_estimate=cost(0, 2 * count * wide * strip_width),
         )(starts, weight)
@@ -367,19 +367,17 @@
         before = before + jnp.where((c & bit) != 0, got, 0.0)
         total = total + got
         bit *= 2
-    total, before, far_2, kept_near, taken, taken_1, taken_2, send_here, place_here, far_1 = together(
-        (total, before, far_2, kept_near, taken, taken_1, taken_2, send_here, place_here, far_1)
+    total, before, far_2, kept_near, taken, taken_1, taken_2, far_1 = together(
+        (total, before, far_2, kept_near, taken, taken_1, taken_2, far_1)
     )
     taken_near = swap(taken, near)
     both_1 = swap(far_1, near)
-    second = (c & PAIR) != 0
-    got = swap(jnp.where(second, total[half // 2 :], total[: half // 2]), bit, keep=lambda i: not i & bit)
+    got = swap(total, bit | PAIR, keep=lambda i: i & PAIR and not i & bit)
     got, kept_parts[2] = together((got, kept_parts[2]))
-    met = swap(got, PAIR, keep=lambda i: i & bit)
+    met = swap(got, PAIR, keep=lambda i: i & bit and not i & PAIR)
     far_3 = swap(kept_parts[2], far)
-    got = jnp.concatenate([jnp.where(second, met, got), jnp.where(second, got, met)])
-    got, far_3, taken_near, both_1, taken_1 = together((got, far_3, taken_near, both_1, taken_1))
-    before = before + got
+    met, far_3, taken_near, both_1, taken_1 = together((met, far_3, taken_near, both_1, taken_1))
+    before = before + got + met
 
     other_prior = swap(before + jnp.where(odd == 0, earlier, 0.0), 1)
     own_mixed = mix(*own_query, before + jnp.where(odd == 1, earlier, 0.0))
@@ -403,7 +401,9 @@
     far_5 = swap(taken_2, far)
     both_2 = swap(far_2, near)
     both_4 = swap(far_4, near)
-    other_met, both, far_5, both_2, both_4 = together((other_met, both, far_5, both_2, both_4))
+    other_met, both, far_5, both_2, both_4, send_here, place_here = together(
+        (other_met, both, far_5, both_2, both_4, send_here, place_here)
+    )
     both_5 = swap(far_5, near)
     last = swap(other_met, 0, head_bits[0])
     own_pieces = spread(

time: 190 us -> 195 us (1.026)
  waiting for transfers between devices: 91.5 us -> 84.6 us
  Pallas kernels: 32.3 us -> 36.5 us
  starting transfers between devices: 47.4 us -> 51.2 us
  local copies, waits for them, and re-layouts: 13 us -> 16.3 us
    ppermute x26, waiting for transfers between devices: 80.8 us -> 74.2 us  [swap(): return lax.ppermute(x, AXES, pairs)]
    ppermute x26, starting transfers between devices: 39.8 us -> 43.2 us  [swap(): return lax.ppermute(x, AXES, pairs)]
    unnamed x52 -> x64, local copies, waits for them, and re-layouts: 11.6 us -> 14.9 us
    pallas_call x4, Pallas kernels: 11.3 us -> 13.5 us  [project(): pl.pallas_call(functools.partial(project_kernel, terms, len(used)), grid=...]
  transfers between devices with their start and end apart: 30 -> 30, of which waited for: 17 -> 13; matrix products, arithmetic and copies ran while one was open for 3% -> 2% of each run, Pallas kernels for 11% -> 13%
where the time goes in v2:
time: 195 us; the launch traced here: 194 us
  waiting for transfers between devices  84.6 us (43%)
  starting transfers between devices  51.2 us (26%)
  Pallas kernels  36.5 us (19%)
  local copies, waits for them, and re-layouts  16.3 us (8%)
  other arithmetic  5.36 us (3%)
    ppermute x26, waiting for transfers between devices, swap(): return lax.ppermute(x, AXES, pairs)  74.2 us
    ppermute x26, starting transfers between devices, swap(): return lax.ppermute(x, AXES, pairs)  43.2 us
    unnamed x64, local copies, waits for them, and re-layouts  14.9 us
    pallas_call x4, Pallas kernels, project(): pl.pallas_call(functools.partial(project_kernel, terms, len(used)), grid=...  13.5 us
    pallas_call x1, Pallas kernels, rest_part(): pl.pallas_call(rest_kernel, grid_spec=pltpu.PrefetchScalarGridSpec(num_sc...  10.6 us
    ppermute x4, waiting for transfers between devices, body(): lax.ppermute(part, AXES, perm)  10.4 us
    ppermute x4, starting transfers between devices, body(): lax.ppermute(part, AXES, perm)  8.09 us
    pallas_call x1, Pallas kernels, key_part(): pl.pallas_call(key_kernel, grid_spec=pltpu.PrefetchScalarGridSpec(num_sca...  4.02 us
  transfers between devices with their start and end apart: 30, of which 13 were waited for; matrix products, arithmetic and copies ran while one was open for 2% of the time, Pallas kernels for 13%

profile of v2, /device:TPU:0, one launch (start us, length us, event | category | flops | bytes accessed | tf_op | source)
XLA Modules:
  0.0 194.3 jit_solution(12282584366702434228)
XLA Ops:
  0.0 4.0 %key_part.1 = (f32[4,264,128]{2,1,0:T(8,128)}, f32[4,256,256]{2,1,0:T(8,128)}) custom-call(s32[1]{0:T(128)} %bitcast.1.first, f32[256,1024]{1,0:T(8,128)} %refs_0_.1, f32[8,128,128]{2,1,0:T(8,128)} %refs_1_.1, f32[256,1024]{1,0:T(8,128)} %refs_7_.1), custom_call_target="tpu_custom_call" | custom-call | flops 603979776 | bytes 3145728 | tf_op jit(solution)/shard_map/key_part/pallas_call | solution.py:231
  4.0 2.9 %collective-permute-start = (f32[4,264,128]{2,1,0:T(8,128)}, f32[4,264,128]{2,1,0:T(8,128)}, u32[]{:S(2)}, u32[]{:S(2)}) collective-permute-start(f32[4,264,128]{2,1,0:T(8,128)} %get-tuple-element.74), channel_id=1, source_target_pairs={{0,4},{1,5},{2,6},{3,7},{4,0},{5,1},{6,2},{7,3},{8,12},{9,13},{10,... | collective-permute-start | bytes 1622024 | tf_op jit(solution)/shard_map/ppermute | solution.py:213
  7.0 2.3 %arrange.1 = (f32[512,128]{1,0:T(8,128)S(1)}, f32[1024,128]{1,0:T(8,128)}, f32[512,128]{1,0:T(8,128)}, f32[2048,128]{1,0:T(8,128)S(1)}, f32[1024,128]{1,0:T(8,12...) custom-call(s32[8]{0:T(128)S(1)} %stack.35.starts, f32[4096,128]{1,0:T(8,128)S(1)} %copy-done.12), custom_call_target="tpu_custom_call" | custom-call | bytes 8388608 | tf_op jit(solution)/shard_map/arrange/pallas_call | solution.py:315
  9.4 2.7 %collective-permute-start.1 = (f32[512,128]{1,0:T(8,128)S(1)}, f32[512,128]{1,0:T(8,128)S(1)}, u32[]{:S(2)}, u32[]{:S(2)}) collective-permute-start(f32[512,128]{1,0:T(8,128)S(1)} %get-tuple-element.77), channel_id=1, source_target_pairs={{0,16},{1,17},{2,18},{3,19},{4,20},{5,21},{6,22},{7,23},{8,24},{9,... | collective-permute-start | bytes 786440 | tf_op jit(solution)/shard_map/ppermute | solution.py:213
  14.2 10.6 %rest_part.1 = (f32[4,264,128]{2,1,0:T(8,128)S(1)}, f32[4,256,256]{2,1,0:T(8,128)S(1)}, f32[4,256,128]{2,1,0:T(8,128)S(1)}, f32[4,256,128]{2,1,0:T(8,128)S(1)}, ...) custom-call(s32[2]{0:T(128)S(1)} %pad_add_fusion.first, f32[256,1024]{1,0:T(8,128)} %refs_0_.1, ...), custom_call_target="tpu_custom_call" | custom-call | flops 3422552064 | bytes 8388608 | tf_op jit(solution)/shard_map/rest_part/pallas_call | solution.py:258
  33.3 17.7 %collective-permute-done.2 = f32[4,264,128]{2,1,0:T(8,128)S(1)} collective-permute-done((f32[4,264,128]{2,1,0:T(8,128)S(1)}, f32[4,264,128]{2,1,0:T(8,128)S(1)}, u32[]{:S(2)}, u32[]{:S(2)}) %collective-permute-start.2) | collective-permute-done | bytes 540704 | tf_op jit(solution)/shard_map/ppermute | solution.py:213
  51.8 2.1 %broadcast_select_fusion = (f32[4,264,128]{2,1,0:T(8,128)}, f32[4,264,128]{2,1,0:T(8,128)S(1)}) fusion(f32[4,264,128]{2,1,0:T(8,128)} %copy-done.31, pred[]{:T(512)S(6)} %ne.3, f32[4,264,128]{2,1,0:T(8,128)} %copy-done.30), kind=kLoop, calls=%fused_computation.3 | loop fusion | flops 270336 | bytes 2162689 | tf_op jit(solution)/shard_map/jit(_where)/select_n | solution.py:367
  53.9 5.7 %collective-permute-done.3.refs_16_.refs_8_ = f32[1024,128]{1,0:T(8,128)} collective-permute-done((f32[1024,128]{1,0:T(8,128)}, f32[1024,128]{1,0:T(8,128)}, u32[]{:S(2)}, u32[]{:S(2)}) %collective-permute-start.3) | collective-permute-done | bytes 524320 | tf_op jit(solution)/shard_map/ppermute | solution.py:213
  64.5 14.0 %collective-permute-start.10 = (f32[512,128]{1,0:T(8,128)}, f32[512,128]{1,0:T(8,128)}, u32[]{:S(2)}, u32[]{:S(2)}) collective-permute-start(f32[512,128]{1,0:T(8,128)} %get-tuple-element.96), channel_id=1, source_target_pairs={{0,16},{1,17},{2,18},{3,19},{4,20},{5,21},{6,22},{7,23},{8,24},{9,... | collective-permute-start | bytes 786440 | tf_op jit(solution)/shard_map/ppermute | solution.py:213
  78.5 12.9 %collective-permute-done.12.refs_9_ = f32[512,128]{1,0:T(8,128)} collective-permute-done((f32[512,128]{1,0:T(8,128)S(1)}, f32[512,128]{1,0:T(8,128)}, u32[]{:S(2)}, u32[]{:S(2)}) %collective-permute-start.12) | collective-permute-done | bytes 262176 | tf_op jit(solution)/shard_map/ppermute | solution.py:213
  96.7 2.5 %collective-permute-start.16 = (f32[256,512]{1,0:T(8,128)S(1)}, f32[256,512]{1,0:T(8,128)S(1)}, u32[]{:S(2)}, u32[]{:S(2)}) collective-permute-start(f32[256,512]{1,0:T(8,128)S(1)} %mix.2.refs_0_), channel_id=1, source_target_pairs={{0,8},{1,9},{2,10},{3,11},{4,12},{5,13},{6,14},{7,15},{8,0},{9,1},... | collective-permute-start | bytes 1572872 | tf_op jit(solution)/shard_map/ppermute | solution.py:213
  102.8 9.1 %collective-permute-done.15.refs_17_ = f32[512,128]{1,0:T(8,128)S(1)} collective-permute-done((f32[512,128]{1,0:T(8,128)}, f32[512,128]{1,0:T(8,128)S(1)}, u32[]{:S(2)}, u32[]{:S(2)}) %collective-permute-start.15) | collective-permute-done | bytes 262176 | tf_op jit(solution)/shard_map/ppermute | solution.py:213
  112.6 7.1 %collective-permute-done.14.refs_6_.refs_13_ = f32[1024,128]{1,0:T(8,128)} collective-permute-done((f32[1024,128]{1,0:T(8,128)}, f32[1024,128]{1,0:T(8,128)}, u32[]{:S(2)}, u32[]{:S(2)}) %collective-permute-start.14) | collective-permute-done | bytes 524320 | tf_op jit(solution)/shard_map/ppermute | solution.py:213
  121.6 2.4 %mix.3 = (f32[256,512]{1,0:T(8,128)}, f32[512,512]{1,0:T(8,128)}) custom-call(f32[4,256,256]{2,1,0:T(8,128)S(1)} %copy-done.14, f32[4,256,128]{2,1,0:T(8,128)S(1)} %copy-done.20, f32[4,256,128]{2,1,0:T(8,128)S(1)} %copy-done.22, f32[4,264,128]{2,1,0:T(8,128)S(1)} %collective-permute-done.13.prior_ref, f32[256,512]{1,0:T(8,128)S(1)} %collective-permute-done.16.refs_0_.refs_1_), custom_call_target="tpu_custom_call" | custom-call | flops 201326592 | bytes 3670016 | tf_op jit(solution)/shard_map/mix/pallas_call | solution.py:284
  125.5 3.4 %collective-permute-start.20 = (f32[1024,128]{1,0:T(8,128)}, f32[1024,128]{1,0:T(8,128)}, u32[]{:S(2)}, u32[]{:S(2)}) collective-permute-start(f32[1024,128]{1,0:T(8,128)} %collective-permute-done.7), channel_id=1, source_target_pairs={{0,16},{1,17},{2,18},{3,19},{4,20},{5,21},{6,22},{7,23},{8,24},{9,... | collective-permute-start | bytes 1572872 | tf_op jit(solution)/shard_map/ppermute | solution.py:213
  132.3 15.7 %collective-permute-done.18.refs_1_ = f32[256,512]{1,0:T(8,128)} collective-permute-done((f32[256,512]{1,0:T(8,128)}, f32[256,512]{1,0:T(8,128)}, u32[]{:S(2)}, u32[]{:S(2)}) %collective-permute-start.18) | collective-permute-done | bytes 524320 | tf_op jit(solution)/shard_map/ppermute | solution.py:213
  148.0 3.0 %collective-permute-done.20.refs_4_.refs_8_ = f32[1024,128]{1,0:T(8,128)} collective-permute-done((f32[1024,128]{1,0:T(8,128)}, f32[1024,128]{1,0:T(8,128)}, u32[]{:S(2)}, u32[]{:S(2)}) %collective-permute-start.20) | collective-permute-done | bytes 524320 | tf_op jit(solution)/shard_map/ppermute | solution.py:213
  159.1 4.8 %project.4.refs_10_ = f32[512,1024]{1,0:T(8,128)S(1)} custom-call(f32[256,512]{1,0:T(8,128)S(1)} %copy-done.4, f32[256,512]{1,0:T(8,128)S(1)} %copy-done.7, f32[256,512]{1,0:T(8,128)S(1)} %copy-done.10, f32[512,512]{1,0:T(8,128)S(1)} %collective-permute-done.19.refs_3_.refs_0_.refs_4_, f32[2048,128]{1,0:T(8,128)S(1)} %copy-done.1, ...), custom_call_target="tpu_custom_call" | custom-call | flops 2818572288 | bytes 5767168 | tf_op jit(solution)/shard_map/project/pallas_call | solution.py:430
  164.0 3.6 %project.5.refs_6_.refs_12_ = f32[512,1024]{1,0:T(8,128)S(1)} custom-call(f32[256,512]{1,0:T(8,128)} %get-tuple-element.110.refs_0_, f32[256,512]{1,0:T(8,128)} %collective-permute-done.18.refs_1_, f32[2048,128]{1,0:T(8,128)S(1)} %copy-done.1, f32[2048,128]{1,0:T(8,128)} %collective-permute-done.11.refs_5_.refs_12_.refs_3_.refs_7_, ...), custom_call_target="tpu_custom_call" | custom-call | flops 1610612736 | bytes 4194304 | tf_op jit(solution)/shard_map/project/pallas_call | solution.py:430
  167.6 3.0 %project.7 = f32[512,512]{1,0:T(8,128)S(1)} custom-call(f32[256,512]{1,0:T(8,128)S(1)} %copy-done.5, f32[256,512]{1,0:T(8,128)S(1)} %copy-done.7, f32[256,512]{1,0:T(8,128)S(1)} %copy-done.11, f32[512,512]{1,0:T(8,128)S(1)} %collective-permute-done.19.refs_3_.refs_0_.refs_4_, f32[512,512]{1,0:T(8,128)S(1)} %collective-permute-done.19.refs_3_.refs_0_.refs_4_, ...), custom_call_target="tpu_custom_call" | custom-call | flops 1207959552 | bytes 2621440 | tf_op jit(solution)/shard_map/project/pallas_call | solution.py:430
  174.7 3.0 %collective-permute-start.27 = (f32[256,256]{1,0:T(8,128)S(1)}, f32[256,256]{1,0:T(8,128)S(1)}, u32[]{:S(2)}, u32[]{:S(2)}) collective-permute-start(f32[256,256]{1,0:T(8,128)S(1)} %get-tuple-element.130), channel_id=1, source_target_pairs={{0,2},{1,0},{2,10},{3,8},{4,6},{5,4},{6,14},{7,12},{8,3},{9,1},{10... | collective-permute-start | bytes 786440 | tf_op jit(solution)/shard_map/ppermute | solution.py:481
  179.0 3.1 %collective-permute-start.29 = (f32[256,256]{1,0:T(8,128)S(1)}, f32[256,256]{1,0:T(8,128)S(1)}, u32[]{:S(2)}, u32[]{:S(2)}) collective-permute-start(f32[256,256]{1,0:T(8,128)S(1)} %get-tuple-element.132), channel_id=1, source_target_pairs={{0,10},{1,8},{2,2},{3,0},{4,14},{5,12},{6,6},{7,4},{8,11},{9,9},{1... | collective-permute-start | bytes 786440 | tf_op jit(solution)/shard_map/ppermute | solution.py:481
  182.2 6.9 %collective-permute-done.27.refs_1_ = f32[256,256]{1,0:T(8,128)S(1)} collective-permute-done((f32[256,256]{1,0:T(8,128)S(1)}, f32[256,256]{1,0:T(8,128)S(1)}, u32[]{:S(2)}, u32[]{:S(2)}) %collective-permute-start.27) | collective-permute-done | bytes 262176 | tf_op jit(solution)/shard_map/ppermute | solution.py:481
  189.8 2.8 %collective-permute-done.29.refs_3_ = f32[256,256]{1,0:T(8,128)S(1)} collective-permute-done((f32[256,256]{1,0:T(8,128)S(1)}, f32[256,256]{1,0:T(8,128)S(1)}, u32[]{:S(2)}, u32[]{:S(2)}) %collective-permute-start.29) | collective-permute-done | bytes 262176 | tf_op jit(solution)/shard_map/ppermute | solution.py:481
  (118 shorter events, 48.6 us)
Async XLA Ops:
  4.0 25.0 %collective-permute-start = (f32[4,264,128]{2,1,0:T(8,128)}, f32[4,264,128]{2,1,0:T(8,128)}, u32[]{:S(2)}, u32[]{:S(2)}) collective-permute-start(f32[4,264,128]{2,1,0:T(8,128)} %get-tuple-element.74), channel_id=1, source_target_pairs={{0,4},{1,5},{2,6},{3,7},{4,0},{5,1},{6,2},{7,3},{8,12},{9,13},{10,... | collective-permute-start | bytes 1622024 | tf_op jit(solution)/shard_map/ppermute | solution.py:213
  9.4 19.6 %collective-permute-start.1 = (f32[512,128]{1,0:T(8,128)S(1)}, f32[512,128]{1,0:T(8,128)S(1)}, u32[]{:S(2)}, u32[]{:S(2)}) collective-permute-start(f32[512,128]{1,0:T(8,128)S(1)} %get-tuple-element.77), channel_id=1, source_target_pairs={{0,16},{1,17},{2,18},{3,19},{4,20},{5,21},{6,22},{7,23},{8,24},{9,... | collective-permute-start | bytes 786440 | tf_op jit(solution)/shard_map/ppermute | solution.py:213
  30.5 20.5 %collective-permute-start.2 = (f32[4,264,128]{2,1,0:T(8,128)S(1)}, f32[4,264,128]{2,1,0:T(8,128)S(1)}, u32[]{:S(2)}, u32[]{:S(2)}) collective-permute-start(f32[4,264,128]{2,1,0:T(8,128)S(1)} %add.57), channel_id=1, source_target_pairs={{0,8},{1,9},{2,10},{3,11},{4,12},{5,13},{6,14},{7,15},{8,0},{9,1},... | collective-permute-start | bytes 1622024 | tf_op jit(solution)/shard_map/ppermute | solution.py:213
  32.2 27.4 %collective-permute-start.4 = (f32[2048,128]{1,0:T(8,128)S(1)}, f32[2048,128]{1,0:T(8,128)S(1)}, u32[]{:S(2)}, u32[]{:S(2)}) collective-permute-start(f32[2048,128]{1,0:T(8,128)S(1)} %get-tuple-element.87.refs_7_.refs_14_.refs_6_.refs_2_), channel_id=1, source_target_pairs={{0,4},{1,5},{2,6},{3,7},{4,0},{5,1},{6,2},{7,3},{8,12},{9,13},{10,... | collective-permute-start | bytes 3145736 | tf_op jit(solution)/shard_map/ppermute | solution.py:213
  32.7 26.9 %collective-permute-start.5 = (f32[2048,128]{1,0:T(8,128)}, f32[2048,128]{1,0:T(8,128)S(1)}, u32[]{:S(2)}, u32[]{:S(2)}) collective-permute-start(f32[2048,128]{1,0:T(8,128)} %get-tuple-element.88), channel_id=1, source_target_pairs={{0,1},{1,0},{2,3},{3,2},{4,5},{5,4},{6,7},{7,6},{8,9},{9,8},{10,11... | collective-permute-start | bytes 3145736 | tf_op jit(solution)/shard_map/ppermute | solution.py:213
  32.7 26.8 %collective-permute-start.3 = (f32[1024,128]{1,0:T(8,128)}, f32[1024,128]{1,0:T(8,128)}, u32[]{:S(2)}, u32[]{:S(2)}) collective-permute-start(f32[1024,128]{1,0:T(8,128)} %get-tuple-element.86), channel_id=1, source_target_pairs={{0,16},{1,17},{2,18},{3,19},{4,20},{5,21},{6,22},{7,23},{8,24},{9,... | collective-permute-start | bytes 1572872 | tf_op jit(solution)/shard_map/ppermute | solution.py:213
  33.1 26.4 %collective-permute-start.6 = (f32[1024,128]{1,0:T(8,128)}, f32[1024,128]{1,0:T(8,128)}, u32[]{:S(2)}, u32[]{:S(2)}) collective-permute-start(f32[1024,128]{1,0:T(8,128)} %get-tuple-element.89), channel_id=1, source_target_pairs={{0,1},{1,0},{2,3},{3,2},{4,5},{5,4},{6,7},{7,6},{8,9},{9,8},{10,11... | collective-permute-start | bytes 1572872 | tf_op jit(solution)/shard_map/ppermute | solution.py:213
  61.1 30.4 %collective-permute-start.11 = (f32[2048,128]{1,0:T(8,128)S(1)}, f32[2048,128]{1,0:T(8,128)}, u32[]{:S(2)}, u32[]{:S(2)}) collective-permute-start(f32[2048,128]{1,0:T(8,128)S(1)} %collective-permute-done.5.refs_4_.refs_11_.refs_2_.refs_6_), channel_id=1, source_target_pairs={{0,4},{1,5},{2,6},{3,7},{4,0},{5,1},{6,2},{7,3},{8,12},{9,13},{10,... | collective-permute-start | bytes 3145736 | tf_op jit(solution)/shard_map/ppermute | solution.py:213
  62.6 29.0 %collective-permute-start.9 = (f32[4,264,128]{2,1,0:T(8,128)}, f32[4,264,128]{2,1,0:T(8,128)}, u32[]{:S(2)}, u32[]{:S(2)}) collective-permute-start(f32[4,264,128]{2,1,0:T(8,128)} %collective-permute-done.8), channel_id=1, source_target_pairs={{16,24},{17,25},{18,26},{19,27},{20,28},{21,29},{22,30},{23,31}} | collective-permute-start | bytes 1622024 | tf_op jit(solution)/shard_map/ppermute | solution.py:213
  64.0 27.5 %collective-permute-start.12 = (f32[512,128]{1,0:T(8,128)S(1)}, f32[512,128]{1,0:T(8,128)}, u32[]{:S(2)}, u32[]{:S(2)}) collective-permute-start(f32[512,128]{1,0:T(8,128)S(1)} %collective-permute-done.1.refs_9_), channel_id=1, source_target_pairs={{0,4},{1,5},{2,6},{3,7},{4,0},{5,1},{6,2},{7,3},{8,12},{9,13},{10,... | collective-permute-start | bytes 786440 | tf_op jit(solution)/shard_map/ppermute | solution.py:213
  64.5 27.0 %collective-permute-start.10 = (f32[512,128]{1,0:T(8,128)}, f32[512,128]{1,0:T(8,128)}, u32[]{:S(2)}, u32[]{:S(2)}) collective-permute-start(f32[512,128]{1,0:T(8,128)} %get-tuple-element.96), channel_id=1, source_target_pairs={{0,16},{1,17},{2,18},{3,19},{4,20},{5,21},{6,22},{7,23},{8,24},{9,... | collective-permute-start | bytes 786440 | tf_op jit(solution)/shard_map/ppermute | solution.py:213
  93.2 28.3 %collective-permute-start.13 = (f32[4,264,128]{2,1,0:T(8,128)S(1)}, f32[4,264,128]{2,1,0:T(8,128)S(1)}, u32[]{:S(2)}, u32[]{:S(2)}) collective-permute-start(f32[4,264,128]{2,1,0:T(8,128)S(1)} %get-tuple-element.134), channel_id=1, source_target_pairs={{0,4},{1,5},{2,6},{3,7},{4,0},{5,1},{6,2},{7,3},{8,12},{9,13},{10,... | collective-permute-start | bytes 1622024 | tf_op jit(solution)/shard_map/ppermute | solution.py:213
  94.8 24.9 %collective-permute-start.14 = (f32[1024,128]{1,0:T(8,128)}, f32[1024,128]{1,0:T(8,128)}, u32[]{:S(2)}, u32[]{:S(2)}) collective-permute-start(f32[1024,128]{1,0:T(8,128)} %collective-permute-done.6), channel_id=1, source_target_pairs={{0,16},{1,17},{2,18},{3,19},{4,20},{5,21},{6,22},{7,23},{8,24},{9,... | collective-permute-start | bytes 1572872 | tf_op jit(solution)/shard_map/ppermute | solution.py:213
  96.7 24.0 %collective-permute-start.16 = (f32[256,512]{1,0:T(8,128)S(1)}, f32[256,512]{1,0:T(8,128)S(1)}, u32[]{:S(2)}, u32[]{:S(2)}) collective-permute-start(f32[256,512]{1,0:T(8,128)S(1)} %mix.2.refs_0_), channel_id=1, source_target_pairs={{0,8},{1,9},{2,10},{3,11},{4,12},{5,13},{6,14},{7,15},{8,0},{9,1},... | collective-permute-start | bytes 1572872 | tf_op jit(solution)/shard_map/ppermute | solution.py:213
  99.2 21.4 %collective-permute-start.17 = (f32[256,512]{1,0:T(8,128)S(1)}, f32[256,512]{1,0:T(8,128)S(1)}, u32[]{:S(2)}, u32[]{:S(2)}) collective-permute-start(f32[256,512]{1,0:T(8,128)S(1)} %mix.2.refs_0_), channel_id=1, source_target_pairs={{0,2},{1,3},{2,0},{3,1},{4,6},{5,7},{6,4},{7,5},{8,10},{9,11},{10,... | collective-permute-start | bytes 1572872 | tf_op jit(solution)/shard_map/ppermute | solution.py:213
  124.0 28.4 %collective-permute-start.19 = (f32[512,512]{1,0:T(8,128)}, f32[512,512]{1,0:T(8,128)S(1)}, u32[]{:S(2)}, u32[]{:S(2)}) collective-permute-start(f32[512,512]{1,0:T(8,128)} %get-tuple-element.111), channel_id=1, source_target_pairs={{0,2},{1,3},{2,0},{3,1},{4,6},{5,7},{6,4},{7,5},{8,10},{9,11},{10,... | collective-permute-start | bytes 3145736 | tf_op jit(solution)/shard_map/ppermute | solution.py:213
  125.5 22.5 %collective-permute-start.18 = (f32[256,512]{1,0:T(8,128)}, f32[256,512]{1,0:T(8,128)}, u32[]{:S(2)}, u32[]{:S(2)}) collective-permute-start(f32[256,512]{1,0:T(8,128)} %get-tuple-element.110.refs_0_), channel_id=1, source_target_pairs={{0,8},{1,9},{2,10},{3,11},{4,12},{5,13},{6,14},{7,15},{8,0},{9,1},... | collective-permute-start | bytes 1572872 | tf_op jit(solution)/shard_map/ppermute | solution.py:213
  125.5 25.5 %collective-permute-start.20 = (f32[1024,128]{1,0:T(8,128)}, f32[1024,128]{1,0:T(8,128)}, u32[]{:S(2)}, u32[]{:S(2)}) collective-permute-start(f32[1024,128]{1,0:T(8,128)} %collective-permute-done.7), channel_id=1, source_target_pairs={{0,16},{1,17},{2,18},{3,19},{4,20},{5,21},{6,22},{7,23},{8,24},{9,... | collective-permute-start | bytes 1572872 | tf_op jit(solution)/shard_map/ppermute | solution.py:213
  128.9 22.1 %collective-permute-start.21 = (f32[1024,128]{1,0:T(8,128)}, f32[1024,128]{1,0:T(8,128)}, u32[]{:S(2)}, u32[]{:S(2)}) collective-permute-start(f32[1024,128]{1,0:T(8,128)} %collective-permute-done.3.refs_16_.refs_8_), channel_id=1, source_target_pairs={{0,4},{1,5},{2,6},{3,7},{4,0},{5,1},{6,2},{7,3},{8,12},{9,13},{10,... | collective-permute-start | bytes 1572872 | tf_op jit(solution)/shard_map/ppermute | solution.py:213
  129.7 22.7 %collective-permute-start.22 = (f32[1024,128]{1,0:T(8,128)}, f32[1024,128]{1,0:T(8,128)}, u32[]{:S(2)}, u32[]{:S(2)}) collective-permute-start(f32[1024,128]{1,0:T(8,128)} %collective-permute-done.14.refs_6_.refs_13_), channel_id=1, source_target_pairs={{0,4},{1,5},{2,6},{3,7},{4,0},{5,1},{6,2},{7,3},{8,12},{9,13},{10,... | collective-permute-start | bytes 1572872 | tf_op jit(solution)/shard_map/ppermute | solution.py:213
  152.4 15.1 %collective-permute-start.23 = (f32[256,512]{1,0:T(8,128)}, f32[256,512]{1,0:T(8,128)S(1)}, u32[]{:S(2)}, u32[]{:S(2)}) collective-permute-start(f32[256,512]{1,0:T(8,128)} %collective-permute-done.18.refs_1_), channel_id=1, source_target_pairs={{0,2},{1,3},{2,0},{3,1},{4,6},{5,7},{6,4},{7,5},{8,10},{9,11},{10,... | collective-permute-start | bytes 1572872 | tf_op jit(solution)/shard_map/ppermute | solution.py:213
  152.9 14.6 %collective-permute-start.24 = (f32[1024,128]{1,0:T(8,128)}, f32[1024,128]{1,0:T(8,128)S(1)}, u32[]{:S(2)}, u32[]{:S(2)}) collective-permute-start(f32[1024,128]{1,0:T(8,128)} %collective-permute-done.20.refs_4_.refs_8_), channel_id=1, source_target_pairs={{0,4},{1,5},{2,6},{3,7},{4,0},{5,1},{6,2},{7,3},{8,12},{9,13},{10,... | collective-permute-start | bytes 1572872 | tf_op jit(solution)/shard_map/ppermute | solution.py:213
  174.7 14.3 %collective-permute-start.27 = (f32[256,256]{1,0:T(8,128)S(1)}, f32[256,256]{1,0:T(8,128)S(1)}, u32[]{:S(2)}, u32[]{:S(2)}) collective-permute-start(f32[256,256]{1,0:T(8,128)S(1)} %get-tuple-element.130), channel_id=1, source_target_pairs={{0,2},{1,0},{2,10},{3,8},{4,6},{5,4},{6,14},{7,12},{8,3},{9,1},{10... | collective-permute-start | bytes 786440 | tf_op jit(solution)/shard_map/ppermute | solution.py:481
  179.0 13.6 %collective-permute-start.29 = (f32[256,256]{1,0:T(8,128)S(1)}, f32[256,256]{1,0:T(8,128)S(1)}, u32[]{:S(2)}, u32[]{:S(2)}) collective-permute-start(f32[256,256]{1,0:T(8,128)S(1)} %get-tuple-element.132), channel_id=1, source_target_pairs={{0,10},{1,8},{2,2},{3,0},{4,14},{5,12},{6,6},{7,4},{8,11},{9,9},{1... | collective-permute-start | bytes 786440 | tf_op jit(solution)/shard_map/ppermute | solution.py:481
  (38 other events, 281.8 us)

commit v3 on v1

--- a/solution.py
+++ b/solution.py
@@ -339,23 +339,25 @@
     out_weight, other_state = together((out_weight, other_state))
     starts = jnp.stack([(h ^ flip ^ d) * depth + which * wide for flip in (0, 1) for which, d in order])
     count = len(order)
-    spans = [(0, part), (part, 3 * part), (3 * part, count), (0, count)]
-    plan = [list(range(*span)) for span in spans]
-    plan += [list(range(count + start, count + stop)) for start, stop in ((0, 2 * part), (2 * part, count), (0, count))]
-    *kept_parts, kept, given_1, given_2, given = arranged(out_weight, starts, plan)
-    kept_parts, kept = [widen(x) for x in kept_parts], widen(kept)
-    far_1 = swap(kept_parts[0], far)
+    (first_part,) = arranged(out_weight, starts, [list(range(part))])
+    first_part = widen(first_part)
+    far_1 = swap(first_part, far)
     from_neighbour = swap(other_state, 1)
     own_state, own_query, other_query = rest_part(jnp.concatenate([own, other]), other_feat)
+    out_weight, own_state = together((out_weight, own_state))
+    spans = [(part, 3 * part), (3 * part, count), (0, count)]
+    spans += [(count, count + 2 * part), (count + 2 * part, 2 * count), (count, 2 * count)]
+    kept_2, kept_3, kept, given_1, given_2, given = arranged(out_weight, starts, [list(range(*span)) for span in spans])
+    kept_2, kept_3, kept = [widen(x) for x in (kept_2, kept_3, kept)]
     groups, perms, send, place = route_tables(ctx, heads, rels)
     steps, size = len(perms), len(groups[0])
     send_here = jnp.asarray(send)[me]
     place_here = jnp.asarray(place)[me]
 
-    from_neighbour, own_state, far_1, kept_parts, kept, given_1, given_2, given = together(
-        (from_neighbour, own_state, far_1, kept_parts, kept, given_1, given_2, given)
-    )
-    far_2 = swap(kept_parts[1], far)
+    from_neighbour, own_state, far_1, kept_2, kept, given_1, given_2, given = together(
+        (from_neighbour, own_state, far_1, kept_2, kept, given_1, given_2, given)
+    )
+    far_2 = swap(kept_2, far)
     kept_near = swap(kept, near)
     taken, taken_1, taken_2 = [widen(swap(x, 0, 1)) for x in (given, given_1, given_2)]
     earlier = jnp.where(odd == 0, own_state, from_neighbour)
@@ -367,18 +369,18 @@
         before = before + jnp.where((c & bit) != 0, got, 0.0)
         total = total + got
         bit *= 2
-    total, before, far_2, kept_near, taken, taken_1, taken_2, send_here, place_here, far_1 = together(
-        (total, before, far_2, kept_near, taken, taken_1, taken_2, send_here, place_here, far_1)
+    total, before, far_2, kept_near, taken, taken_1, taken_2, far_1 = together(
+        (total, before, far_2, kept_near, taken, taken_1, taken_2, far_1)
     )
     taken_near = swap(taken, near)
     both_1 = swap(far_1, near)
     second = (c & PAIR) != 0
     got = swap(jnp.where(second, total[half // 2 :], total[: half // 2]), bit, keep=lambda i: not i & bit)
-    got, kept_parts[2] = together((got, kept_parts[2]))
+    got, kept_3 = together((got, kept_3))
     met = swap(got, PAIR, keep=lambda i: i & bit)
-    far_3 = swap(kept_parts[2], far)
+    far_3 = swap(kept_3, far)
     got = jnp.concatenate([jnp.where(second, met, got), jnp.where(second, got, met)])
-    got, far_3, taken_near, both_1, taken_1 = together((got, far_3, taken_near, both_1, taken_1))
+    got, taken_near, both_1, taken_1, far_2 = together((got, taken_near, both_1, taken_1, far_2))
     before = before + got
 
     other_prior = swap(before + jnp.where(odd == 0, earlier, 0.0), 1)
@@ -391,19 +393,22 @@
                 pieces[d, j | bit] = (swap(x[i * rows : (i + 1) * rows], 0, bit), 0)
         return [(pieces[0, j], pieces[PAIR, j]) for j in even]
 
+    own_mixed, far_3 = together((own_mixed, far_3))
     met, across = swap(own_mixed, PAIR), swap(own_mixed, 0, head_bits[0])
     far_4 = swap(taken_1, far)
-    both_3 = swap(far_3, near)
-    other_prior, far_2, far_4, both_3, met, across, taken_2 = together(
-        (other_prior, far_2, far_4, both_3, met, across, taken_2)
+    both_2 = swap(far_2, near)
+    other_prior, far_3, far_4, both_2, met, across, taken_2 = together(
+        (other_prior, far_3, far_4, both_2, met, across, taken_2)
     )
     other_mixed, both = mix(*other_query, other_prior, met)
     other_met = swap(other_mixed, PAIR)
     both = swap(both, 0, head_bits[0])
     far_5 = swap(taken_2, far)
-    both_2 = swap(far_2, near)
+    both_3 = swap(far_3, near)
     both_4 = swap(far_4, near)
-    other_met, both, far_5, both_2, both_4 = together((other_met, both, far_5, both_2, both_4))
+    other_met, both, far_5, both_3, both_4, send_here, place_here = together(
+        (other_met, both, far_5, both_3, both_4, send_here, place_here)
+    )
     both_5 = swap(far_5, near)
     last = swap(other_met, 0, head_bits[0])
     own_pieces = spread(

time: 190 us -> 192 us (1.011)
  waiting for transfers between devices: 91.5 us -> 84 us
  Pallas kernels: 32.3 us -> 36.3 us
  local copies, waits for them, and re-layouts: 13 us -> 16.9 us
    ppermute x26, waiting for transfers between devices: 80.8 us -> 73.9 us  [swap(): return lax.ppermute(x, AXES, pairs)]
    unnamed x52 -> x84, local copies, waits for them, and re-layouts: 11.6 us -> 15.4 us
    pallas_call x4, Pallas kernels: 11.3 us -> 13.5 us  [project(): pl.pallas_call(functools.partial(project_kernel, terms, len(used)), grid=...]
  transfers between devices with their start and end apart: 30 -> 30, of which waited for: 17 -> 11; matrix products, arithmetic and copies ran while one was open for 3% -> 3% of each run, Pallas kernels for 11% -> 13%
where the time goes in v3:
time: 192 us; the launch traced here: 191 us
  waiting for transfers between devices  84 us (44%)
  starting transfers between devices  49.1 us (26%)
  Pallas kernels  36.3 us (19%)
  local copies, waits for them, and re-layouts  16.9 us (9%)
  other arithmetic  4.6 us (2%)
    ppermute x26, waiting for transfers between devices, swap(): return lax.ppermute(x, AXES, pairs)  73.9 us
    ppermute x26, starting transfers between devices, swap(): return lax.ppermute(x, AXES, pairs)  41 us
    unnamed x84, local copies, waits for them, and re-layouts  15.4 us
    pallas_call x4, Pallas kernels, project(): pl.pallas_call(functools.partial(project_kernel, terms, len(used)), grid=...  13.5 us
    ppermute x4, waiting for transfers between devices, body(): lax.ppermute(part, AXES, perm)  10.2 us
    pallas_call x1, Pallas kernels, rest_part(): pl.pallas_call(rest_kernel, grid_spec=pltpu.PrefetchScalarGridSpec(num_sc...  9.61 us
    ppermute x4, starting transfers between devices, body(): lax.ppermute(part, AXES, perm)  8.1 us
    pallas_call x1, Pallas kernels, key_part(): pl.pallas_call(key_kernel, grid_spec=pltpu.PrefetchScalarGridSpec(num_sca...  4.05 us
  transfers between devices with their start and end apart: 30, of which 11 were waited for; matrix products, arithmetic and copies ran while one was open for 3% of the time, Pallas kernels for 13%

profile of v3, /device:TPU:0, one launch (start us, length us, event | category | flops | bytes accessed | tf_op | source)
XLA Modules:
  0.0 191.4 jit_solution(4711171558155998999)
XLA Ops:
  0.0 4.1 %key_part.1 = (f32[4,264,128]{2,1,0:T(8,128)}, f32[4,256,256]{2,1,0:T(8,128)}) custom-call(s32[1]{0:T(128)} %bitcast.1.first, f32[256,1024]{1,0:T(8,128)} %refs_0_.1, f32[8,128,128]{2,1,0:T(8,128)} %refs_1_.1, f32[256,1024]{1,0:T(8,128)} %refs_7_.1), custom_call_target="tpu_custom_call" | custom-call | flops 603979776 | bytes 3145728 | tf_op jit(solution)/shard_map/key_part/pallas_call | solution.py:231
  4.1 2.9 %collective-permute-start = (f32[4,264,128]{2,1,0:T(8,128)}, f32[4,264,128]{2,1,0:T(8,128)}, u32[]{:S(2)}, u32[]{:S(2)}) collective-permute-start(f32[4,264,128]{2,1,0:T(8,128)} %get-tuple-element.76), channel_id=1, source_target_pairs={{0,4},{1,5},{2,6},{3,7},{4,0},{5,1},{6,2},{7,3},{8,12},{9,13},{10,... | collective-permute-start | bytes 1622024 | tf_op jit(solution)/shard_map/ppermute | solution.py:213
  7.7 2.7 %collective-permute-start.1 = (f32[512,128]{1,0:T(8,128)S(1)}, f32[512,128]{1,0:T(8,128)S(1)}, u32[]{:S(2)}, u32[]{:S(2)}) collective-permute-start(f32[512,128]{1,0:T(8,128)S(1)} %arrange.2), channel_id=1, source_target_pairs={{0,16},{1,17},{2,18},{3,19},{4,20},{5,21},{6,22},{7,23},{8,24},{9,... | collective-permute-start | bytes 786440 | tf_op jit(solution)/shard_map/ppermute | solution.py:213
  13.9 9.6 %rest_part.1 = (f32[4,264,128]{2,1,0:T(8,128)S(1)}, f32[4,256,256]{2,1,0:T(8,128)S(1)}, f32[4,256,128]{2,1,0:T(8,128)S(1)}, f32[4,256,128]{2,1,0:T(8,128)S(1)}, ...) custom-call(s32[2]{0:T(128)S(1)} %pad_add_fusion.first, ...), custom_call_target="tpu_custom_call" | custom-call | flops 3422552064 | bytes 8388608 | tf_op jit(solution)/shard_map/rest_part/pallas_call | solution.py:258
  25.2 2.6 %arrange.3 = (f32[1024,128]{1,0:T(8,128)}, f32[512,128]{1,0:T(8,128)S(1)}, f32[2048,128]{1,0:T(8,128)S(1)}, f32[1024,128]{1,0:T(8,128)}, f32[1024,128]{1,0:T(8,128)}, /*index=5*/f32[2048,128]{1,0:T(8,128)}) custom-call(s32[8]{0:T(128)S(1)} %stack.35.starts, f32[4096,128]{1,0:T(8,128)S(1)} %copy-done.4), custom_call_target="tpu_custom_call" | custom-call | bytes 7864320 | tf_op jit(solution)/shard_map/arrange/pallas_call | solution.py:315
  32.7 18.0 %collective-permute-done.2 = f32[4,264,128]{2,1,0:T(8,128)S(1)} collective-permute-done((f32[4,264,128]{2,1,0:T(8,128)S(1)}, f32[4,264,128]{2,1,0:T(8,128)S(1)}, u32[]{:S(2)}, u32[]{:S(2)}) %collective-permute-start.2) | collective-permute-done | bytes 540704 | tf_op jit(solution)/shard_map/ppermute | solution.py:213
  53.6 5.1 %collective-permute-done.3.refs_16_.refs_8_ = f32[1024,128]{1,0:T(8,128)} collective-permute-done((f32[1024,128]{1,0:T(8,128)}, f32[1024,128]{1,0:T(8,128)}, u32[]{:S(2)}, u32[]{:S(2)}) %collective-permute-start.3) | collective-permute-done | bytes 524320 | tf_op jit(solution)/shard_map/ppermute | solution.py:213
  62.5 4.7 %collective-permute-done.8 = f32[2,264,128]{2,1,0:T(8,128)} collective-permute-done((f32[2,264,128]{2,1,0:T(8,128)S(1)}, f32[2,264,128]{2,1,0:T(8,128)}, u32[]{:S(2)}, u32[]{:S(2)}) %collective-permute-start.8) | collective-permute-done | bytes 270368 | tf_op jit(solution)/shard_map/ppermute | solution.py:213
  69.1 11.4 %collective-permute-start.13 = (f32[512,128]{1,0:T(8,128)}, f32[512,128]{1,0:T(8,128)}, u32[]{:S(2)}, u32[]{:S(2)}) collective-permute-start(f32[512,128]{1,0:T(8,128)} %copy-done.38), channel_id=1, source_target_pairs={{0,16},{1,17},{2,18},{3,19},{4,20},{5,21},{6,22},{7,23},{8,24},{9,... | collective-permute-start | bytes 786440 | tf_op jit(solution)/shard_map/ppermute | solution.py:213
  81.7 7.4 %collective-permute-done.11.refs_9_ = f32[512,128]{1,0:T(8,128)S(1)} collective-permute-done((f32[512,128]{1,0:T(8,128)S(1)}, f32[512,128]{1,0:T(8,128)S(1)}, u32[]{:S(2)}, u32[]{:S(2)}) %collective-permute-start.11) | collective-permute-done | bytes 262176 | tf_op jit(solution)/shard_map/ppermute | solution.py:213
  90.0 2.6 %collective-permute-start.12 = (f32[4,264,128]{2,1,0:T(8,128)S(1)}, f32[4,264,128]{2,1,0:T(8,128)S(1)}, u32[]{:S(2)}, u32[]{:S(2)}) collective-permute-start(f32[4,264,128]{2,1,0:T(8,128)S(1)} %get-tuple-element.138), channel_id=1, source_target_pairs={{0,4},{1,5},{2,6},{3,7},{4,0},{5,1},{6,2},{7,3},{8,12},{9,13},{10,... | collective-permute-start | bytes 1622024 | tf_op jit(solution)/shard_map/ppermute | solution.py:213
  94.0 2.7 %collective-permute-start.16 = (f32[256,512]{1,0:T(8,128)S(1)}, f32[256,512]{1,0:T(8,128)S(1)}, u32[]{:S(2)}, u32[]{:S(2)}) collective-permute-start(f32[256,512]{1,0:T(8,128)S(1)} %mix.2.refs_0_), channel_id=1, source_target_pairs={{0,8},{1,9},{2,10},{3,11},{4,12},{5,13},{6,14},{7,15},{8,0},{9,1},... | collective-permute-start | bytes 1572872 | tf_op jit(solution)/shard_map/ppermute | solution.py:213
  99.1 18.4 %collective-permute-done.14.refs_6_.refs_13_ = f32[1024,128]{1,0:T(8,128)} collective-permute-done((f32[1024,128]{1,0:T(8,128)}, f32[1024,128]{1,0:T(8,128)}, u32[]{:S(2)}, u32[]{:S(2)}) %collective-permute-start.14) | collective-permute-done | bytes 524320 | tf_op jit(solution)/shard_map/ppermute | solution.py:213
  119.3 2.4 %mix.3 = (f32[256,512]{1,0:T(8,128)}, f32[512,512]{1,0:T(8,128)}) custom-call(f32[4,256,256]{2,1,0:T(8,128)S(1)} %copy-done.18, f32[4,256,128]{2,1,0:T(8,128)S(1)} %copy-done.26, f32[4,256,128]{2,1,0:T(8,128)S(1)} %copy-done.28, f32[4,264,128]{2,1,0:T(8,128)S(1)} %collective-permute-done.12.prior_ref, f32[256,512]{1,0:T(8,128)S(1)} %collective-permute-done.16.refs_0_.refs_1_), custom_call_target="tpu_custom_call" | custom-call | flops 201326592 | bytes 3670016 | tf_op jit(solution)/shard_map/mix/pallas_call | solution.py:284
  123.2 2.9 %collective-permute-start.20 = (f32[1024,128]{1,0:T(8,128)}, f32[1024,128]{1,0:T(8,128)}, u32[]{:S(2)}, u32[]{:S(2)}) collective-permute-start(f32[1024,128]{1,0:T(8,128)} %collective-permute-done.7), channel_id=1, source_target_pairs={{0,16},{1,17},{2,18},{3,19},{4,20},{5,21},{6,22},{7,23},{8,24},{9,... | collective-permute-start | bytes 1572872 | tf_op jit(solution)/shard_map/ppermute | solution.py:213
  129.5 15.4 %collective-permute-done.21.refs_17_ = f32[512,128]{1,0:T(8,128)} collective-permute-done((f32[512,128]{1,0:T(8,128)}, f32[512,128]{1,0:T(8,128)}, u32[]{:S(2)}, u32[]{:S(2)}) %collective-permute-start.21) | collective-permute-done | bytes 262176 | tf_op jit(solution)/shard_map/ppermute | solution.py:213
  144.9 3.0 %collective-permute-done.18.refs_1_ = f32[256,512]{1,0:T(8,128)} collective-permute-done((f32[256,512]{1,0:T(8,128)}, f32[256,512]{1,0:T(8,128)}, u32[]{:S(2)}, u32[]{:S(2)}) %collective-permute-start.18) | collective-permute-done | bytes 524320 | tf_op jit(solution)/shard_map/ppermute | solution.py:213
  156.4 4.9 %project.4.refs_10_ = f32[512,1024]{1,0:T(8,128)S(1)} custom-call(f32[256,512]{1,0:T(8,128)S(1)} %copy-done.6, f32[256,512]{1,0:T(8,128)S(1)} %copy-done.9, f32[256,512]{1,0:T(8,128)S(1)} %copy-done.13, f32[512,512]{1,0:T(8,128)S(1)} %collective-permute-done.19.refs_3_.refs_0_.refs_4_, f32[2048,128]{1,0:T(8,128)S(1)} %copy-done.1, ...), custom_call_target="tpu_custom_call" | custom-call | flops 2818572288 | bytes 5767168 | tf_op jit(solution)/shard_map/project/pallas_call | solution.py:435
  161.3 3.5 %project.5.refs_6_.refs_12_ = f32[512,1024]{1,0:T(8,128)S(1)} custom-call(f32[256,512]{1,0:T(8,128)} %get-tuple-element.114.refs_0_, f32[256,512]{1,0:T(8,128)} %collective-permute-done.18.refs_1_, f32[2048,128]{1,0:T(8,128)S(1)} %copy-done.1, f32[2048,128]{1,0:T(8,128)} %collective-permute-done.10.refs_5_.refs_12_.refs_3_.refs_7_, ...), custom_call_target="tpu_custom_call" | custom-call | flops 1610612736 | bytes 4194304 | tf_op jit(solution)/shard_map/project/pallas_call | solution.py:435
  164.8 3.1 %project.7 = f32[512,512]{1,0:T(8,128)S(1)} custom-call(f32[256,512]{1,0:T(8,128)S(1)} %copy-done.7, f32[256,512]{1,0:T(8,128)S(1)} %copy-done.9, f32[256,512]{1,0:T(8,128)S(1)} %copy-done.13, f32[512,512]{1,0:T(8,128)S(1)} %collective-permute-done.19.refs_3_.refs_0_.refs_4_, f32[512,512]{1,0:T(8,128)S(1)} %collective-permute-done.19.refs_3_.refs_0_.refs_4_, ...), custom_call_target="tpu_custom_call" | custom-call | flops 1207959552 | bytes 2621440 | tf_op jit(solution)/shard_map/project/pallas_call | solution.py:435
  172.0 2.8 %collective-permute-start.27 = (f32[256,256]{1,0:T(8,128)S(1)}, f32[256,256]{1,0:T(8,128)S(1)}, u32[]{:S(2)}, u32[]{:S(2)}) collective-permute-start(f32[256,256]{1,0:T(8,128)S(1)} %get-tuple-element.134), channel_id=1, source_target_pairs={{0,2},{1,0},{2,10},{3,8},{4,6},{5,4},{6,14},{7,12},{8,3},{9,1},{10... | collective-permute-start | bytes 786440 | tf_op jit(solution)/shard_map/ppermute | solution.py:486
  176.0 3.4 %collective-permute-start.29 = (f32[256,256]{1,0:T(8,128)S(1)}, f32[256,256]{1,0:T(8,128)S(1)}, u32[]{:S(2)}, u32[]{:S(2)}) collective-permute-start(f32[256,256]{1,0:T(8,128)S(1)} %get-tuple-element.136), channel_id=1, source_target_pairs={{0,10},{1,8},{2,2},{3,0},{4,14},{5,12},{6,6},{7,4},{8,11},{9,9},{1... | collective-permute-start | bytes 786440 | tf_op jit(solution)/shard_map/ppermute | solution.py:486
  179.4 6.9 %collective-permute-done.27.refs_1_ = f32[256,256]{1,0:T(8,128)S(1)} collective-permute-done((f32[256,256]{1,0:T(8,128)S(1)}, f32[256,256]{1,0:T(8,128)S(1)}, u32[]{:S(2)}, u32[]{:S(2)}) %collective-permute-start.27) | collective-permute-done | bytes 262176 | tf_op jit(solution)/shard_map/ppermute | solution.py:486
  186.4 3.2 %collective-permute-done.29.refs_3_ = f32[256,256]{1,0:T(8,128)S(1)} collective-permute-done((f32[256,256]{1,0:T(8,128)S(1)}, f32[256,256]{1,0:T(8,128)S(1)}, u32[]{:S(2)}, u32[]{:S(2)}) %collective-permute-start.29) | collective-permute-done | bytes 262176 | tf_op jit(solution)/shard_map/ppermute | solution.py:486
  (142 shorter events, 47.4 us)
Async XLA Ops:
  4.1 24.5 %collective-permute-start = (f32[4,264,128]{2,1,0:T(8,128)}, f32[4,264,128]{2,1,0:T(8,128)}, u32[]{:S(2)}, u32[]{:S(2)}) collective-permute-start(f32[4,264,128]{2,1,0:T(8,128)} %get-tuple-element.76), channel_id=1, source_target_pairs={{0,4},{1,5},{2,6},{3,7},{4,0},{5,1},{6,2},{7,3},{8,12},{9,13},{10,... | collective-permute-start | bytes 1622024 | tf_op jit(solution)/shard_map/ppermute | solution.py:213
  7.7 20.8 %collective-permute-start.1 = (f32[512,128]{1,0:T(8,128)S(1)}, f32[512,128]{1,0:T(8,128)S(1)}, u32[]{:S(2)}, u32[]{:S(2)}) collective-permute-start(f32[512,128]{1,0:T(8,128)S(1)} %arrange.2), channel_id=1, source_target_pairs={{0,16},{1,17},{2,18},{3,19},{4,20},{5,21},{6,22},{7,23},{8,24},{9,... | collective-permute-start | bytes 786440 | tf_op jit(solution)/shard_map/ppermute | solution.py:213
  29.6 21.0 %collective-permute-start.2 = (f32[4,264,128]{2,1,0:T(8,128)S(1)}, f32[4,264,128]{2,1,0:T(8,128)S(1)}, u32[]{:S(2)}, u32[]{:S(2)}) collective-permute-start(f32[4,264,128]{2,1,0:T(8,128)S(1)} %add.54), channel_id=1, source_target_pairs={{0,8},{1,9},{2,10},{3,11},{4,12},{5,13},{6,14},{7,15},{8,0},{9,1},... | collective-permute-start | bytes 1622024 | tf_op jit(solution)/shard_map/ppermute | solution.py:213
  31.3 27.4 %collective-permute-start.4 = (f32[2048,128]{1,0:T(8,128)S(1)}, f32[2048,128]{1,0:T(8,128)S(1)}, u32[]{:S(2)}, u32[]{:S(2)}) collective-permute-start(f32[2048,128]{1,0:T(8,128)S(1)} %get-tuple-element.89.refs_7_.refs_14_.refs_6_.refs_2_), channel_id=1, source_target_pairs={{0,4},{1,5},{2,6},{3,7},{4,0},{5,1},{6,2},{7,3},{8,12},{9,13},{10,... | collective-permute-start | bytes 3145736 | tf_op jit(solution)/shard_map/ppermute | solution.py:213
  31.8 26.9 %collective-permute-start.5 = (f32[2048,128]{1,0:T(8,128)}, f32[2048,128]{1,0:T(8,128)S(1)}, u32[]{:S(2)}, u32[]{:S(2)}) collective-permute-start(f32[2048,128]{1,0:T(8,128)} %get-tuple-element.90), channel_id=1, source_target_pairs={{0,1},{1,0},{2,3},{3,2},{4,5},{5,4},{6,7},{7,6},{8,9},{9,8},{10,11... | collective-permute-start | bytes 3145736 | tf_op jit(solution)/shard_map/ppermute | solution.py:213
  31.8 26.8 %collective-permute-start.3 = (f32[1024,128]{1,0:T(8,128)}, f32[1024,128]{1,0:T(8,128)}, u32[]{:S(2)}, u32[]{:S(2)}) collective-permute-start(f32[1024,128]{1,0:T(8,128)} %get-tuple-element.88), channel_id=1, source_target_pairs={{0,16},{1,17},{2,18},{3,19},{4,20},{5,21},{6,22},{7,23},{8,24},{9,... | collective-permute-start | bytes 1572872 | tf_op jit(solution)/shard_map/ppermute | solution.py:213
  32.5 26.2 %collective-permute-start.6 = (f32[1024,128]{1,0:T(8,128)}, f32[1024,128]{1,0:T(8,128)}, u32[]{:S(2)}, u32[]{:S(2)}) collective-permute-start(f32[1024,128]{1,0:T(8,128)} %get-tuple-element.91), channel_id=1, source_target_pairs={{0,1},{1,0},{2,3},{3,2},{4,5},{5,4},{6,7},{7,6},{8,9},{9,8},{10,11... | collective-permute-start | bytes 1572872 | tf_op jit(solution)/shard_map/ppermute | solution.py:213
  58.7 31.1 %collective-permute-start.10 = (f32[2048,128]{1,0:T(8,128)S(1)}, f32[2048,128]{1,0:T(8,128)}, u32[]{:S(2)}, u32[]{:S(2)}) collective-permute-start(f32[2048,128]{1,0:T(8,128)S(1)} %collective-permute-done.5.refs_4_.refs_11_.refs_2_.refs_6_), channel_id=1, source_target_pairs={{0,4},{1,5},{2,6},{3,7},{4,0},{5,1},{6,2},{7,3},{8,12},{9,13},{10,... | collective-permute-start | bytes 3145736 | tf_op jit(solution)/shard_map/ppermute | solution.py:213
  68.5 20.6 %collective-permute-start.11 = (f32[512,128]{1,0:T(8,128)S(1)}, f32[512,128]{1,0:T(8,128)S(1)}, u32[]{:S(2)}, u32[]{:S(2)}) collective-permute-start(f32[512,128]{1,0:T(8,128)S(1)} %collective-permute-done.1.refs_9_), channel_id=1, source_target_pairs={{0,4},{1,5},{2,6},{3,7},{4,0},{5,1},{6,2},{7,3},{8,12},{9,13},{10,... | collective-permute-start | bytes 786440 | tf_op jit(solution)/shard_map/ppermute | solution.py:213
  69.1 24.8 %collective-permute-start.13 = (f32[512,128]{1,0:T(8,128)}, f32[512,128]{1,0:T(8,128)}, u32[]{:S(2)}, u32[]{:S(2)}) collective-permute-start(f32[512,128]{1,0:T(8,128)} %copy-done.38), channel_id=1, source_target_pairs={{0,16},{1,17},{2,18},{3,19},{4,20},{5,21},{6,22},{7,23},{8,24},{9,... | collective-permute-start | bytes 786440 | tf_op jit(solution)/shard_map/ppermute | solution.py:213
  90.0 29.2 %collective-permute-start.12 = (f32[4,264,128]{2,1,0:T(8,128)S(1)}, f32[4,264,128]{2,1,0:T(8,128)S(1)}, u32[]{:S(2)}, u32[]{:S(2)}) collective-permute-start(f32[4,264,128]{2,1,0:T(8,128)S(1)} %get-tuple-element.138), channel_id=1, source_target_pairs={{0,4},{1,5},{2,6},{3,7},{4,0},{5,1},{6,2},{7,3},{8,12},{9,13},{10,... | collective-permute-start | bytes 1622024 | tf_op jit(solution)/shard_map/ppermute | solution.py:213
  93.9 23.6 %collective-permute-start.14 = (f32[1024,128]{1,0:T(8,128)}, f32[1024,128]{1,0:T(8,128)}, u32[]{:S(2)}, u32[]{:S(2)}) collective-permute-start(f32[1024,128]{1,0:T(8,128)} %collective-permute-done.6), channel_id=1, source_target_pairs={{0,16},{1,17},{2,18},{3,19},{4,20},{5,21},{6,22},{7,23},{8,24},{9,... | collective-permute-start | bytes 1572872 | tf_op jit(solution)/shard_map/ppermute | solution.py:213
  93.9 23.6 %collective-permute-start.15 = (f32[1024,128]{1,0:T(8,128)}, f32[1024,128]{1,0:T(8,128)S(1)}, u32[]{:S(2)}, u32[]{:S(2)}) collective-permute-start(f32[1024,128]{1,0:T(8,128)} %collective-permute-done.3.refs_16_.refs_8_), channel_id=1, source_target_pairs={{0,4},{1,5},{2,6},{3,7},{4,0},{5,1},{6,2},{7,3},{8,12},{9,13},{10,... | collective-permute-start | bytes 1572872 | tf_op jit(solution)/shard_map/ppermute | solution.py:213
  94.0 24.3 %collective-permute-start.16 = (f32[256,512]{1,0:T(8,128)S(1)}, f32[256,512]{1,0:T(8,128)S(1)}, u32[]{:S(2)}, u32[]{:S(2)}) collective-permute-start(f32[256,512]{1,0:T(8,128)S(1)} %mix.2.refs_0_), channel_id=1, source_target_pairs={{0,8},{1,9},{2,10},{3,11},{4,12},{5,13},{6,14},{7,15},{8,0},{9,1},... | collective-permute-start | bytes 1572872 | tf_op jit(solution)/shard_map/ppermute | solution.py:213
  96.8 21.6 %collective-permute-start.17 = (f32[256,512]{1,0:T(8,128)S(1)}, f32[256,512]{1,0:T(8,128)S(1)}, u32[]{:S(2)}, u32[]{:S(2)}) collective-permute-start(f32[256,512]{1,0:T(8,128)S(1)} %mix.2.refs_0_), channel_id=1, source_target_pairs={{0,2},{1,3},{2,0},{3,1},{4,6},{5,7},{6,4},{7,5},{8,10},{9,11},{10,... | collective-permute-start | bytes 1572872 | tf_op jit(solution)/shard_map/ppermute | solution.py:213
  121.7 27.5 %collective-permute-start.19 = (f32[512,512]{1,0:T(8,128)}, f32[512,512]{1,0:T(8,128)S(1)}, u32[]{:S(2)}, u32[]{:S(2)}) collective-permute-start(f32[512,512]{1,0:T(8,128)} %get-tuple-element.115), channel_id=1, source_target_pairs={{0,2},{1,3},{2,0},{3,1},{4,6},{5,7},{6,4},{7,5},{8,10},{9,11},{10,... | collective-permute-start | bytes 3145736 | tf_op jit(solution)/shard_map/ppermute | solution.py:213
  123.2 24.7 %collective-permute-start.18 = (f32[256,512]{1,0:T(8,128)}, f32[256,512]{1,0:T(8,128)}, u32[]{:S(2)}, u32[]{:S(2)}) collective-permute-start(f32[256,512]{1,0:T(8,128)} %get-tuple-element.114.refs_0_), channel_id=1, source_target_pairs={{0,8},{1,9},{2,10},{3,11},{4,12},{5,13},{6,14},{7,15},{8,0},{9,1},... | collective-permute-start | bytes 1572872 | tf_op jit(solution)/shard_map/ppermute | solution.py:213
  123.2 26.0 %collective-permute-start.20 = (f32[1024,128]{1,0:T(8,128)}, f32[1024,128]{1,0:T(8,128)}, u32[]{:S(2)}, u32[]{:S(2)}) collective-permute-start(f32[1024,128]{1,0:T(8,128)} %collective-permute-done.7), channel_id=1, source_target_pairs={{0,16},{1,17},{2,18},{3,19},{4,20},{5,21},{6,22},{7,23},{8,24},{9,... | collective-permute-start | bytes 1572872 | tf_op jit(solution)/shard_map/ppermute | solution.py:213
  126.1 23.1 %collective-permute-start.22 = (f32[1024,128]{1,0:T(8,128)}, f32[1024,128]{1,0:T(8,128)}, u32[]{:S(2)}, u32[]{:S(2)}) collective-permute-start(f32[1024,128]{1,0:T(8,128)} %collective-permute-done.14.refs_6_.refs_13_), channel_id=1, source_target_pairs={{0,4},{1,5},{2,6},{3,7},{4,0},{5,1},{6,2},{7,3},{8,12},{9,13},{10,... | collective-permute-start | bytes 1572872 | tf_op jit(solution)/shard_map/ppermute | solution.py:213
  127.0 17.9 %collective-permute-start.21 = (f32[512,128]{1,0:T(8,128)}, f32[512,128]{1,0:T(8,128)}, u32[]{:S(2)}, u32[]{:S(2)}) collective-permute-start(f32[512,128]{1,0:T(8,128)} %collective-permute-done.13.refs_4_), channel_id=1, source_target_pairs={{0,4},{1,5},{2,6},{3,7},{4,0},{5,1},{6,2},{7,3},{8,12},{9,13},{10,... | collective-permute-start | bytes 786440 | tf_op jit(solution)/shard_map/ppermute | solution.py:213
  149.1 15.6 %collective-permute-start.23 = (f32[256,512]{1,0:T(8,128)}, f32[256,512]{1,0:T(8,128)S(1)}, u32[]{:S(2)}, u32[]{:S(2)}) collective-permute-start(f32[256,512]{1,0:T(8,128)} %collective-permute-done.18.refs_1_), channel_id=1, source_target_pairs={{0,2},{1,3},{2,0},{3,1},{4,6},{5,7},{6,4},{7,5},{8,10},{9,11},{10,... | collective-permute-start | bytes 1572872 | tf_op jit(solution)/shard_map/ppermute | solution.py:213
  149.6 15.1 %collective-permute-start.24 = (f32[1024,128]{1,0:T(8,128)}, f32[1024,128]{1,0:T(8,128)S(1)}, u32[]{:S(2)}, u32[]{:S(2)}) collective-permute-start(f32[1024,128]{1,0:T(8,128)} %collective-permute-done.20.refs_4_.refs_8_), channel_id=1, source_target_pairs={{0,4},{1,5},{2,6},{3,7},{4,0},{5,1},{6,2},{7,3},{8,12},{9,13},{10,... | collective-permute-start | bytes 1572872 | tf_op jit(solution)/shard_map/ppermute | solution.py:213
  172.0 14.4 %collective-permute-start.27 = (f32[256,256]{1,0:T(8,128)S(1)}, f32[256,256]{1,0:T(8,128)S(1)}, u32[]{:S(2)}, u32[]{:S(2)}) collective-permute-start(f32[256,256]{1,0:T(8,128)S(1)} %get-tuple-element.134), channel_id=1, source_target_pairs={{0,2},{1,0},{2,10},{3,8},{4,6},{5,4},{6,14},{7,12},{8,3},{9,1},{10... | collective-permute-start | bytes 786440 | tf_op jit(solution)/shard_map/ppermute | solution.py:486
  176.0 13.6 %collective-permute-start.29 = (f32[256,256]{1,0:T(8,128)S(1)}, f32[256,256]{1,0:T(8,128)S(1)}, u32[]{:S(2)}, u32[]{:S(2)}) collective-permute-start(f32[256,256]{1,0:T(8,128)S(1)} %get-tuple-element.136), channel_id=1, source_target_pairs={{0,10},{1,8},{2,2},{3,0},{4,14},{5,12},{6,6},{7,4},{8,11},{9,9},{1... | collective-permute-start | bytes 786440 | tf_op jit(solution)/shard_map/ppermute | solution.py:486
  (48 other events, 388.5 us)

commit v4 on v3

--- a/solution.py
+++ b/solution.py
@@ -200,7 +200,6 @@
     strip_width = out_weight.shape[1]
     c = lax.axis_index("ctx")
     h = lax.axis_index("head")
-    me = c * heads + h
     odd = c & 1
 
     def swap(x, by_ctx, by_head=0, keep=lambda c: True):
@@ -265,7 +264,7 @@
                 out_specs=[head_block(*shape.shape[1:]) for shape in shapes],
             ),
             out_shape=shapes,
-            compiler_params=params(40),
+            compiler_params=params(48),
             name="rest_part",
             cost_estimate=cost(
                 6 * half * rows * (head_size * (3 * feat_half + feat_size) + 2 * rows * (feat_size + head_size)),
@@ -332,18 +331,21 @@
             x = jnp.concatenate([x, swap(x, bit)], axis=1)
         return x
 
-    order = [(which, d) for which in (odd, 1 - odd) for d in even]
+    order = [(which, d) for which in (0, 1) for d in even]
     part = len(order) // 4
-    own, other = odd.reshape(1), (1 - odd).reshape(1)
+    firsts = odd ^ np.array([0, 1], np.int32)
+    other = odd ^ np.array([1], np.int32)
     other_state, other_feat = key_part(other)
     out_weight, other_state = together((out_weight, other_state))
-    starts = jnp.stack([(h ^ flip ^ d) * depth + which * wide for flip in (0, 1) for which, d in order])
     count = len(order)
+    head_masks = np.array([flip ^ d for flip in (0, 1) for _, d in order], np.int32)
+    half_masks = np.array([which for _ in (0, 1) for which, _ in order], np.int32)
+    starts = (h ^ head_masks) * depth + (odd ^ half_masks) * wide
     (first_part,) = arranged(out_weight, starts, [list(range(part))])
     first_part = widen(first_part)
     far_1 = swap(first_part, far)
     from_neighbour = swap(other_state, 1)
-    own_state, own_query, other_query = rest_part(jnp.concatenate([own, other]), other_feat)
+    own_state, own_query, other_query = rest_part(firsts, other_feat)
     out_weight, own_state = together((out_weight, own_state))
     spans = [(part, 3 * part), (3 * part, count), (0, count)]
     spans += [(count, count + 2 * part), (count + 2 * part, 2 * count), (count, 2 * count)]
@@ -351,8 +353,12 @@
     kept_2, kept_3, kept = [widen(x) for x in (kept_2, kept_3, kept)]
     groups, perms, send, place = route_tables(ctx, heads, rels)
     steps, size = len(perms), len(groups[0])
-    send_here = jnp.asarray(send)[me]
-    place_here = jnp.asarray(place)[me]
+    send_here, place_here = [
+        lax.dynamic_slice(
+            x.reshape(ctx, heads, -1), (c, h, 0), (1, 1, x.shape[1]), allow_negative_indices=False
+        ).reshape(-1)
+        for x in (send, place)
+    ]
 
     from_neighbour, own_state, far_1, kept_2, kept, given_1, given_2, given = together(
         (from_neighbour, own_state, far_1, kept_2, kept, given_1, given_2, given)
@@ -397,10 +403,10 @@
     met, across = swap(own_mixed, PAIR), swap(own_mixed, 0, head_bits[0])
     far_4 = swap(taken_1, far)
     both_2 = swap(far_2, near)
-    other_prior, far_3, far_4, both_2, met, across, taken_2 = together(
-        (other_prior, far_3, far_4, both_2, met, across, taken_2)
-    )
     other_mixed, both = mix(*other_query, other_prior, met)
+    other_mixed, both, across, far_3, far_4, both_2, taken_2 = together(
+        (other_mixed, both, across, far_3, far_4, both_2, taken_2)
+    )
     other_met = swap(other_mixed, PAIR)
     both = swap(both, 0, head_bits[0])
     far_5 = swap(taken_2, far)

time: 192 us -> 180 us (0.938)
  local copies, waits for them, and re-layouts: 16.9 us -> 5.63 us
  waiting for transfers between devices: 84 us -> 86.8 us
  Pallas kernels: 36.3 us -> 34.1 us
    unnamed x84 -> x48, local copies, waits for them, and re-layouts: 15.4 us -> 4.25 us
    ppermute x26, waiting for transfers between devices: 73.9 us -> 76.6 us  [swap(): return lax.ppermute(x, AXES, pairs)]
    pallas_call x4, Pallas kernels: 13.5 us -> 11.4 us  [project(): pl.pallas_call(functools.partial(project_kernel, terms, len(used)), grid=...]
  transfers between devices with their start and end apart: 30 -> 30, of which waited for: 11 -> 15; matrix products, arithmetic and copies ran while one was open for 3% -> 3% of each run, Pallas kernels for 13% -> 14%
where the time goes in v4:
time: 180 us; the launch traced here: 179 us
  waiting for transfers between devices  86.8 us (48%)
  starting transfers between devices  47.9 us (27%)
  Pallas kernels  34.1 us (19%)
  local copies, waits for them, and re-layouts  5.63 us (3%)
  other arithmetic  4.5 us (2%)
    ppermute x26, waiting for transfers between devices, swap(): return lax.ppermute(x, AXES, pairs)  76.6 us
    ppermute x26, starting transfers between devices, swap(): return lax.ppermute(x, AXES, pairs)  39.6 us
    pallas_call x4, Pallas kernels, project(): pl.pallas_call(functools.partial(project_kernel, terms, len(used)), grid=...  11.4 us
    pallas_call x1, Pallas kernels, rest_part(): pl.pallas_call(rest_kernel, grid_spec=pltpu.PrefetchScalarGridSpec(num_sc...  10.6 us
    ppermute x4, waiting for transfers between devices, body(): lax.ppermute(part, AXES, perm)  10.2 us
    ppermute x4, starting transfers between devices, body(): lax.ppermute(part, AXES, perm)  8.22 us
    unnamed x48, local copies, waits for them, and re-layouts  4.25 us
    pallas_call x1, Pallas kernels, key_part(): pl.pallas_call(key_kernel, grid_spec=pltpu.PrefetchScalarGridSpec(num_sca...  4.02 us
  transfers between devices with their start and end apart: 30, of which 15 were waited for; matrix products, arithmetic and copies ran while one was open for 3% of the time, Pallas kernels for 14%

profile of v4, /device:TPU:0, one launch (start us, length us, event | category | flops | bytes accessed | tf_op | source)
XLA Modules:
  0.0 179.2 jit_solution(7238511119305577672)
XLA Ops:
  0.0 4.0 %key_part.1 = (f32[4,264,128]{2,1,0:T(8,128)}, f32[4,256,256]{2,1,0:T(8,128)}) custom-call(s32[1]{0:T(128)} %bitcast.first, f32[256,1024]{1,0:T(8,128)} %refs_0_.1, f32[8,128,128]{2,1,0:T(8,128)} %refs_1_.1, f32[256,1024]{1,0:T(8,128)} %refs_7_.1), custom_call_target="tpu_custom_call" | custom-call | flops 603979776 | bytes 3145728 | tf_op jit(solution)/shard_map/key_part/pallas_call | solution.py:230
  4.0 3.0 %collective-permute-start = (f32[4,264,128]{2,1,0:T(8,128)}, f32[4,264,128]{2,1,0:T(8,128)}, u32[]{:S(2)}, u32[]{:S(2)}) collective-permute-start(f32[4,264,128]{2,1,0:T(8,128)} %get-tuple-element.76), channel_id=1, source_target_pairs={{0,4},{1,5},{2,6},{3,7},{4,0},{5,1},{6,2},{7,3},{8,12},{9,13},{10,... | collective-permute-start | bytes 1622024 | tf_op jit(solution)/shard_map/ppermute | solution.py:212
  7.6 2.7 %collective-permute-start.1 = (f32[512,128]{1,0:T(8,128)S(1)}, f32[512,128]{1,0:T(8,128)S(1)}, u32[]{:S(2)}, u32[]{:S(2)}) collective-permute-start(f32[512,128]{1,0:T(8,128)S(1)} %arrange.2), channel_id=1, source_target_pairs={{0,16},{1,17},{2,18},{3,19},{4,20},{5,21},{6,22},{7,23},{8,24},{9,... | collective-permute-start | bytes 786440 | tf_op jit(solution)/shard_map/ppermute | solution.py:212
  11.3 10.6 %rest_part.1 = (f32[4,264,128]{2,1,0:T(8,128)S(1)}, f32[4,256,256]{2,1,0:T(8,128)S(1)}, f32[4,256,128]{2,1,0:T(8,128)S(1)}, f32[4,256,128]{2,1,0:T(8,128)S(1)}, ...) custom-call(s32[2]{0:T(128)S(1)} %iota_xor_fusion.first, f32[256,1024]{1,0:T(8,128)} %refs_0_.1, ...), custom_call_target="tpu_custom_call" | custom-call | flops 3422552064 | bytes 8388608 | tf_op jit(solution)/shard_map/rest_part/pallas_call | solution.py:257
  23.5 2.5 %arrange.3 = (f32[1024,128]{1,0:T(8,128)}, f32[512,128]{1,0:T(8,128)S(1)}, f32[2048,128]{1,0:T(8,128)S(1)}, f32[1024,128]{1,0:T(8,128)}, f32[1024,128]{1,0:T(8,128)}, /*index=5*/f32[2048,128]{1,0:T(8,128)}) custom-call(s32[8]{0:T(128)S(1)} %multiply_add_fusion.starts, f32[4096,128]{1,0:T(8,128)S(1)} %copy-done), custom_call_target="tpu_custom_call" | custom-call | bytes 7864320 | tf_op jit(solution)/shard_map/arrange/pallas_call | solution.py:314
  30.7 17.7 %collective-permute-done.2 = f32[4,264,128]{2,1,0:T(8,128)S(1)} collective-permute-done((f32[4,264,128]{2,1,0:T(8,128)S(1)}, f32[4,264,128]{2,1,0:T(8,128)S(1)}, u32[]{:S(2)}, u32[]{:S(2)}) %collective-permute-start.2) | collective-permute-done | bytes 540704 | tf_op jit(solution)/shard_map/ppermute | solution.py:212
  49.2 2.1 %broadcast_select_fusion = (f32[4,264,128]{2,1,0:T(8,128)}, f32[4,264,128]{2,1,0:T(8,128)S(1)}) fusion(f32[4,264,128]{2,1,0:T(8,128)} %copy-done.21, pred[]{:T(512)S(6)} %ne.4, f32[4,264,128]{2,1,0:T(8,128)} %copy-done.19), kind=kLoop, calls=%fused_computation.4 | loop fusion | flops 270336 | bytes 2162689 | tf_op jit(solution)/shard_map/jit(_where)/select_n | solution.py:375
  51.3 5.6 %collective-permute-done.3.refs_16_.refs_8_ = f32[1024,128]{1,0:T(8,128)} collective-permute-done((f32[1024,128]{1,0:T(8,128)}, f32[1024,128]{1,0:T(8,128)}, u32[]{:S(2)}, u32[]{:S(2)}) %collective-permute-start.3) | collective-permute-done | bytes 524320 | tf_op jit(solution)/shard_map/ppermute | solution.py:212
  58.5 2.2 %collective-permute-start.8 = (f32[2,264,128]{2,1,0:T(8,128)S(1)}, f32[2,264,128]{2,1,0:T(8,128)}, u32[]{:S(2)}, u32[]{:S(2)}) collective-permute-start(f32[2,264,128]{2,1,0:T(8,128)S(1)} %slice_select_fusion), channel_id=1, source_target_pairs={{0,16},{1,17},{2,18},{3,19},{4,20},{5,21},{6,22},{7,23},{8,24},{9,... | collective-permute-start | bytes 811016 | tf_op jit(solution)/shard_map/ppermute | solution.py:212
  60.7 4.7 %collective-permute-done.8 = f32[2,264,128]{2,1,0:T(8,128)} collective-permute-done((f32[2,264,128]{2,1,0:T(8,128)S(1)}, f32[2,264,128]{2,1,0:T(8,128)}, u32[]{:S(2)}, u32[]{:S(2)}) %collective-permute-start.8) | collective-permute-done | bytes 270368 | tf_op jit(solution)/shard_map/ppermute | solution.py:212
  67.3 11.3 %collective-permute-start.13 = (f32[512,128]{1,0:T(8,128)}, f32[512,128]{1,0:T(8,128)S(1)}, u32[]{:S(2)}, u32[]{:S(2)}) collective-permute-start(f32[512,128]{1,0:T(8,128)} %copy-done.18), channel_id=1, source_target_pairs={{0,16},{1,17},{2,18},{3,19},{4,20},{5,21},{6,22},{7,23},{8,24},{9,... | collective-permute-start | bytes 786440 | tf_op jit(solution)/shard_map/ppermute | solution.py:212
  79.8 7.6 %collective-permute-done.11.refs_9_ = f32[512,128]{1,0:T(8,128)S(1)} collective-permute-done((f32[512,128]{1,0:T(8,128)S(1)}, f32[512,128]{1,0:T(8,128)S(1)}, u32[]{:S(2)}, u32[]{:S(2)}) %collective-permute-start.11) | collective-permute-done | bytes 262176 | tf_op jit(solution)/shard_map/ppermute | solution.py:212
  87.6 2.6 %collective-permute-start.12 = (f32[4,264,128]{2,1,0:T(8,128)S(1)}, f32[4,264,128]{2,1,0:T(8,128)S(1)}, u32[]{:S(2)}, u32[]{:S(2)}) collective-permute-start(f32[4,264,128]{2,1,0:T(8,128)S(1)} %get-tuple-element.138), channel_id=1, source_target_pairs={{0,4},{1,5},{2,6},{3,7},{4,0},{5,1},{6,2},{7,3},{8,12},{9,13},{10,... | collective-permute-start | bytes 1622024 | tf_op jit(solution)/shard_map/ppermute | solution.py:212
  95.8 16.5 %collective-permute-done.14.refs_0_.refs_1_ = f32[256,512]{1,0:T(8,128)S(1)} collective-permute-done((f32[256,512]{1,0:T(8,128)S(1)}, f32[256,512]{1,0:T(8,128)S(1)}, u32[]{:S(2)}, u32[]{:S(2)}) %collective-permute-start.14) | collective-permute-done | bytes 524320 | tf_op jit(solution)/shard_map/ppermute | solution.py:212
  113.8 3.7 %collective-permute-done.16.refs_6_.refs_13_ = f32[1024,128]{1,0:T(8,128)S(1)} collective-permute-done((f32[1024,128]{1,0:T(8,128)}, f32[1024,128]{1,0:T(8,128)S(1)}, u32[]{:S(2)}, u32[]{:S(2)}) %collective-permute-start.16) | collective-permute-done | bytes 524320 | tf_op jit(solution)/shard_map/ppermute | solution.py:212
  123.3 12.5 %collective-permute-done.21.refs_17_ = f32[512,128]{1,0:T(8,128)S(1)} collective-permute-done((f32[512,128]{1,0:T(8,128)S(1)}, f32[512,128]{1,0:T(8,128)S(1)}, u32[]{:S(2)}, u32[]{:S(2)}) %collective-permute-start.21) | collective-permute-done | bytes 262176 | tf_op jit(solution)/shard_map/ppermute | solution.py:212
  135.9 3.4 %collective-permute-done.18.refs_1_ = f32[256,512]{1,0:T(8,128)S(1)} collective-permute-done((f32[256,512]{1,0:T(8,128)S(1)}, f32[256,512]{1,0:T(8,128)S(1)}, u32[]{:S(2)}, u32[]{:S(2)}) %collective-permute-start.18) | collective-permute-done | bytes 524320 | tf_op jit(solution)/shard_map/ppermute | solution.py:212
  143.3 4.6 %project.4.refs_10_ = f32[512,1024]{1,0:T(8,128)S(1)} custom-call(f32[256,512]{1,0:T(8,128)S(1)} %mix.2.refs_0_, f32[256,512]{1,0:T(8,128)S(1)} %collective-permute-done.14.refs_0_.refs_1_, f32[256,512]{1,0:T(8,128)S(1)} %collective-permute-done.15.refs_2_, f32[512,512]{1,0:T(8,128)S(1)} %collective-permute-done.19.refs_3_.refs_0_.refs_4_, ...), custom_call_target="tpu_custom_call" | custom-call | flops 2818572288 | bytes 5767168 | tf_op jit(solution)/shard_map/project/pallas_call | solution.py:441
  147.9 2.9 %project.5.refs_6_.refs_12_ = f32[512,1024]{1,0:T(8,128)S(1)} custom-call(f32[256,512]{1,0:T(8,128)S(1)} %get-tuple-element.114.refs_0_, f32[256,512]{1,0:T(8,128)S(1)} %collective-permute-done.18.refs_1_, f32[2048,128]{1,0:T(8,128)S(1)} %collective-permute-done.5.refs_4_.refs_11_.refs_2_.refs_6_, ...), custom_call_target="tpu_custom_call" | custom-call | flops 1610612736 | bytes 4194304 | tf_op jit(solution)/shard_map/project/pallas_call | solution.py:441
  152.7 3.0 %project.7 = f32[512,512]{1,0:T(8,128)S(1)} custom-call(f32[256,512]{1,0:T(8,128)S(1)} %mix.2.refs_0_, f32[256,512]{1,0:T(8,128)S(1)} %collective-permute-done.14.refs_0_.refs_1_, f32[256,512]{1,0:T(8,128)S(1)} %collective-permute-done.15.refs_2_, f32[512,512]{1,0:T(8,128)S(1)} %collective-permute-done.19.refs_3_.refs_0_.refs_4_, ...), custom_call_target="tpu_custom_call" | custom-call | flops 1207959552 | bytes 2621440 | tf_op jit(solution)/shard_map/project/pallas_call | solution.py:441
  159.8 2.9 %collective-permute-start.27 = (f32[256,256]{1,0:T(8,128)S(1)}, f32[256,256]{1,0:T(8,128)S(1)}, u32[]{:S(2)}, u32[]{:S(2)}) collective-permute-start(f32[256,256]{1,0:T(8,128)S(1)} %get-tuple-element.134), channel_id=1, source_target_pairs={{0,2},{1,0},{2,10},{3,8},{4,6},{5,4},{6,14},{7,12},{8,3},{9,1},{10... | collective-permute-start | bytes 786440 | tf_op jit(solution)/shard_map/ppermute | solution.py:492
  163.9 3.4 %collective-permute-start.29 = (f32[256,256]{1,0:T(8,128)S(1)}, f32[256,256]{1,0:T(8,128)S(1)}, u32[]{:S(2)}, u32[]{:S(2)}) collective-permute-start(f32[256,256]{1,0:T(8,128)S(1)} %get-tuple-element.136), channel_id=1, source_target_pairs={{0,10},{1,8},{2,2},{3,0},{4,14},{5,12},{6,6},{7,4},{8,11},{9,9},{1... | collective-permute-start | bytes 786440 | tf_op jit(solution)/shard_map/ppermute | solution.py:492
  167.3 7.1 %collective-permute-done.27.refs_1_ = f32[256,256]{1,0:T(8,128)S(1)} collective-permute-done((f32[256,256]{1,0:T(8,128)S(1)}, f32[256,256]{1,0:T(8,128)S(1)}, u32[]{:S(2)}, u32[]{:S(2)}) %collective-permute-start.27) | collective-permute-done | bytes 262176 | tf_op jit(solution)/shard_map/ppermute | solution.py:492
  174.5 3.0 %collective-permute-done.29.refs_3_ = f32[256,256]{1,0:T(8,128)S(1)} collective-permute-done((f32[256,256]{1,0:T(8,128)S(1)}, f32[256,256]{1,0:T(8,128)S(1)}, u32[]{:S(2)}, u32[]{:S(2)}) %collective-permute-start.29) | collective-permute-done | bytes 262176 | tf_op jit(solution)/shard_map/ppermute | solution.py:492
  (106 shorter events, 39.4 us)
Async XLA Ops:
  4.0 22.8 %collective-permute-start = (f32[4,264,128]{2,1,0:T(8,128)}, f32[4,264,128]{2,1,0:T(8,128)}, u32[]{:S(2)}, u32[]{:S(2)}) collective-permute-start(f32[4,264,128]{2,1,0:T(8,128)} %get-tuple-element.76), channel_id=1, source_target_pairs={{0,4},{1,5},{2,6},{3,7},{4,0},{5,1},{6,2},{7,3},{8,12},{9,13},{10,... | collective-permute-start | bytes 1622024 | tf_op jit(solution)/shard_map/ppermute | solution.py:212
  7.6 19.2 %collective-permute-start.1 = (f32[512,128]{1,0:T(8,128)S(1)}, f32[512,128]{1,0:T(8,128)S(1)}, u32[]{:S(2)}, u32[]{:S(2)}) collective-permute-start(f32[512,128]{1,0:T(8,128)S(1)} %arrange.2), channel_id=1, source_target_pairs={{0,16},{1,17},{2,18},{3,19},{4,20},{5,21},{6,22},{7,23},{8,24},{9,... | collective-permute-start | bytes 786440 | tf_op jit(solution)/shard_map/ppermute | solution.py:212
  27.9 20.5 %collective-permute-start.2 = (f32[4,264,128]{2,1,0:T(8,128)S(1)}, f32[4,264,128]{2,1,0:T(8,128)S(1)}, u32[]{:S(2)}, u32[]{:S(2)}) collective-permute-start(f32[4,264,128]{2,1,0:T(8,128)S(1)} %add.19), channel_id=1, source_target_pairs={{0,8},{1,9},{2,10},{3,11},{4,12},{5,13},{6,14},{7,15},{8,0},{9,1},... | collective-permute-start | bytes 1622024 | tf_op jit(solution)/shard_map/ppermute | solution.py:212
  29.5 27.4 %collective-permute-start.4 = (f32[2048,128]{1,0:T(8,128)S(1)}, f32[2048,128]{1,0:T(8,128)S(1)}, u32[]{:S(2)}, u32[]{:S(2)}) collective-permute-start(f32[2048,128]{1,0:T(8,128)S(1)} %get-tuple-element.89.refs_7_.refs_14_.refs_6_.refs_2_), channel_id=1, source_target_pairs={{0,4},{1,5},{2,6},{3,7},{4,0},{5,1},{6,2},{7,3},{8,12},{9,13},{10,... | collective-permute-start | bytes 3145736 | tf_op jit(solution)/shard_map/ppermute | solution.py:212
  30.1 26.9 %collective-permute-start.5 = (f32[2048,128]{1,0:T(8,128)}, f32[2048,128]{1,0:T(8,128)S(1)}, u32[]{:S(2)}, u32[]{:S(2)}) collective-permute-start(f32[2048,128]{1,0:T(8,128)} %get-tuple-element.90), channel_id=1, source_target_pairs={{0,1},{1,0},{2,3},{3,2},{4,5},{5,4},{6,7},{7,6},{8,9},{9,8},{10,11... | collective-permute-start | bytes 3145736 | tf_op jit(solution)/shard_map/ppermute | solution.py:212
  30.1 26.8 %collective-permute-start.3 = (f32[1024,128]{1,0:T(8,128)}, f32[1024,128]{1,0:T(8,128)}, u32[]{:S(2)}, u32[]{:S(2)}) collective-permute-start(f32[1024,128]{1,0:T(8,128)} %get-tuple-element.88), channel_id=1, source_target_pairs={{0,16},{1,17},{2,18},{3,19},{4,20},{5,21},{6,22},{7,23},{8,24},{9,... | collective-permute-start | bytes 1572872 | tf_op jit(solution)/shard_map/ppermute | solution.py:212
  30.5 26.4 %collective-permute-start.6 = (f32[1024,128]{1,0:T(8,128)}, f32[1024,128]{1,0:T(8,128)}, u32[]{:S(2)}, u32[]{:S(2)}) collective-permute-start(f32[1024,128]{1,0:T(8,128)} %get-tuple-element.91), channel_id=1, source_target_pairs={{0,1},{1,0},{2,3},{3,2},{4,5},{5,4},{6,7},{7,6},{8,9},{9,8},{10,11... | collective-permute-start | bytes 1572872 | tf_op jit(solution)/shard_map/ppermute | solution.py:212
  56.9 30.4 %collective-permute-start.10 = (f32[2048,128]{1,0:T(8,128)S(1)}, f32[2048,128]{1,0:T(8,128)}, u32[]{:S(2)}, u32[]{:S(2)}) collective-permute-start(f32[2048,128]{1,0:T(8,128)S(1)} %collective-permute-done.5.refs_4_.refs_11_.refs_2_.refs_6_), channel_id=1, source_target_pairs={{0,4},{1,5},{2,6},{3,7},{4,0},{5,1},{6,2},{7,3},{8,12},{9,13},{10,... | collective-permute-start | bytes 3145736 | tf_op jit(solution)/shard_map/ppermute | solution.py:212
  65.4 13.2 %collective-permute-start.9 = (f32[2,264,128]{2,1,0:T(8,128)}, f32[2,264,128]{2,1,0:T(8,128)}, u32[]{:S(2)}, u32[]{:S(2)}) collective-permute-start(f32[2,264,128]{2,1,0:T(8,128)} %collective-permute-done.8), channel_id=1, source_target_pairs={{16,24},{17,25},{18,26},{19,27},{20,28},{21,29},{22,30},{23,31},{2... | collective-permute-start | bytes 811016 | tf_op jit(solution)/shard_map/ppermute | solution.py:212
  66.8 20.6 %collective-permute-start.11 = (f32[512,128]{1,0:T(8,128)S(1)}, f32[512,128]{1,0:T(8,128)S(1)}, u32[]{:S(2)}, u32[]{:S(2)}) collective-permute-start(f32[512,128]{1,0:T(8,128)S(1)} %collective-permute-done.1.refs_9_), channel_id=1, source_target_pairs={{0,4},{1,5},{2,6},{3,7},{4,0},{5,1},{6,2},{7,3},{8,12},{9,13},{10,... | collective-permute-start | bytes 786440 | tf_op jit(solution)/shard_map/ppermute | solution.py:212
  67.3 24.0 %collective-permute-start.13 = (f32[512,128]{1,0:T(8,128)}, f32[512,128]{1,0:T(8,128)S(1)}, u32[]{:S(2)}, u32[]{:S(2)}) collective-permute-start(f32[512,128]{1,0:T(8,128)} %copy-done.18), channel_id=1, source_target_pairs={{0,16},{1,17},{2,18},{3,19},{4,20},{5,21},{6,22},{7,23},{8,24},{9,... | collective-permute-start | bytes 786440 | tf_op jit(solution)/shard_map/ppermute | solution.py:212
  87.6 24.8 %collective-permute-start.12 = (f32[4,264,128]{2,1,0:T(8,128)S(1)}, f32[4,264,128]{2,1,0:T(8,128)S(1)}, u32[]{:S(2)}, u32[]{:S(2)}) collective-permute-start(f32[4,264,128]{2,1,0:T(8,128)S(1)} %get-tuple-element.138), channel_id=1, source_target_pairs={{0,4},{1,5},{2,6},{3,7},{4,0},{5,1},{6,2},{7,3},{8,12},{9,13},{10,... | collective-permute-start | bytes 1622024 | tf_op jit(solution)/shard_map/ppermute | solution.py:212
  91.4 21.0 %collective-permute-start.14 = (f32[256,512]{1,0:T(8,128)S(1)}, f32[256,512]{1,0:T(8,128)S(1)}, u32[]{:S(2)}, u32[]{:S(2)}) collective-permute-start(f32[256,512]{1,0:T(8,128)S(1)} %mix.2.refs_0_), channel_id=1, source_target_pairs={{0,8},{1,9},{2,10},{3,11},{4,12},{5,13},{6,14},{7,15},{8,0},{9,1},... | collective-permute-start | bytes 1572872 | tf_op jit(solution)/shard_map/ppermute | solution.py:212
  91.4 22.3 %collective-permute-start.15 = (f32[256,512]{1,0:T(8,128)S(1)}, f32[256,512]{1,0:T(8,128)S(1)}, u32[]{:S(2)}, u32[]{:S(2)}) collective-permute-start(f32[256,512]{1,0:T(8,128)S(1)} %mix.2.refs_0_), channel_id=1, source_target_pairs={{0,2},{1,3},{2,0},{3,1},{4,6},{5,7},{6,4},{7,5},{8,10},{9,11},{10,... | collective-permute-start | bytes 1572872 | tf_op jit(solution)/shard_map/ppermute | solution.py:212
  93.0 24.5 %collective-permute-start.16 = (f32[1024,128]{1,0:T(8,128)}, f32[1024,128]{1,0:T(8,128)S(1)}, u32[]{:S(2)}, u32[]{:S(2)}) collective-permute-start(f32[1024,128]{1,0:T(8,128)} %collective-permute-done.6), channel_id=1, source_target_pairs={{0,16},{1,17},{2,18},{3,19},{4,20},{5,21},{6,22},{7,23},{8,24},{9,... | collective-permute-start | bytes 1572872 | tf_op jit(solution)/shard_map/ppermute | solution.py:212
  94.3 23.2 %collective-permute-start.17 = (f32[1024,128]{1,0:T(8,128)}, f32[1024,128]{1,0:T(8,128)S(1)}, u32[]{:S(2)}, u32[]{:S(2)}) collective-permute-start(f32[1024,128]{1,0:T(8,128)} %collective-permute-done.3.refs_16_.refs_8_), channel_id=1, source_target_pairs={{0,4},{1,5},{2,6},{3,7},{4,0},{5,1},{6,2},{7,3},{8,12},{9,13},{10,... | collective-permute-start | bytes 1572872 | tf_op jit(solution)/shard_map/ppermute | solution.py:212
  117.5 23.0 %collective-permute-start.19 = (f32[512,512]{1,0:T(8,128)S(1)}, f32[512,512]{1,0:T(8,128)S(1)}, u32[]{:S(2)}, u32[]{:S(2)}) collective-permute-start(f32[512,512]{1,0:T(8,128)S(1)} %get-tuple-element.115), channel_id=1, source_target_pairs={{0,2},{1,3},{2,0},{3,1},{4,6},{5,7},{6,4},{7,5},{8,10},{9,11},{10,... | collective-permute-start | bytes 3145736 | tf_op jit(solution)/shard_map/ppermute | solution.py:212
  118.0 21.2 %collective-permute-start.18 = (f32[256,512]{1,0:T(8,128)S(1)}, f32[256,512]{1,0:T(8,128)S(1)}, u32[]{:S(2)}, u32[]{:S(2)}) collective-permute-start(f32[256,512]{1,0:T(8,128)S(1)} %get-tuple-element.114.refs_0_), channel_id=1, source_target_pairs={{0,8},{1,9},{2,10},{3,11},{4,12},{5,13},{6,14},{7,15},{8,0},{9,1},... | collective-permute-start | bytes 1572872 | tf_op jit(solution)/shard_map/ppermute | solution.py:212
  118.0 22.5 %collective-permute-start.20 = (f32[1024,128]{1,0:T(8,128)}, f32[1024,128]{1,0:T(8,128)S(1)}, u32[]{:S(2)}, u32[]{:S(2)}) collective-permute-start(f32[1024,128]{1,0:T(8,128)} %collective-permute-done.7), channel_id=1, source_target_pairs={{0,16},{1,17},{2,18},{3,19},{4,20},{5,21},{6,22},{7,23},{8,24},{9,... | collective-permute-start | bytes 1572872 | tf_op jit(solution)/shard_map/ppermute | solution.py:212
  119.9 20.6 %collective-permute-start.22 = (f32[1024,128]{1,0:T(8,128)S(1)}, f32[1024,128]{1,0:T(8,128)S(1)}, u32[]{:S(2)}, u32[]{:S(2)}) collective-permute-start(f32[1024,128]{1,0:T(8,128)S(1)} %collective-permute-done.16.refs_6_.refs_13_), channel_id=1, source_target_pairs={{0,4},{1,5},{2,6},{3,7},{4,0},{5,1},{6,2},{7,3},{8,12},{9,13},{10,... | collective-permute-start | bytes 1572872 | tf_op jit(solution)/shard_map/ppermute | solution.py:212
  121.1 14.8 %collective-permute-start.21 = (f32[512,128]{1,0:T(8,128)S(1)}, f32[512,128]{1,0:T(8,128)S(1)}, u32[]{:S(2)}, u32[]{:S(2)}) collective-permute-start(f32[512,128]{1,0:T(8,128)S(1)} %collective-permute-done.13.refs_4_), channel_id=1, source_target_pairs={{0,4},{1,5},{2,6},{3,7},{4,0},{5,1},{6,2},{7,3},{8,12},{9,13},{10,... | collective-permute-start | bytes 786440 | tf_op jit(solution)/shard_map/ppermute | solution.py:212
  140.5 12.1 %collective-permute-start.23 = (f32[256,512]{1,0:T(8,128)S(1)}, f32[256,512]{1,0:T(8,128)S(1)}, u32[]{:S(2)}, u32[]{:S(2)}) collective-permute-start(f32[256,512]{1,0:T(8,128)S(1)} %collective-permute-done.18.refs_1_), channel_id=1, source_target_pairs={{0,2},{1,3},{2,0},{3,1},{4,6},{5,7},{6,4},{7,5},{8,10},{9,11},{10,... | collective-permute-start | bytes 1572872 | tf_op jit(solution)/shard_map/ppermute | solution.py:212
  159.8 14.6 %collective-permute-start.27 = (f32[256,256]{1,0:T(8,128)S(1)}, f32[256,256]{1,0:T(8,128)S(1)}, u32[]{:S(2)}, u32[]{:S(2)}) collective-permute-start(f32[256,256]{1,0:T(8,128)S(1)} %get-tuple-element.134), channel_id=1, source_target_pairs={{0,2},{1,0},{2,10},{3,8},{4,6},{5,4},{6,14},{7,12},{8,3},{9,1},{10... | collective-permute-start | bytes 786440 | tf_op jit(solution)/shard_map/ppermute | solution.py:492
  163.9 13.6 %collective-permute-start.29 = (f32[256,256]{1,0:T(8,128)S(1)}, f32[256,256]{1,0:T(8,128)S(1)}, u32[]{:S(2)}, u32[]{:S(2)}) collective-permute-start(f32[256,256]{1,0:T(8,128)S(1)} %get-tuple-element.136), channel_id=1, source_target_pairs={{0,10},{1,8},{2,2},{3,0},{4,14},{5,12},{6,6},{7,4},{8,11},{9,9},{1... | collective-permute-start | bytes 786440 | tf_op jit(solution)/shard_map/ppermute | solution.py:492
  (30 other events, 305.9 us)

commit v5 on v4

--- a/solution.py
+++ b/solution.py
@@ -72,10 +72,8 @@
     denom_ref[0] = jnp.broadcast_to(jnp.sum(weights, axis=-1, keepdims=True), denom_ref.shape[1:])
 
 
-def rest_kernel(first, *refs):
-    k_ref, k_map_ref, q_ref, q_map_ref, v_ref, other_q_ref, other_q_map_ref, other_v_ref, other_feat_ref = refs[:9]
-    state_ref, feat_ref, numer_ref, denom_ref, other_out_ref, other_numer_ref, other_denom_ref = refs[9:]
-    heads, head_size, feat_half = k_map_ref.shape
+def own_kernel(first, k_ref, k_map_ref, q_ref, q_map_ref, v_ref, state_ref, feat_ref, numer_ref, denom_ref):
+    feat_half = k_map_ref.shape[2]
     size = 2 * feat_half
     row = lax.broadcasted_iota(jnp.int32, (EXTRA, feat_half), 0)
     key_feat = features(k_ref[...], k_map_ref[0])
@@ -85,9 +83,12 @@
     feat = features(q_ref[...], q_map_ref[0])
     feat_ref[0] = feat
     attend(feat, key_feat, v_ref[...], numer_ref, denom_ref)
-    feat = features(other_q_ref[...], other_q_map_ref[0])
-    other_out_ref[0] = feat
-    attend(feat, other_feat_ref[0], other_v_ref[...], other_numer_ref, other_denom_ref)
+
+
+def query_kernel(first, q_ref, q_map_ref, v_ref, key_feat_ref, feat_ref, numer_ref, denom_ref):
+    feat = features(q_ref[...], q_map_ref[0])
+    feat_ref[0] = feat
+    attend(feat, key_feat_ref[0], v_ref[...], numer_ref, denom_ref)
 
 
 def mix_kernel(qfeat_ref, numer_ref, denom_ref, prior_ref, *refs):
@@ -245,34 +246,49 @@
             ),
         )(first, keys, key_map, values)
 
-    def rest_part(firsts, other_feat):
-        def columns(which):
-            return pl.BlockSpec((rows, head_size), lambda i, first: (0, first[which] * half + i))
-
-        def maps(which):
-            return pl.BlockSpec((1, head_size, feat_half), lambda i, first: (first[which] * half + i, 0, 0))
-
-        query_shapes = [of(half, rows, feat_size), of(half, rows, head_size), of(half, rows, head_size)]
-        shapes = [of(half, feat_size + EXTRA, head_size), *query_shapes, *query_shapes]
+    columns = pl.BlockSpec((rows, head_size), lambda i, first: (0, first[0] * half + i))
+    maps = pl.BlockSpec((1, head_size, feat_half), lambda i, first: (first[0] * half + i, 0, 0))
+    query_shapes = [of(half, rows, feat_size), of(half, rows, head_size), of(half, rows, head_size)]
+    query_specs = [head_block(*shape.shape[1:]) for shape in query_shapes]
+
+    def own_part(first):
         outs = pl.pallas_call(
-            rest_kernel,
+            own_kernel,
             grid_spec=pltpu.PrefetchScalarGridSpec(
                 num_scalar_prefetch=1,
                 grid=(half,),
-                in_specs=[columns(0), maps(0), columns(0), maps(0), columns(0)]
-                + [columns(1), maps(1), columns(1), head_block(rows, feat_size)],
-                out_specs=[head_block(*shape.shape[1:]) for shape in shapes],
-            ),
-            out_shape=shapes,
+                in_specs=[columns, maps, columns, maps, columns],
+                out_specs=[head_block(feat_size + EXTRA, head_size), *query_specs],
+            ),
+            out_shape=[of(half, feat_size + EXTRA, head_size), *query_shapes],
             compiler_params=params(48),
-            name="rest_part",
+            name="own_part",
             cost_estimate=cost(
-                6 * half * rows * (head_size * (3 * feat_half + feat_size) + 2 * rows * (feat_size + head_size)),
-                half * rows * (8 * head_size + 4 * feat_size),
-                3 * half * rows * feat_size,
-            ),
-        )(firsts, keys, key_map, queries, query_map, values, queries, query_map, values, other_feat)
-        return outs[0], outs[1:4], outs[4:]
+                6 * half * rows * (head_size * (2 * feat_half + feat_size) + rows * (feat_size + head_size)),
+                half * rows * (5 * head_size + 3 * feat_size),
+                2 * half * rows * feat_size,
+            ),
+        )(first, keys, key_map, queries, query_map, values)
+        return outs[0], outs[1:]
+
+    def query_part(first, key_feat):
+        return pl.pallas_call(
+            query_kernel,
+            grid_spec=pltpu.PrefetchScalarGridSpec(
+                num_scalar_prefetch=1,
+                grid=(half,),
+                in_specs=[columns, maps, columns, head_block(rows, feat_size)],
+                out_specs=query_specs,
+            ),
+            out_shape=query_shapes,
+            compiler_params=params(32),
+            name="query_part",
+            cost_estimate=cost(
+                6 * half * rows * (head_size * feat_half + rows * (feat_size + head_size)),
+                half * rows * (4 * head_size + 2 * feat_size),
+                half * rows * feat_size,
+            ),
+        )(first, queries, query_map, values, key_feat)
 
     def mix(qfeat, numer, denom, prior, below=None):
         columns = pl.BlockSpec((rows, head_size), lambda i: (0, i))
@@ -333,10 +349,11 @@
 
     order = [(which, d) for which in (0, 1) for d in even]
     part = len(order) // 4
-    firsts = odd ^ np.array([0, 1], np.int32)
+    own = odd ^ np.array([0], np.int32)
     other = odd ^ np.array([1], np.int32)
     other_state, other_feat = key_part(other)
-    out_weight, other_state = together((out_weight, other_state))
+    flags = {1 << b: (c & 1 << b) != 0 for b in range(ctx.bit_length() - 1)}
+    out_weight, other_state, flags = together((out_weight, other_state, flags))
     count = len(order)
     head_masks = np.array([flip ^ d for flip in (0, 1) for _, d in order], np.int32)
     half_masks = np.array([which for _ in (0, 1) for which, _ in order], np.int32)
@@ -345,7 +362,7 @@
     first_part = widen(first_part)
     far_1 = swap(first_part, far)
     from_neighbour = swap(other_state, 1)
-    own_state, own_query, other_query = rest_part(firsts, other_feat)
+    own_state, own_query = own_part(own)
     out_weight, own_state = together((out_weight, own_state))
     spans = [(part, 3 * part), (3 * part, count), (0, count)]
     spans += [(count, count + 2 * part), (count + 2 * part, 2 * count), (count, 2 * count)]
@@ -366,31 +383,36 @@
     far_2 = swap(kept_2, far)
     kept_near = swap(kept, near)
     taken, taken_1, taken_2 = [widen(swap(x, 0, 1)) for x in (given, given_1, given_2)]
-    earlier = jnp.where(odd == 0, own_state, from_neighbour)
+    earlier = jnp.where(flags[1], from_neighbour, own_state)
     total = own_state + from_neighbour
-    before = jnp.zeros_like(total)
+    parts = []
     bit = 2
     while 2 * bit < ctx:
-        got = swap(total, bit)
-        before = before + jnp.where((c & bit) != 0, got, 0.0)
-        total = total + got
+        if parts:
+            total = total + parts[-1]
+        parts.append(swap(total, bit))
         bit *= 2
-    total, before, far_2, kept_near, taken, taken_1, taken_2, far_1 = together(
-        (total, before, far_2, kept_near, taken, taken_1, taken_2, far_1)
+    total, parts, far_2, kept_near, taken, taken_1, taken_2, far_1 = together(
+        (total, parts, far_2, kept_near, taken, taken_1, taken_2, far_1)
     )
     taken_near = swap(taken, near)
     both_1 = swap(far_1, near)
-    second = (c & PAIR) != 0
-    got = swap(jnp.where(second, total[half // 2 :], total[: half // 2]), bit, keep=lambda i: not i & bit)
+    second = flags[PAIR]
+    sent = sum(jnp.where(second, x[half // 2 :], x[: half // 2]) for x in (total, *parts[-1:]))
+    got = swap(sent, bit, keep=lambda i: not i & bit)
     got, kept_3 = together((got, kept_3))
     met = swap(got, PAIR, keep=lambda i: i & bit)
     far_3 = swap(kept_3, far)
     got = jnp.concatenate([jnp.where(second, met, got), jnp.where(second, got, met)])
-    got, taken_near, both_1, taken_1, far_2 = together((got, taken_near, both_1, taken_1, far_2))
-    before = before + got
-
-    other_prior = swap(before + jnp.where(odd == 0, earlier, 0.0), 1)
-    own_mixed = mix(*own_query, before + jnp.where(odd == 1, earlier, 0.0))
+    got, taken_near, both_1, taken_1, far_2, other_feat = together(
+        (got, taken_near, both_1, taken_1, far_2, other_feat)
+    )
+    before = got
+    for b, part_sum in enumerate(parts):
+        before = before + jnp.where(flags[2 << b], part_sum, 0.0)
+
+    other_prior = swap(before + jnp.where(flags[1], 0.0, earlier), 1)
+    own_mixed = mix(*own_query, before + jnp.where(flags[1], earlier, 0.0))
     head_bits = [1 << b for b in range(1, heads.bit_length() - 1)]
 
     def spread(pieces):
@@ -403,7 +425,7 @@
     met, across = swap(own_mixed, PAIR), swap(own_mixed, 0, head_bits[0])
     far_4 = swap(taken_1, far)
     both_2 = swap(far_2, near)
-    other_mixed, both = mix(*other_query, other_prior, met)
+    other_mixed, both = mix(*query_part(other, other_feat), other_prior, met)
     other_mixed, both, across, far_3, far_4, both_2, taken_2 = together(
         (other_mixed, both, across, far_3, far_4, both_2, taken_2)
     )

time: 180 us -> 173 us (0.961)
  starting transfers between devices: 47.9 us -> 52.9 us
  Pallas kernels: 34.1 us -> 29.5 us
  local copies, waits for them, and re-layouts: 5.63 us -> 2.46 us
  other arithmetic: 4.5 us -> 1.43 us
    ppermute x26, starting transfers between devices: 39.6 us -> 45 us  [swap(): return lax.ppermute(x, AXES, pairs)]
    unnamed x48 -> x22, local copies, waits for them, and re-layouts: 4.25 us -> 1.08 us
    pallas_call x4, Pallas kernels: 11.4 us -> 8.28 us  [project(): pl.pallas_call(functools.partial(project_kernel, terms, len(used)), grid=...]
    select_n x2 -> x0, other arithmetic: 2.1 us -> none  [the longest x1 2.07 us: body(): before = before + jnp.where(c & bit != 0, got, 0.0)]
    pallas_call x1 -> x2, Pallas kernels: 10.6 us -> 10.6 us  [the longest x1 6.27 us: own_part(): pl.pallas_call(own_kernel, grid_spec=pltpu.PrefetchScalarGridSpec(num_sca...]
  transfers between devices with their start and end apart: 30 -> 30, of which waited for: 15 -> 18; matrix products, arithmetic and copies ran while one was open for 3% -> 2% of each run, Pallas kernels for 14% -> 12%
where the time goes in v5:
time: 173 us; the launch traced here: 172 us
  waiting for transfers between devices  85.6 us (49%)
  starting transfers between devices  52.9 us (31%)
  Pallas kernels  29.5 us (17%)
  local copies, waits for them, and re-layouts  2.46 us (1%)
    ppermute x26, waiting for transfers between devices, swap(): return lax.ppermute(x, AXES, pairs)  75.3 us
    ppermute x26, starting transfers between devices, swap(): return lax.ppermute(x, AXES, pairs)  45 us
    ppermute x4, waiting for transfers between devices, body(): lax.ppermute(part, AXES, perm)  10.2 us
    pallas_call x4, Pallas kernels, project(): pl.pallas_call(functools.partial(project_kernel, terms, len(used)), grid=...  8.28 us
    ppermute x4, starting transfers between devices, body(): lax.ppermute(part, AXES, perm)  7.91 us
    pallas_call x1, Pallas kernels, own_part(): pl.pallas_call(own_kernel, grid_spec=pltpu.PrefetchScalarGridSpec(num_sca...  6.27 us
    pallas_call x1, Pallas kernels, query_part(): pl.pallas_call(query_kernel, grid_spec=pltpu.PrefetchScalarGridSpec(num_s...  4.29 us
    pallas_call x1, Pallas kernels, key_part(): pl.pallas_call(key_kernel, grid_spec=pltpu.PrefetchScalarGridSpec(num_sca...  4.04 us
  transfers between devices with their start and end apart: 30, of which 18 were waited for; matrix products, arithmetic and copies ran while one was open for 2% of the time, Pallas kernels for 12%

profile of v5, /device:TPU:0, one launch (start us, length us, event | category | flops | bytes accessed | tf_op | source)
XLA Modules:
  0.0 172.1 jit_solution(3059671054047400534)
XLA Ops:
  0.0 4.0 %key_part.1 = (f32[4,264,128]{2,1,0:T(8,128)}, f32[4,256,256]{2,1,0:T(8,128)}) custom-call(s32[1]{0:T(128)S(6)} %xor.23.first, f32[256,1024]{1,0:T(8,128)} %k_ref.3, f32[8,128,128]{2,1,0:T(8,128)} %k_map_ref.1, f32[256,1024]{1,0:T(8,128)} %v_ref.5), custom_call_target="tpu_custom_call" | custom-call | flops 603979776 | bytes 3145728 | tf_op jit(solution)/shard_map/key_part/pallas_call | solution.py:231
  4.1 3.0 %collective-permute-start = (f32[4,264,128]{2,1,0:T(8,128)}, f32[4,264,128]{2,1,0:T(8,128)}, u32[]{:S(2)}, u32[]{:S(2)}) collective-permute-start(f32[4,264,128]{2,1,0:T(8,128)} %get-tuple-element.76), channel_id=1, source_target_pairs={{0,4},{1,5},{2,6},{3,7},{4,0},{5,1},{6,2},{7,3},{8,12},{9,13},{10,... | collective-permute-start | bytes 1622024 | tf_op jit(solution)/shard_map/ppermute | solution.py:213
  7.6 2.7 %collective-permute-start.1 = (f32[512,128]{1,0:T(8,128)S(1)}, f32[512,128]{1,0:T(8,128)S(1)}, u32[]{:S(2)}, u32[]{:S(2)}) collective-permute-start(f32[512,128]{1,0:T(8,128)S(1)} %arrange.2), channel_id=1, source_target_pairs={{0,16},{1,17},{2,18},{3,19},{4,20},{5,21},{6,22},{7,23},{8,24},{9,... | collective-permute-start | bytes 786440 | tf_op jit(solution)/shard_map/ppermute | solution.py:213
  11.3 6.3 %own_part.1 = (f32[4,264,128]{2,1,0:T(8,128)S(1)}, f32[4,256,256]{2,1,0:T(8,128)S(1)}, f32[4,256,128]{2,1,0:T(8,128)S(1)}, f32[4,256,128]{2,1,0:T(8,128)S(1)}) custom-call(s32[1]{0:T(128)} %bitcast.first, f32[256,1024]{1,0:T(8,128)S(1)} %copy-done.1, f32[8,128,128]{2,1,0:T(8,128)S(1)} %copy-done.4, f32[256,1024]{1,0:T(8,128)S(1)} %copy-done.5, ...), custom_call_target="tpu_custom_call" | custom-call | flops 2013265920 | bytes 5767168 | tf_op jit(solution)/shard_map/own_part/pallas_call | solution.py:255
  18.7 3.3 %collective-permute-done.1.refs_9_ = f32[512,128]{1,0:T(8,128)S(1)} collective-permute-done((f32[512,128]{1,0:T(8,128)S(1)}, f32[512,128]{1,0:T(8,128)S(1)}, u32[]{:S(2)}, u32[]{:S(2)}) %collective-permute-start.1) | collective-permute-done | bytes 262176 | tf_op jit(solution)/shard_map/ppermute | solution.py:213
  25.1 2.7 %collective-permute-start.2 = (f32[4,264,128]{2,1,0:T(8,128)S(1)}, f32[4,264,128]{2,1,0:T(8,128)S(1)}, u32[]{:S(2)}, u32[]{:S(2)}) collective-permute-start(f32[4,264,128]{2,1,0:T(8,128)S(1)} %add.19), channel_id=1, source_target_pairs={{0,8},{1,9},{2,10},{3,11},{4,12},{5,13},{6,14},{7,15},{8,0},{9,1},... | collective-permute-start | bytes 1622024 | tf_op jit(solution)/shard_map/ppermute | solution.py:213
  28.0 19.0 %collective-permute-done.3.refs_16_.refs_8_ = f32[1024,128]{1,0:T(8,128)S(1)} collective-permute-done((f32[1024,128]{1,0:T(8,128)S(1)}, f32[1024,128]{1,0:T(8,128)S(1)}, u32[]{:S(2)}, u32[]{:S(2)}) %collective-permute-start.3) | collective-permute-done | bytes 524320 | tf_op jit(solution)/shard_map/ppermute | solution.py:213
  51.4 3.1 %collective-permute-start.8 = (f32[2,264,128]{2,1,0:T(8,128)S(1)}, f32[2,264,128]{2,1,0:T(8,128)S(1)}, u32[]{:S(2)}, u32[]{:S(2)}) collective-permute-start(f32[2,264,128]{2,1,0:T(8,128)S(1)} %select_add_fusion.3), channel_id=1, source_target_pairs={{0,16},{1,17},{2,18},{3,19},{4,20},{5,21},{6,22},{7,23},{8,24},{9,... | collective-permute-start | bytes 811016 | tf_op jit(solution)/shard_map/ppermute | solution.py:213
  54.6 5.4 %collective-permute-done.8 = f32[2,264,128]{2,1,0:T(8,128)S(1)} collective-permute-done((f32[2,264,128]{2,1,0:T(8,128)S(1)}, f32[2,264,128]{2,1,0:T(8,128)S(1)}, u32[]{:S(2)}, u32[]{:S(2)}) %collective-permute-start.8) | collective-permute-done | bytes 270368 | tf_op jit(solution)/shard_map/ppermute | solution.py:213
  61.4 11.8 %collective-permute-start.13 = (f32[512,128]{1,0:T(8,128)S(1)}, f32[512,128]{1,0:T(8,128)S(1)}, u32[]{:S(2)}, u32[]{:S(2)}) collective-permute-start(f32[512,128]{1,0:T(8,128)S(1)} %get-tuple-element.112), channel_id=1, source_target_pairs={{0,16},{1,17},{2,18},{3,19},{4,20},{5,21},{6,22},{7,23},{8,24},{9,... | collective-permute-start | bytes 786440 | tf_op jit(solution)/shard_map/ppermute | solution.py:213
  73.3 7.2 %collective-permute-done.11.refs_9_ = f32[512,128]{1,0:T(8,128)S(1)} collective-permute-done((f32[512,128]{1,0:T(8,128)S(1)}, f32[512,128]{1,0:T(8,128)S(1)}, u32[]{:S(2)}, u32[]{:S(2)}) %collective-permute-start.11) | collective-permute-done | bytes 262176 | tf_op jit(solution)/shard_map/ppermute | solution.py:213
  80.7 2.6 %collective-permute-start.12 = (f32[4,264,128]{2,1,0:T(8,128)S(1)}, f32[4,264,128]{2,1,0:T(8,128)S(1)}, u32[]{:S(2)}, u32[]{:S(2)}) collective-permute-start(f32[4,264,128]{2,1,0:T(8,128)S(1)} %get-tuple-element.144), channel_id=1, source_target_pairs={{0,4},{1,5},{2,6},{3,7},{4,0},{5,1},{6,2},{7,3},{8,12},{9,13},{10,... | collective-permute-start | bytes 1622024 | tf_op jit(solution)/shard_map/ppermute | solution.py:213
  86.3 3.2 %collective-permute-start.16 = (f32[1024,128]{1,0:T(8,128)S(1)}, f32[1024,128]{1,0:T(8,128)S(1)}, u32[]{:S(2)}, u32[]{:S(2)}) collective-permute-start(f32[1024,128]{1,0:T(8,128)S(1)} %collective-permute-done.6), channel_id=1, source_target_pairs={{0,16},{1,17},{2,18},{3,19},{4,20},{5,21},{6,22},{7,23},{8,24},{9,... | collective-permute-start | bytes 1572872 | tf_op jit(solution)/shard_map/ppermute | solution.py:213
  90.8 4.3 %query_part.1 = (f32[4,256,256]{2,1,0:T(8,128)S(1)}, f32[4,256,128]{2,1,0:T(8,128)S(1)}, f32[4,256,128]{2,1,0:T(8,128)S(1)}) custom-call(s32[1]{0:T(128)S(6)} %xor.23.first, f32[256,1024]{1,0:T(8,128)S(1)} %copy-done.5, f32[8,128,128]{2,1,0:T(8,128)S(1)} %copy-done.8, f32[256,1024]{1,0:T(8,128)S(1)} %copy-done.2, f32[4,256,256]{2,1,0:T(8,128)S(1)} %copy-done.6), custom_call_target="tpu_custom_call" | custom-call | flops 1409286144 | bytes 4194304 | tf_op jit(solution)/shard_map/query_part/pallas_call | solution.py:275
  95.1 11.6 %collective-permute-done.14.refs_0_.refs_1_ = f32[256,512]{1,0:T(8,128)S(1)} collective-permute-done((f32[256,512]{1,0:T(8,128)S(1)}, f32[256,512]{1,0:T(8,128)S(1)}, u32[]{:S(2)}, u32[]{:S(2)}) %collective-permute-start.14) | collective-permute-done | bytes 524320 | tf_op jit(solution)/shard_map/ppermute | solution.py:213
  108.1 3.1 %collective-permute-done.16.refs_6_.refs_13_ = f32[1024,128]{1,0:T(8,128)S(1)} collective-permute-done((f32[1024,128]{1,0:T(8,128)S(1)}, f32[1024,128]{1,0:T(8,128)S(1)}, u32[]{:S(2)}, u32[]{:S(2)}) %collective-permute-start.16) | collective-permute-done | bytes 524320 | tf_op jit(solution)/shard_map/ppermute | solution.py:213
  111.7 2.7 %collective-permute-start.20 = (f32[1024,128]{1,0:T(8,128)S(1)}, f32[1024,128]{1,0:T(8,128)S(1)}, u32[]{:S(2)}, u32[]{:S(2)}) collective-permute-start(f32[1024,128]{1,0:T(8,128)S(1)} %collective-permute-done.7), channel_id=1, source_target_pairs={{0,16},{1,17},{2,18},{3,19},{4,20},{5,21},{6,22},{7,23},{8,24},{9,... | collective-permute-start | bytes 1572872 | tf_op jit(solution)/shard_map/ppermute | solution.py:213
  117.8 13.2 %collective-permute-done.21.refs_17_ = f32[512,128]{1,0:T(8,128)S(1)} collective-permute-done((f32[512,128]{1,0:T(8,128)S(1)}, f32[512,128]{1,0:T(8,128)S(1)}, u32[]{:S(2)}, u32[]{:S(2)}) %collective-permute-start.21) | collective-permute-done | bytes 262176 | tf_op jit(solution)/shard_map/ppermute | solution.py:213
  138.0 3.5 %project.4.refs_10_ = f32[512,1024]{1,0:T(8,128)S(1)} custom-call(f32[256,512]{1,0:T(8,128)S(1)} %mix.2.refs_0_, f32[256,512]{1,0:T(8,128)S(1)} %collective-permute-done.14.refs_0_.refs_1_, f32[256,512]{1,0:T(8,128)S(1)} %collective-permute-done.15.refs_2_, f32[512,512]{1,0:T(8,128)S(1)} %collective-permute-done.19.refs_3_.refs_0_.refs_4_, ...), custom_call_target="tpu_custom_call" | custom-call | flops 2818572288 | bytes 5767168 | tf_op jit(solution)/shard_map/project/pallas_call | solution.py:463
  143.4 2.7 %collective-permute-done.23.refs_1_.refs_5_ = f32[256,512]{1,0:T(8,128)S(1)} collective-permute-done((f32[256,512]{1,0:T(8,128)S(1)}, f32[256,512]{1,0:T(8,128)S(1)}, u32[]{:S(2)}, u32[]{:S(2)}) %collective-permute-start.23) | collective-permute-done | bytes 524320 | tf_op jit(solution)/shard_map/ppermute | solution.py:213
  152.9 2.8 %collective-permute-start.27 = (f32[256,256]{1,0:T(8,128)S(1)}, f32[256,256]{1,0:T(8,128)S(1)}, u32[]{:S(2)}, u32[]{:S(2)}) collective-permute-start(f32[256,256]{1,0:T(8,128)S(1)} %get-tuple-element.140), channel_id=1, source_target_pairs={{0,2},{1,0},{2,10},{3,8},{4,6},{5,4},{6,14},{7,12},{8,3},{9,1},{10... | collective-permute-start | bytes 786440 | tf_op jit(solution)/shard_map/ppermute | solution.py:514
  156.7 3.4 %collective-permute-start.29 = (f32[256,256]{1,0:T(8,128)S(1)}, f32[256,256]{1,0:T(8,128)S(1)}, u32[]{:S(2)}, u32[]{:S(2)}) collective-permute-start(f32[256,256]{1,0:T(8,128)S(1)} %get-tuple-element.142), channel_id=1, source_target_pairs={{0,10},{1,8},{2,2},{3,0},{4,14},{5,12},{6,6},{7,4},{8,11},{9,9},{1... | collective-permute-start | bytes 786440 | tf_op jit(solution)/shard_map/ppermute | solution.py:514
  160.1 6.6 %collective-permute-done.27.refs_1_ = f32[256,256]{1,0:T(8,128)S(1)} collective-permute-done((f32[256,256]{1,0:T(8,128)S(1)}, f32[256,256]{1,0:T(8,128)S(1)}, u32[]{:S(2)}, u32[]{:S(2)}) %collective-permute-start.27) | collective-permute-done | bytes 262176 | tf_op jit(solution)/shard_map/ppermute | solution.py:514
  167.4 3.0 %collective-permute-done.29.refs_3_ = f32[256,256]{1,0:T(8,128)S(1)} collective-permute-done((f32[256,256]{1,0:T(8,128)S(1)}, f32[256,256]{1,0:T(8,128)S(1)}, u32[]{:S(2)}, u32[]{:S(2)}) %collective-permute-start.29) | collective-permute-done | bytes 262176 | tf_op jit(solution)/shard_map/ppermute | solution.py:514
  (79 shorter events, 40.7 us)
Async XLA Ops:
  4.1 17.9 %collective-permute-start = (f32[4,264,128]{2,1,0:T(8,128)}, f32[4,264,128]{2,1,0:T(8,128)}, u32[]{:S(2)}, u32[]{:S(2)}) collective-permute-start(f32[4,264,128]{2,1,0:T(8,128)} %get-tuple-element.76), channel_id=1, source_target_pairs={{0,4},{1,5},{2,6},{3,7},{4,0},{5,1},{6,2},{7,3},{8,12},{9,13},{10,... | collective-permute-start | bytes 1622024 | tf_op jit(solution)/shard_map/ppermute | solution.py:213
  7.6 14.3 %collective-permute-start.1 = (f32[512,128]{1,0:T(8,128)S(1)}, f32[512,128]{1,0:T(8,128)S(1)}, u32[]{:S(2)}, u32[]{:S(2)}) collective-permute-start(f32[512,128]{1,0:T(8,128)S(1)} %arrange.2), channel_id=1, source_target_pairs={{0,16},{1,17},{2,18},{3,19},{4,20},{5,21},{6,22},{7,23},{8,24},{9,... | collective-permute-start | bytes 786440 | tf_op jit(solution)/shard_map/ppermute | solution.py:213
  22.0 25.0 %collective-permute-start.3 = (f32[1024,128]{1,0:T(8,128)S(1)}, f32[1024,128]{1,0:T(8,128)S(1)}, u32[]{:S(2)}, u32[]{:S(2)}) collective-permute-start(f32[1024,128]{1,0:T(8,128)S(1)} %get-tuple-element.88), channel_id=1, source_target_pairs={{0,16},{1,17},{2,18},{3,19},{4,20},{5,21},{6,22},{7,23},{8,24},{9,... | collective-permute-start | bytes 1572872 | tf_op jit(solution)/shard_map/ppermute | solution.py:213
  22.4 27.5 %collective-permute-start.4 = (f32[2048,128]{1,0:T(8,128)S(1)}, f32[2048,128]{1,0:T(8,128)S(1)}, u32[]{:S(2)}, u32[]{:S(2)}) collective-permute-start(f32[2048,128]{1,0:T(8,128)S(1)} %get-tuple-element.89.refs_7_.refs_14_.refs_6_.refs_2_), channel_id=1, source_target_pairs={{0,4},{1,5},{2,6},{3,7},{4,0},{5,1},{6,2},{7,3},{8,12},{9,13},{10,... | collective-permute-start | bytes 3145736 | tf_op jit(solution)/shard_map/ppermute | solution.py:213
  23.9 26.0 %collective-permute-start.5 = (f32[2048,128]{1,0:T(8,128)S(1)}, f32[2048,128]{1,0:T(8,128)S(1)}, u32[]{:S(2)}, u32[]{:S(2)}) collective-permute-start(f32[2048,128]{1,0:T(8,128)S(1)} %get-tuple-element.90), channel_id=1, source_target_pairs={{0,1},{1,0},{2,3},{3,2},{4,5},{5,4},{6,7},{7,6},{8,9},{9,8},{10,11... | collective-permute-start | bytes 3145736 | tf_op jit(solution)/shard_map/ppermute | solution.py:213
  25.1 24.9 %collective-permute-start.2 = (f32[4,264,128]{2,1,0:T(8,128)S(1)}, f32[4,264,128]{2,1,0:T(8,128)S(1)}, u32[]{:S(2)}, u32[]{:S(2)}) collective-permute-start(f32[4,264,128]{2,1,0:T(8,128)S(1)} %add.19), channel_id=1, source_target_pairs={{0,8},{1,9},{2,10},{3,11},{4,12},{5,13},{6,14},{7,15},{8,0},{9,1},... | collective-permute-start | bytes 1622024 | tf_op jit(solution)/shard_map/ppermute | solution.py:213
  27.8 19.3 %collective-permute-start.6 = (f32[1024,128]{1,0:T(8,128)S(1)}, f32[1024,128]{1,0:T(8,128)S(1)}, u32[]{:S(2)}, u32[]{:S(2)}) collective-permute-start(f32[1024,128]{1,0:T(8,128)S(1)} %get-tuple-element.91), channel_id=1, source_target_pairs={{0,1},{1,0},{2,3},{3,2},{4,5},{5,4},{6,7},{7,6},{8,9},{9,8},{10,11... | collective-permute-start | bytes 1572872 | tf_op jit(solution)/shard_map/ppermute | solution.py:213
  49.9 30.6 %collective-permute-start.10 = (f32[2048,128]{1,0:T(8,128)S(1)}, f32[2048,128]{1,0:T(8,128)S(1)}, u32[]{:S(2)}, u32[]{:S(2)}) collective-permute-start(f32[2048,128]{1,0:T(8,128)S(1)} %collective-permute-done.5.refs_4_.refs_11_.refs_2_.refs_6_), channel_id=1, source_target_pairs={{0,4},{1,5},{2,6},{3,7},{4,0},{5,1},{6,2},{7,3},{8,12},{9,13},{10,... | collective-permute-start | bytes 3145736 | tf_op jit(solution)/shard_map/ppermute | solution.py:213
  59.9 13.3 %collective-permute-start.9 = (f32[2,264,128]{2,1,0:T(8,128)S(1)}, f32[2,264,128]{2,1,0:T(8,128)S(1)}, u32[]{:S(2)}, u32[]{:S(2)}) collective-permute-start(f32[2,264,128]{2,1,0:T(8,128)S(1)} %collective-permute-done.8), channel_id=1, source_target_pairs={{16,24},{17,25},{18,26},{19,27},{20,28},{21,29},{22,30},{23,31},{2... | collective-permute-start | bytes 811016 | tf_op jit(solution)/shard_map/ppermute | solution.py:213
  60.8 19.7 %collective-permute-start.11 = (f32[512,128]{1,0:T(8,128)S(1)}, f32[512,128]{1,0:T(8,128)S(1)}, u32[]{:S(2)}, u32[]{:S(2)}) collective-permute-start(f32[512,128]{1,0:T(8,128)S(1)} %collective-permute-done.1.refs_9_), channel_id=1, source_target_pairs={{0,4},{1,5},{2,6},{3,7},{4,0},{5,1},{6,2},{7,3},{8,12},{9,13},{10,... | collective-permute-start | bytes 786440 | tf_op jit(solution)/shard_map/ppermute | solution.py:213
  61.4 23.4 %collective-permute-start.13 = (f32[512,128]{1,0:T(8,128)S(1)}, f32[512,128]{1,0:T(8,128)S(1)}, u32[]{:S(2)}, u32[]{:S(2)}) collective-permute-start(f32[512,128]{1,0:T(8,128)S(1)} %get-tuple-element.112), channel_id=1, source_target_pairs={{0,16},{1,17},{2,18},{3,19},{4,20},{5,21},{6,22},{7,23},{8,24},{9,... | collective-permute-start | bytes 786440 | tf_op jit(solution)/shard_map/ppermute | solution.py:213
  80.7 26.0 %collective-permute-start.12 = (f32[4,264,128]{2,1,0:T(8,128)S(1)}, f32[4,264,128]{2,1,0:T(8,128)S(1)}, u32[]{:S(2)}, u32[]{:S(2)}) collective-permute-start(f32[4,264,128]{2,1,0:T(8,128)S(1)} %get-tuple-element.144), channel_id=1, source_target_pairs={{0,4},{1,5},{2,6},{3,7},{4,0},{5,1},{6,2},{7,3},{8,12},{9,13},{10,... | collective-permute-start | bytes 1622024 | tf_op jit(solution)/shard_map/ppermute | solution.py:213
  84.8 21.9 %collective-permute-start.14 = (f32[256,512]{1,0:T(8,128)S(1)}, f32[256,512]{1,0:T(8,128)S(1)}, u32[]{:S(2)}, u32[]{:S(2)}) collective-permute-start(f32[256,512]{1,0:T(8,128)S(1)} %mix.2.refs_0_), channel_id=1, source_target_pairs={{0,8},{1,9},{2,10},{3,11},{4,12},{5,13},{6,14},{7,15},{8,0},{9,1},... | collective-permute-start | bytes 1572872 | tf_op jit(solution)/shard_map/ppermute | solution.py:213
  84.8 23.3 %collective-permute-start.15 = (f32[256,512]{1,0:T(8,128)S(1)}, f32[256,512]{1,0:T(8,128)S(1)}, u32[]{:S(2)}, u32[]{:S(2)}) collective-permute-start(f32[256,512]{1,0:T(8,128)S(1)} %mix.2.refs_0_), channel_id=1, source_target_pairs={{0,2},{1,3},{2,0},{3,1},{4,6},{5,7},{6,4},{7,5},{8,10},{9,11},{10,... | collective-permute-start | bytes 1572872 | tf_op jit(solution)/shard_map/ppermute | solution.py:213
  86.3 24.9 %collective-permute-start.16 = (f32[1024,128]{1,0:T(8,128)S(1)}, f32[1024,128]{1,0:T(8,128)S(1)}, u32[]{:S(2)}, u32[]{:S(2)}) collective-permute-start(f32[1024,128]{1,0:T(8,128)S(1)} %collective-permute-done.6), channel_id=1, source_target_pairs={{0,16},{1,17},{2,18},{3,19},{4,20},{5,21},{6,22},{7,23},{8,24},{9,... | collective-permute-start | bytes 1572872 | tf_op jit(solution)/shard_map/ppermute | solution.py:213
  89.6 21.7 %collective-permute-start.17 = (f32[1024,128]{1,0:T(8,128)S(1)}, f32[1024,128]{1,0:T(8,128)S(1)}, u32[]{:S(2)}, u32[]{:S(2)}) collective-permute-start(f32[1024,128]{1,0:T(8,128)S(1)} %collective-permute-done.3.refs_16_.refs_8_), channel_id=1, source_target_pairs={{0,4},{1,5},{2,6},{3,7},{4,0},{5,1},{6,2},{7,3},{8,12},{9,13},{10,... | collective-permute-start | bytes 1572872 | tf_op jit(solution)/shard_map/ppermute | solution.py:213
  111.2 24.0 %collective-permute-start.19 = (f32[512,512]{1,0:T(8,128)S(1)}, f32[512,512]{1,0:T(8,128)S(1)}, u32[]{:S(2)}, u32[]{:S(2)}) collective-permute-start(f32[512,512]{1,0:T(8,128)S(1)} %get-tuple-element.121), channel_id=1, source_target_pairs={{0,2},{1,3},{2,0},{3,1},{4,6},{5,7},{6,4},{7,5},{8,10},{9,11},{10,... | collective-permute-start | bytes 3145736 | tf_op jit(solution)/shard_map/ppermute | solution.py:213
  111.7 21.8 %collective-permute-start.18 = (f32[256,512]{1,0:T(8,128)S(1)}, f32[256,512]{1,0:T(8,128)S(1)}, u32[]{:S(2)}, u32[]{:S(2)}) collective-permute-start(f32[256,512]{1,0:T(8,128)S(1)} %get-tuple-element.120.refs_0_), channel_id=1, source_target_pairs={{0,8},{1,9},{2,10},{3,11},{4,12},{5,13},{6,14},{7,15},{8,0},{9,1},... | collective-permute-start | bytes 1572872 | tf_op jit(solution)/shard_map/ppermute | solution.py:213
  111.7 23.5 %collective-permute-start.20 = (f32[1024,128]{1,0:T(8,128)S(1)}, f32[1024,128]{1,0:T(8,128)S(1)}, u32[]{:S(2)}, u32[]{:S(2)}) collective-permute-start(f32[1024,128]{1,0:T(8,128)S(1)} %collective-permute-done.7), channel_id=1, source_target_pairs={{0,16},{1,17},{2,18},{3,19},{4,20},{5,21},{6,22},{7,23},{8,24},{9,... | collective-permute-start | bytes 1572872 | tf_op jit(solution)/shard_map/ppermute | solution.py:213
  114.4 20.8 %collective-permute-start.22 = (f32[1024,128]{1,0:T(8,128)S(1)}, f32[1024,128]{1,0:T(8,128)S(1)}, u32[]{:S(2)}, u32[]{:S(2)}) collective-permute-start(f32[1024,128]{1,0:T(8,128)S(1)} %collective-permute-done.16.refs_6_.refs_13_), channel_id=1, source_target_pairs={{0,4},{1,5},{2,6},{3,7},{4,0},{5,1},{6,2},{7,3},{8,12},{9,13},{10,... | collective-permute-start | bytes 1572872 | tf_op jit(solution)/shard_map/ppermute | solution.py:213
  115.9 15.1 %collective-permute-start.21 = (f32[512,128]{1,0:T(8,128)S(1)}, f32[512,128]{1,0:T(8,128)S(1)}, u32[]{:S(2)}, u32[]{:S(2)}) collective-permute-start(f32[512,128]{1,0:T(8,128)S(1)} %collective-permute-done.13.refs_4_), channel_id=1, source_target_pairs={{0,4},{1,5},{2,6},{3,7},{4,0},{5,1},{6,2},{7,3},{8,12},{9,13},{10,... | collective-permute-start | bytes 786440 | tf_op jit(solution)/shard_map/ppermute | solution.py:213
  152.9 13.9 %collective-permute-start.27 = (f32[256,256]{1,0:T(8,128)S(1)}, f32[256,256]{1,0:T(8,128)S(1)}, u32[]{:S(2)}, u32[]{:S(2)}) collective-permute-start(f32[256,256]{1,0:T(8,128)S(1)} %get-tuple-element.140), channel_id=1, source_target_pairs={{0,2},{1,0},{2,10},{3,8},{4,6},{5,4},{6,14},{7,12},{8,3},{9,1},{10... | collective-permute-start | bytes 786440 | tf_op jit(solution)/shard_map/ppermute | solution.py:514
  155.7 11.7 %collective-permute-start.28 = (f32[256,256]{1,0:T(8,128)S(1)}, f32[256,256]{1,0:T(8,128)S(1)}, u32[]{:S(2)}, u32[]{:S(2)}) collective-permute-start(f32[256,256]{1,0:T(8,128)S(1)} %get-tuple-element.141), channel_id=1, source_target_pairs={{0,8},{1,10},{2,0},{3,2},{4,12},{5,14},{6,4},{7,6},{8,9},{9,11},{1... | collective-permute-start | bytes 786440 | tf_op jit(solution)/shard_map/ppermute | solution.py:514
  156.7 13.6 %collective-permute-start.29 = (f32[256,256]{1,0:T(8,128)S(1)}, f32[256,256]{1,0:T(8,128)S(1)}, u32[]{:S(2)}, u32[]{:S(2)}) collective-permute-start(f32[256,256]{1,0:T(8,128)S(1)} %get-tuple-element.142), channel_id=1, source_target_pairs={{0,10},{1,8},{2,2},{3,0},{4,14},{5,12},{6,6},{7,4},{8,11},{9,9},{1... | collective-permute-start | bytes 786440 | tf_op jit(solution)/shard_map/ppermute | solution.py:514
  (17 other events, 132.8 us)

commit v6 on v5

--- a/solution.py
+++ b/solution.py
@@ -396,7 +396,6 @@
         (total, parts, far_2, kept_near, taken, taken_1, taken_2, far_1)
     )
     taken_near = swap(taken, near)
-    both_1 = swap(far_1, near)
     second = flags[PAIR]
     sent = sum(jnp.where(second, x[half // 2 :], x[: half // 2]) for x in (total, *parts[-1:]))
     got = swap(sent, bit, keep=lambda i: not i & bit)
@@ -404,9 +403,7 @@
     met = swap(got, PAIR, keep=lambda i: i & bit)
     far_3 = swap(kept_3, far)
     got = jnp.concatenate([jnp.where(second, met, got), jnp.where(second, got, met)])
-    got, taken_near, both_1, taken_1, far_2, other_feat = together(
-        (got, taken_near, both_1, taken_1, far_2, other_feat)
-    )
+    got, taken_near, taken_1, far_2, other_feat = together((got, taken_near, taken_1, far_2, other_feat))
     before = got
     for b, part_sum in enumerate(parts):
         before = before + jnp.where(flags[2 << b], part_sum, 0.0)
@@ -426,16 +423,17 @@
     far_4 = swap(taken_1, far)
     both_2 = swap(far_2, near)
     other_mixed, both = mix(*query_part(other, other_feat), other_prior, met)
-    other_mixed, both, across, far_3, far_4, both_2, taken_2 = together(
-        (other_mixed, both, across, far_3, far_4, both_2, taken_2)
+    outer = jnp.concatenate([far_1, far_3])
+    other_mixed, both, across, outer, far_4, both_2, taken_2 = together(
+        (other_mixed, both, across, outer, far_4, both_2, taken_2)
     )
     other_met = swap(other_mixed, PAIR)
     both = swap(both, 0, head_bits[0])
     far_5 = swap(taken_2, far)
-    both_3 = swap(far_3, near)
+    both_1 = swap(outer, near)
     both_4 = swap(far_4, near)
-    other_met, both, far_5, both_3, both_4, send_here, place_here = together(
-        (other_met, both, far_5, both_3, both_4, send_here, place_here)
+    other_met, both, far_5, both_1, both_4, send_here, place_here = together(
+        (other_met, both, far_5, both_1, both_4, send_here, place_here)
     )
     both_5 = swap(far_5, near)
     last = swap(other_met, 0, head_bits[0])
@@ -483,7 +481,7 @@
         strip([(kept, 0, 4)]),
         strip([(kept_near, 0, 4)], True),
         strip([(far_1, 0, 1), (far_2, 0, 2), (far_3, 0, 1)]),
-        strip([(both_1, 0, 1), (both_2, 0, 2), (both_3, 0, 1)], True),
+        strip([(both_1, 0, 1), (both_2, 0, 2), (both_1, 1, 2)], True),
     ]
     pieces = own_pieces + other_pieces(last)
     product = project(pieces, theirs + mine, [(0, 0, 3), (0, 4, 8), (1, 0, 3), (1, 4, 8)])
@@ -517,10 +515,12 @@
             functools.partial(assemble_kernel, size),
             grid_spec=pltpu.PrefetchScalarGridSpec(
                 num_scalar_prefetch=1,
-                grid=(1,),
-                in_specs=[pl.BlockSpec(x.shape, lambda i, place: (0, 0)) for x in (*arrived, residual)],
-                out_specs=pl.BlockSpec(residual.shape, lambda i, place: (0, 0)),
-                scratch_shapes=[pltpu.VMEM((ctx, rows, strip_width), jnp.float32)],
+                grid=(blocks,),
+                in_specs=[
+                    pl.BlockSpec((rows // blocks, x.shape[1]), lambda i, place: (i, 0)) for x in (*arrived, residual)
+                ],
+                out_specs=pl.BlockSpec((rows // blocks, residual.shape[1]), lambda i, place: (i, 0)),
+                scratch_shapes=[pltpu.VMEM((ctx, rows // blocks, strip_width), jnp.float32)],
             ),
             out_shape=of(*residual.shape),
             compiler_params=params(12),

time: 173 us -> 174 us (level)
  waiting for transfers between devices: 85.6 us -> 88.9 us
    ppermute x26 -> x25, waiting for transfers between devices: 75.3 us -> 78.1 us  [swap(): return lax.ppermute(x, AXES, pairs)]
    ppermute x26 -> x25, starting transfers between devices: 45 us -> 43.6 us  [swap(): return lax.ppermute(x, AXES, pairs)]
  transfers between devices with their start and end apart: 30 -> 29, of which waited for: 18 -> 18; matrix products, arithmetic and copies ran while one was open for 2% -> 2% of each run, Pallas kernels for 12% -> 12%
where the time goes in v6:
time: 174 us
  waiting for transfers between devices  88.9 us (51%)
  starting transfers between devices  51.4 us (30%)
  Pallas kernels  29.4 us (17%)
  local copies, waits for them, and re-layouts  2.45 us (1%)
    ppermute x25, waiting for transfers between devices, swap(): return lax.ppermute(x, AXES, pairs)  78.1 us
    ppermute x25, starting transfers between devices, swap(): return lax.ppermute(x, AXES, pairs)  43.6 us
    ppermute x4, waiting for transfers between devices, body(): lax.ppermute(part, AXES, perm)  10.8 us
    pallas_call x4, Pallas kernels, project(): pl.pallas_call(functools.partial(project_kernel, terms, len(used)), grid=...  8.27 us
    ppermute x4, starting transfers between devices, body(): lax.ppermute(part, AXES, perm)  7.78 us
    pallas_call x1, Pallas kernels, own_part(): pl.pallas_call(own_kernel, grid_spec=pltpu.PrefetchScalarGridSpec(num_sca...  6.27 us
    pallas_call x1, Pallas kernels, query_part(): pl.pallas_call(query_kernel, grid_spec=pltpu.PrefetchScalarGridSpec(num_s...  4.29 us
    pallas_call x1, Pallas kernels, key_part(): pl.pallas_call(key_kernel, grid_spec=pltpu.PrefetchScalarGridSpec(num_sca...  4.03 us
  transfers between devices with their start and end apart: 29, of which 18 were waited for; matrix products, arithmetic and copies ran while one was open for 2% of the time, Pallas kernels for 12%

profile of v6, /device:TPU:0, one launch (start us, length us, event | category | flops | bytes accessed | tf_op | source)
XLA Modules:
  0.0 173.8 jit_solution(12548214848305199544)
XLA Ops:
  0.0 4.0 %key_part.1 = (f32[4,264,128]{2,1,0:T(8,128)}, f32[4,256,256]{2,1,0:T(8,128)}) custom-call(s32[1]{0:T(128)S(6)} %xor.23.first, f32[256,1024]{1,0:T(8,128)} %k_ref.3, f32[8,128,128]{2,1,0:T(8,128)} %k_map_ref.1, f32[256,1024]{1,0:T(8,128)} %v_ref.5), custom_call_target="tpu_custom_call" | custom-call | flops 603979776 | bytes 3145728 | tf_op jit(solution)/shard_map/key_part/pallas_call | solution.py:231
  4.0 3.0 %collective-permute-start = (f32[4,264,128]{2,1,0:T(8,128)}, f32[4,264,128]{2,1,0:T(8,128)}, u32[]{:S(2)}, u32[]{:S(2)}) collective-permute-start(f32[4,264,128]{2,1,0:T(8,128)} %get-tuple-element.75), channel_id=1, source_target_pairs={{0,4},{1,5},{2,6},{3,7},{4,0},{5,1},{6,2},{7,3},{8,12},{9,13},{10,... | collective-permute-start | bytes 1622024 | tf_op jit(solution)/shard_map/ppermute | solution.py:213
  7.6 2.7 %collective-permute-start.1 = (f32[512,128]{1,0:T(8,128)S(1)}, f32[512,128]{1,0:T(8,128)S(1)}, u32[]{:S(2)}, u32[]{:S(2)}) collective-permute-start(f32[512,128]{1,0:T(8,128)S(1)} %arrange.2), channel_id=1, source_target_pairs={{0,16},{1,17},{2,18},{3,19},{4,20},{5,21},{6,22},{7,23},{8,24},{9,... | collective-permute-start | bytes 786440 | tf_op jit(solution)/shard_map/ppermute | solution.py:213
  11.3 6.3 %own_part.1 = (f32[4,264,128]{2,1,0:T(8,128)S(1)}, f32[4,256,256]{2,1,0:T(8,128)S(1)}, f32[4,256,128]{2,1,0:T(8,128)S(1)}, f32[4,256,128]{2,1,0:T(8,128)S(1)}) custom-call(s32[1]{0:T(128)} %bitcast.first, f32[256,1024]{1,0:T(8,128)S(1)} %copy-done.1, f32[8,128,128]{2,1,0:T(8,128)S(1)} %copy-done.4, f32[256,1024]{1,0:T(8,128)S(1)} %copy-done.5, ...), custom_call_target="tpu_custom_call" | custom-call | flops 2013265920 | bytes 5767168 | tf_op jit(solution)/shard_map/own_part/pallas_call | solution.py:255
  18.6 3.3 %collective-permute-done.1.refs_9_ = f32[512,128]{1,0:T(8,128)S(1)} collective-permute-done((f32[512,128]{1,0:T(8,128)S(1)}, f32[512,128]{1,0:T(8,128)S(1)}, u32[]{:S(2)}, u32[]{:S(2)}) %collective-permute-start.1) | collective-permute-done | bytes 262176 | tf_op jit(solution)/shard_map/ppermute | solution.py:213
  25.0 2.7 %collective-permute-start.2 = (f32[4,264,128]{2,1,0:T(8,128)S(1)}, f32[4,264,128]{2,1,0:T(8,128)S(1)}, u32[]{:S(2)}, u32[]{:S(2)}) collective-permute-start(f32[4,264,128]{2,1,0:T(8,128)S(1)} %add.19), channel_id=1, source_target_pairs={{0,8},{1,9},{2,10},{3,11},{4,12},{5,13},{6,14},{7,15},{8,0},{9,1},... | collective-permute-start | bytes 1622024 | tf_op jit(solution)/shard_map/ppermute | solution.py:213
  28.0 19.0 %collective-permute-done.3.refs_16_.refs_8_ = f32[1024,128]{1,0:T(8,128)S(1)} collective-permute-done((f32[1024,128]{1,0:T(8,128)S(1)}, f32[1024,128]{1,0:T(8,128)S(1)}, u32[]{:S(2)}, u32[]{:S(2)}) %collective-permute-start.3) | collective-permute-done | bytes 524320 | tf_op jit(solution)/shard_map/ppermute | solution.py:213
  51.5 3.1 %collective-permute-start.8 = (f32[2,264,128]{2,1,0:T(8,128)S(1)}, f32[2,264,128]{2,1,0:T(8,128)S(1)}, u32[]{:S(2)}, u32[]{:S(2)}) collective-permute-start(f32[2,264,128]{2,1,0:T(8,128)S(1)} %select_add_fusion.3), channel_id=1, source_target_pairs={{0,16},{1,17},{2,18},{3,19},{4,20},{5,21},{6,22},{7,23},{8,24},{9,... | collective-permute-start | bytes 811016 | tf_op jit(solution)/shard_map/ppermute | solution.py:213
  54.6 5.4 %collective-permute-done.8 = f32[2,264,128]{2,1,0:T(8,128)S(1)} collective-permute-done((f32[2,264,128]{2,1,0:T(8,128)S(1)}, f32[2,264,128]{2,1,0:T(8,128)S(1)}, u32[]{:S(2)}, u32[]{:S(2)}) %collective-permute-start.8) | collective-permute-done | bytes 270368 | tf_op jit(solution)/shard_map/ppermute | solution.py:213
  60.8 11.9 %collective-permute-start.12 = (f32[512,128]{1,0:T(8,128)S(1)}, f32[512,128]{1,0:T(8,128)S(1)}, u32[]{:S(2)}, u32[]{:S(2)}) collective-permute-start(f32[512,128]{1,0:T(8,128)S(1)} %get-tuple-element.110), channel_id=1, source_target_pairs={{0,16},{1,17},{2,18},{3,19},{4,20},{5,21},{6,22},{7,23},{8,24},{9,... | collective-permute-start | bytes 786440 | tf_op jit(solution)/shard_map/ppermute | solution.py:213
  75.1 2.6 %collective-permute-start.11 = (f32[4,264,128]{2,1,0:T(8,128)S(1)}, f32[4,264,128]{2,1,0:T(8,128)S(1)}, u32[]{:S(2)}, u32[]{:S(2)}) collective-permute-start(f32[4,264,128]{2,1,0:T(8,128)S(1)} %get-tuple-element.142), channel_id=1, source_target_pairs={{0,4},{1,5},{2,6},{3,7},{4,0},{5,1},{6,2},{7,3},{8,12},{9,13},{10,... | collective-permute-start | bytes 1622024 | tf_op jit(solution)/shard_map/ppermute | solution.py:213
  78.8 5.7 %collective-permute-done.12.refs_4_ = f32[512,128]{1,0:T(8,128)S(1)} collective-permute-done((f32[512,128]{1,0:T(8,128)S(1)}, f32[512,128]{1,0:T(8,128)S(1)}, u32[]{:S(2)}, u32[]{:S(2)}) %collective-permute-start.12) | collective-permute-done | bytes 262176 | tf_op jit(solution)/shard_map/ppermute | solution.py:213
  86.3 2.7 %collective-permute-start.15 = (f32[1024,128]{1,0:T(8,128)S(1)}, f32[1024,128]{1,0:T(8,128)S(1)}, u32[]{:S(2)}, u32[]{:S(2)}) collective-permute-start(f32[1024,128]{1,0:T(8,128)S(1)} %collective-permute-done.6), channel_id=1, source_target_pairs={{0,16},{1,17},{2,18},{3,19},{4,20},{5,21},{6,22},{7,23},{8,24},{9,... | collective-permute-start | bytes 1572872 | tf_op jit(solution)/shard_map/ppermute | solution.py:213
  89.6 4.3 %query_part.1 = (f32[4,256,256]{2,1,0:T(8,128)S(1)}, f32[4,256,128]{2,1,0:T(8,128)S(1)}, f32[4,256,128]{2,1,0:T(8,128)S(1)}) custom-call(s32[1]{0:T(128)S(6)} %xor.23.first, f32[256,1024]{1,0:T(8,128)S(1)} %copy-done.5, f32[8,128,128]{2,1,0:T(8,128)S(1)} %copy-done.8, f32[256,1024]{1,0:T(8,128)S(1)} %copy-done.2, f32[4,256,256]{2,1,0:T(8,128)S(1)} %copy-done.6), custom_call_target="tpu_custom_call" | custom-call | flops 1409286144 | bytes 4194304 | tf_op jit(solution)/shard_map/query_part/pallas_call | solution.py:275
  93.9 12.0 %collective-permute-done.13.refs_0_.refs_1_ = f32[256,512]{1,0:T(8,128)S(1)} collective-permute-done((f32[256,512]{1,0:T(8,128)S(1)}, f32[256,512]{1,0:T(8,128)S(1)}, u32[]{:S(2)}, u32[]{:S(2)}) %collective-permute-start.13) | collective-permute-done | bytes 524320 | tf_op jit(solution)/shard_map/ppermute | solution.py:213
  107.3 4.0 %collective-permute-done.15.refs_6_.refs_13_ = f32[1024,128]{1,0:T(8,128)S(1)} collective-permute-done((f32[1024,128]{1,0:T(8,128)S(1)}, f32[1024,128]{1,0:T(8,128)S(1)}, u32[]{:S(2)}, u32[]{:S(2)}) %collective-permute-start.15) | collective-permute-done | bytes 524320 | tf_op jit(solution)/shard_map/ppermute | solution.py:213
  111.8 2.6 %collective-permute-start.19 = (f32[1024,128]{1,0:T(8,128)S(1)}, f32[1024,128]{1,0:T(8,128)S(1)}, u32[]{:S(2)}, u32[]{:S(2)}) collective-permute-start(f32[1024,128]{1,0:T(8,128)S(1)} %collective-permute-done.7), channel_id=1, source_target_pairs={{0,16},{1,17},{2,18},{3,19},{4,20},{5,21},{6,22},{7,23},{8,24},{9,... | collective-permute-start | bytes 1572872 | tf_op jit(solution)/shard_map/ppermute | solution.py:213
  117.8 15.3 %collective-permute-done.17.refs_1_ = f32[256,512]{1,0:T(8,128)S(1)} collective-permute-done((f32[256,512]{1,0:T(8,128)S(1)}, f32[256,512]{1,0:T(8,128)S(1)}, u32[]{:S(2)}, u32[]{:S(2)}) %collective-permute-start.17) | collective-permute-done | bytes 524320 | tf_op jit(solution)/shard_map/ppermute | solution.py:213
  133.2 2.4 %collective-permute-done.19.refs_4_.refs_8_ = f32[1024,128]{1,0:T(8,128)S(1)} collective-permute-done((f32[1024,128]{1,0:T(8,128)S(1)}, f32[1024,128]{1,0:T(8,128)S(1)}, u32[]{:S(2)}, u32[]{:S(2)}) %collective-permute-start.19) | collective-permute-done | bytes 524320 | tf_op jit(solution)/shard_map/ppermute | solution.py:213
  136.7 2.4 %collective-permute-start.22 = (f32[256,512]{1,0:T(8,128)S(1)}, f32[256,512]{1,0:T(8,128)S(1)}, u32[]{:S(2)}, u32[]{:S(2)}) collective-permute-start(f32[256,512]{1,0:T(8,128)S(1)} %collective-permute-done.17.refs_1_), channel_id=1, source_target_pairs={{0,2},{1,3},{2,0},{3,1},{4,6},{5,7},{6,4},{7,5},{8,10},{9,11},{10,... | collective-permute-start | bytes 1572872 | tf_op jit(solution)/shard_map/ppermute | solution.py:213
  139.6 3.5 %project.4.refs_10_ = f32[512,1024]{1,0:T(8,128)S(1)} custom-call(f32[256,512]{1,0:T(8,128)S(1)} %mix.2.refs_0_, f32[256,512]{1,0:T(8,128)S(1)} %collective-permute-done.13.refs_0_.refs_1_, f32[256,512]{1,0:T(8,128)S(1)} %collective-permute-done.14.refs_2_, f32[512,512]{1,0:T(8,128)S(1)} %collective-permute-done.18.refs_3_.refs_0_.refs_4_, ...), custom_call_target="tpu_custom_call" | custom-call | flops 2818572288 | bytes 5767168 | tf_op jit(solution)/shard_map/project/pallas_call | solution.py:461
  154.2 3.1 %collective-permute-start.26 = (f32[256,256]{1,0:T(8,128)S(1)}, f32[256,256]{1,0:T(8,128)S(1)}, u32[]{:S(2)}, u32[]{:S(2)}) collective-permute-start(f32[256,256]{1,0:T(8,128)S(1)} %get-tuple-element.138), channel_id=1, source_target_pairs={{0,2},{1,0},{2,10},{3,8},{4,6},{5,4},{6,14},{7,12},{8,3},{9,1},{10... | collective-permute-start | bytes 786440 | tf_op jit(solution)/shard_map/ppermute | solution.py:512
  158.2 3.1 %collective-permute-start.28 = (f32[256,256]{1,0:T(8,128)S(1)}, f32[256,256]{1,0:T(8,128)S(1)}, u32[]{:S(2)}, u32[]{:S(2)}) collective-permute-start(f32[256,256]{1,0:T(8,128)S(1)} %get-tuple-element.140), channel_id=1, source_target_pairs={{0,10},{1,8},{2,2},{3,0},{4,14},{5,12},{6,6},{7,4},{8,11},{9,9},{1... | collective-permute-start | bytes 786440 | tf_op jit(solution)/shard_map/ppermute | solution.py:512
  161.4 6.4 %collective-permute-done.26.refs_1_ = f32[256,256]{1,0:T(8,128)S(1)} collective-permute-done((f32[256,256]{1,0:T(8,128)S(1)}, f32[256,256]{1,0:T(8,128)S(1)}, u32[]{:S(2)}, u32[]{:S(2)}) %collective-permute-start.26) | collective-permute-done | bytes 262176 | tf_op jit(solution)/shard_map/ppermute | solution.py:512
  (78 shorter events, 42.2 us)
Async XLA Ops:
  4.0 17.9 %collective-permute-start = (f32[4,264,128]{2,1,0:T(8,128)}, f32[4,264,128]{2,1,0:T(8,128)}, u32[]{:S(2)}, u32[]{:S(2)}) collective-permute-start(f32[4,264,128]{2,1,0:T(8,128)} %get-tuple-element.75), channel_id=1, source_target_pairs={{0,4},{1,5},{2,6},{3,7},{4,0},{5,1},{6,2},{7,3},{8,12},{9,13},{10,... | collective-permute-start | bytes 1622024 | tf_op jit(solution)/shard_map/ppermute | solution.py:213
  7.6 14.3 %collective-permute-start.1 = (f32[512,128]{1,0:T(8,128)S(1)}, f32[512,128]{1,0:T(8,128)S(1)}, u32[]{:S(2)}, u32[]{:S(2)}) collective-permute-start(f32[512,128]{1,0:T(8,128)S(1)} %arrange.2), channel_id=1, source_target_pairs={{0,16},{1,17},{2,18},{3,19},{4,20},{5,21},{6,22},{7,23},{8,24},{9,... | collective-permute-start | bytes 786440 | tf_op jit(solution)/shard_map/ppermute | solution.py:213
  22.0 25.0 %collective-permute-start.3 = (f32[1024,128]{1,0:T(8,128)S(1)}, f32[1024,128]{1,0:T(8,128)S(1)}, u32[]{:S(2)}, u32[]{:S(2)}) collective-permute-start(f32[1024,128]{1,0:T(8,128)S(1)} %get-tuple-element.87), channel_id=1, source_target_pairs={{0,16},{1,17},{2,18},{3,19},{4,20},{5,21},{6,22},{7,23},{8,24},{9,... | collective-permute-start | bytes 1572872 | tf_op jit(solution)/shard_map/ppermute | solution.py:213
  22.4 27.5 %collective-permute-start.4 = (f32[2048,128]{1,0:T(8,128)S(1)}, f32[2048,128]{1,0:T(8,128)S(1)}, u32[]{:S(2)}, u32[]{:S(2)}) collective-permute-start(f32[2048,128]{1,0:T(8,128)S(1)} %get-tuple-element.88.refs_7_.refs_14_.refs_6_.refs_2_), channel_id=1, source_target_pairs={{0,4},{1,5},{2,6},{3,7},{4,0},{5,1},{6,2},{7,3},{8,12},{9,13},{10,... | collective-permute-start | bytes 3145736 | tf_op jit(solution)/shard_map/ppermute | solution.py:213
  23.9 26.0 %collective-permute-start.5 = (f32[2048,128]{1,0:T(8,128)S(1)}, f32[2048,128]{1,0:T(8,128)S(1)}, u32[]{:S(2)}, u32[]{:S(2)}) collective-permute-start(f32[2048,128]{1,0:T(8,128)S(1)} %get-tuple-element.89), channel_id=1, source_target_pairs={{0,1},{1,0},{2,3},{3,2},{4,5},{5,4},{6,7},{7,6},{8,9},{9,8},{10,11... | collective-permute-start | bytes 3145736 | tf_op jit(solution)/shard_map/ppermute | solution.py:213
  25.0 24.9 %collective-permute-start.2 = (f32[4,264,128]{2,1,0:T(8,128)S(1)}, f32[4,264,128]{2,1,0:T(8,128)S(1)}, u32[]{:S(2)}, u32[]{:S(2)}) collective-permute-start(f32[4,264,128]{2,1,0:T(8,128)S(1)} %add.19), channel_id=1, source_target_pairs={{0,8},{1,9},{2,10},{3,11},{4,12},{5,13},{6,14},{7,15},{8,0},{9,1},... | collective-permute-start | bytes 1622024 | tf_op jit(solution)/shard_map/ppermute | solution.py:213
  27.8 19.3 %collective-permute-start.6 = (f32[1024,128]{1,0:T(8,128)S(1)}, f32[1024,128]{1,0:T(8,128)S(1)}, u32[]{:S(2)}, u32[]{:S(2)}) collective-permute-start(f32[1024,128]{1,0:T(8,128)S(1)} %get-tuple-element.90), channel_id=1, source_target_pairs={{0,1},{1,0},{2,3},{3,2},{4,5},{5,4},{6,7},{7,6},{8,9},{9,8},{10,11... | collective-permute-start | bytes 1572872 | tf_op jit(solution)/shard_map/ppermute | solution.py:213
  49.9 25.0 %collective-permute-start.10 = (f32[2048,128]{1,0:T(8,128)S(1)}, f32[2048,128]{1,0:T(8,128)S(1)}, u32[]{:S(2)}, u32[]{:S(2)}) collective-permute-start(f32[2048,128]{1,0:T(8,128)S(1)} %collective-permute-done.5.refs_4_.refs_11_.refs_2_.refs_6_), channel_id=1, source_target_pairs={{0,4},{1,5},{2,6},{3,7},{4,0},{5,1},{6,2},{7,3},{8,12},{9,13},{10,... | collective-permute-start | bytes 3145736 | tf_op jit(solution)/shard_map/ppermute | solution.py:213
  60.0 12.7 %collective-permute-start.9 = (f32[2,264,128]{2,1,0:T(8,128)S(1)}, f32[2,264,128]{2,1,0:T(8,128)S(1)}, u32[]{:S(2)}, u32[]{:S(2)}) collective-permute-start(f32[2,264,128]{2,1,0:T(8,128)S(1)} %collective-permute-done.8), channel_id=1, source_target_pairs={{16,24},{17,25},{18,26},{19,27},{20,28},{21,29},{22,30},{23,31},{2... | collective-permute-start | bytes 811016 | tf_op jit(solution)/shard_map/ppermute | solution.py:213
  60.8 23.7 %collective-permute-start.12 = (f32[512,128]{1,0:T(8,128)S(1)}, f32[512,128]{1,0:T(8,128)S(1)}, u32[]{:S(2)}, u32[]{:S(2)}) collective-permute-start(f32[512,128]{1,0:T(8,128)S(1)} %get-tuple-element.110), channel_id=1, source_target_pairs={{0,16},{1,17},{2,18},{3,19},{4,20},{5,21},{6,22},{7,23},{8,24},{9,... | collective-permute-start | bytes 786440 | tf_op jit(solution)/shard_map/ppermute | solution.py:213
  75.1 30.8 %collective-permute-start.11 = (f32[4,264,128]{2,1,0:T(8,128)S(1)}, f32[4,264,128]{2,1,0:T(8,128)S(1)}, u32[]{:S(2)}, u32[]{:S(2)}) collective-permute-start(f32[4,264,128]{2,1,0:T(8,128)S(1)} %get-tuple-element.142), channel_id=1, source_target_pairs={{0,4},{1,5},{2,6},{3,7},{4,0},{5,1},{6,2},{7,3},{8,12},{9,13},{10,... | collective-permute-start | bytes 1622024 | tf_op jit(solution)/shard_map/ppermute | solution.py:213
  84.5 21.4 %collective-permute-start.13 = (f32[256,512]{1,0:T(8,128)S(1)}, f32[256,512]{1,0:T(8,128)S(1)}, u32[]{:S(2)}, u32[]{:S(2)}) collective-permute-start(f32[256,512]{1,0:T(8,128)S(1)} %mix.2.refs_0_), channel_id=1, source_target_pairs={{0,8},{1,9},{2,10},{3,11},{4,12},{5,13},{6,14},{7,15},{8,0},{9,1},... | collective-permute-start | bytes 1572872 | tf_op jit(solution)/shard_map/ppermute | solution.py:213
  84.8 22.5 %collective-permute-start.14 = (f32[256,512]{1,0:T(8,128)S(1)}, f32[256,512]{1,0:T(8,128)S(1)}, u32[]{:S(2)}, u32[]{:S(2)}) collective-permute-start(f32[256,512]{1,0:T(8,128)S(1)} %mix.2.refs_0_), channel_id=1, source_target_pairs={{0,2},{1,3},{2,0},{3,1},{4,6},{5,7},{6,4},{7,5},{8,10},{9,11},{10,... | collective-permute-start | bytes 1572872 | tf_op jit(solution)/shard_map/ppermute | solution.py:213
  86.3 24.9 %collective-permute-start.15 = (f32[1024,128]{1,0:T(8,128)S(1)}, f32[1024,128]{1,0:T(8,128)S(1)}, u32[]{:S(2)}, u32[]{:S(2)}) collective-permute-start(f32[1024,128]{1,0:T(8,128)S(1)} %collective-permute-done.6), channel_id=1, source_target_pairs={{0,16},{1,17},{2,18},{3,19},{4,20},{5,21},{6,22},{7,23},{8,24},{9,... | collective-permute-start | bytes 1572872 | tf_op jit(solution)/shard_map/ppermute | solution.py:213
  89.0 22.3 %collective-permute-start.16 = (f32[1024,128]{1,0:T(8,128)S(1)}, f32[1024,128]{1,0:T(8,128)S(1)}, u32[]{:S(2)}, u32[]{:S(2)}) collective-permute-start(f32[1024,128]{1,0:T(8,128)S(1)} %collective-permute-done.3.refs_16_.refs_8_), channel_id=1, source_target_pairs={{0,4},{1,5},{2,6},{3,7},{4,0},{5,1},{6,2},{7,3},{8,12},{9,13},{10,... | collective-permute-start | bytes 1572872 | tf_op jit(solution)/shard_map/ppermute | solution.py:213
  111.3 25.4 %collective-permute-start.18 = (f32[512,512]{1,0:T(8,128)S(1)}, f32[512,512]{1,0:T(8,128)S(1)}, u32[]{:S(2)}, u32[]{:S(2)}) collective-permute-start(f32[512,512]{1,0:T(8,128)S(1)} %get-tuple-element.120), channel_id=1, source_target_pairs={{0,2},{1,3},{2,0},{3,1},{4,6},{5,7},{6,4},{7,5},{8,10},{9,11},{10,... | collective-permute-start | bytes 3145736 | tf_op jit(solution)/shard_map/ppermute | solution.py:213
  111.8 21.4 %collective-permute-start.17 = (f32[256,512]{1,0:T(8,128)S(1)}, f32[256,512]{1,0:T(8,128)S(1)}, u32[]{:S(2)}, u32[]{:S(2)}) collective-permute-start(f32[256,512]{1,0:T(8,128)S(1)} %get-tuple-element.119.refs_0_), channel_id=1, source_target_pairs={{0,8},{1,9},{2,10},{3,11},{4,12},{5,13},{6,14},{7,15},{8,0},{9,1},... | collective-permute-start | bytes 1572872 | tf_op jit(solution)/shard_map/ppermute | solution.py:213
  111.8 23.7 %collective-permute-start.19 = (f32[1024,128]{1,0:T(8,128)S(1)}, f32[1024,128]{1,0:T(8,128)S(1)}, u32[]{:S(2)}, u32[]{:S(2)}) collective-permute-start(f32[1024,128]{1,0:T(8,128)S(1)} %collective-permute-done.7), channel_id=1, source_target_pairs={{0,16},{1,17},{2,18},{3,19},{4,20},{5,21},{6,22},{7,23},{8,24},{9,... | collective-permute-start | bytes 1572872 | tf_op jit(solution)/shard_map/ppermute | solution.py:213
  114.4 21.1 %collective-permute-start.20 = (f32[1024,128]{1,0:T(8,128)S(1)}, f32[1024,128]{1,0:T(8,128)S(1)}, u32[]{:S(2)}, u32[]{:S(2)}) collective-permute-start(f32[1024,128]{1,0:T(8,128)S(1)} %pad_maximum_fusion.1), channel_id=1, source_target_pairs={{0,4},{1,5},{2,6},{3,7},{4,0},{5,1},{6,2},{7,3},{8,12},{9,13},{10,... | collective-permute-start | bytes 1572872 | tf_op jit(solution)/shard_map/ppermute | solution.py:213
  115.0 21.7 %collective-permute-start.21 = (f32[1024,128]{1,0:T(8,128)S(1)}, f32[1024,128]{1,0:T(8,128)S(1)}, u32[]{:S(2)}, u32[]{:S(2)}) collective-permute-start(f32[1024,128]{1,0:T(8,128)S(1)} %collective-permute-done.15.refs_6_.refs_13_), channel_id=1, source_target_pairs={{0,4},{1,5},{2,6},{3,7},{4,0},{5,1},{6,2},{7,3},{8,12},{9,13},{10,... | collective-permute-start | bytes 1572872 | tf_op jit(solution)/shard_map/ppermute | solution.py:213
  136.7 10.1 %collective-permute-start.22 = (f32[256,512]{1,0:T(8,128)S(1)}, f32[256,512]{1,0:T(8,128)S(1)}, u32[]{:S(2)}, u32[]{:S(2)}) collective-permute-start(f32[256,512]{1,0:T(8,128)S(1)} %collective-permute-done.17.refs_1_), channel_id=1, source_target_pairs={{0,2},{1,3},{2,0},{3,1},{4,6},{5,7},{6,4},{7,5},{8,10},{9,11},{10,... | collective-permute-start | bytes 1572872 | tf_op jit(solution)/shard_map/ppermute | solution.py:213
  154.2 13.5 %collective-permute-start.26 = (f32[256,256]{1,0:T(8,128)S(1)}, f32[256,256]{1,0:T(8,128)S(1)}, u32[]{:S(2)}, u32[]{:S(2)}) collective-permute-start(f32[256,256]{1,0:T(8,128)S(1)} %get-tuple-element.138), channel_id=1, source_target_pairs={{0,2},{1,0},{2,10},{3,8},{4,6},{5,4},{6,14},{7,12},{8,3},{9,1},{10... | collective-permute-start | bytes 786440 | tf_op jit(solution)/shard_map/ppermute | solution.py:512
  157.3 12.5 %collective-permute-start.27 = (f32[256,256]{1,0:T(8,128)S(1)}, f32[256,256]{1,0:T(8,128)S(1)}, u32[]{:S(2)}, u32[]{:S(2)}) collective-permute-start(f32[256,256]{1,0:T(8,128)S(1)} %get-tuple-element.139), channel_id=1, source_target_pairs={{0,8},{1,10},{2,0},{3,2},{4,12},{5,14},{6,4},{7,6},{8,9},{9,11},{1... | collective-permute-start | bytes 786440 | tf_op jit(solution)/shard_map/ppermute | solution.py:512
  158.2 13.9 %collective-permute-start.28 = (f32[256,256]{1,0:T(8,128)S(1)}, f32[256,256]{1,0:T(8,128)S(1)}, u32[]{:S(2)}, u32[]{:S(2)}) collective-permute-start(f32[256,256]{1,0:T(8,128)S(1)} %get-tuple-element.140), channel_id=1, source_target_pairs={{0,10},{1,8},{2,2},{3,0},{4,14},{5,12},{6,6},{7,4},{8,11},{9,9},{1... | collective-permute-start | bytes 786440 | tf_op jit(solution)/shard_map/ppermute | solution.py:512
  (16 other events, 125.8 us)

commit v7 on v5

--- a/solution.py
+++ b/solution.py
@@ -165,7 +165,12 @@
                     found[to] = d * len(groups) + g
             targets[c * heads + h] = found
     classes = {}
-    for device in sorted(targets):
+
+    def turn(device):
+        c, h = divmod(device, heads)
+        return c, h & 1, (h >> 1) ^ (h & 1)
+
+    for device in sorted(targets, key=turn):
         classes.setdefault(tuple(sorted(targets[device])), []).append(device)
     steps = 2 * len(groups)
     perms = [[] for _ in range(steps)]

time: 173 us -> 172 us (level)
  transfers between devices with their start and end apart: 30 -> 30, of which waited for: 18 -> 17; matrix products, arithmetic and copies ran while one was open for 2% -> 2% of each run, Pallas kernels for 12% -> 12%
where the time goes in v7:
time: 172 us; the launch traced here: 171 us
  waiting for transfers between devices  85.4 us (50%)
  starting transfers between devices  52.3 us (30%)
  Pallas kernels  29.5 us (17%)
  local copies, waits for them, and re-layouts  2.46 us (1%)
    ppermute x26, waiting for transfers between devices, swap(): return lax.ppermute(x, AXES, pairs)  75.3 us
    ppermute x26, starting transfers between devices, swap(): return lax.ppermute(x, AXES, pairs)  45 us
    ppermute x4, waiting for transfers between devices, body(): lax.ppermute(part, AXES, perm)  10.1 us
    pallas_call x4, Pallas kernels, project(): pl.pallas_call(functools.partial(project_kernel, terms, len(used)), grid=...  8.28 us
    ppermute x4, starting transfers between devices, body(): lax.ppermute(part, AXES, perm)  7.27 us
    pallas_call x1, Pallas kernels, own_part(): pl.pallas_call(own_kernel, grid_spec=pltpu.PrefetchScalarGridSpec(num_sca...  6.27 us
    pallas_call x1, Pallas kernels, query_part(): pl.pallas_call(query_kernel, grid_spec=pltpu.PrefetchScalarGridSpec(num_s...  4.29 us
    pallas_call x1, Pallas kernels, key_part(): pl.pallas_call(key_kernel, grid_spec=pltpu.PrefetchScalarGridSpec(num_sca...  4.04 us
  transfers between devices with their start and end apart: 30, of which 17 were waited for; matrix products, arithmetic and copies ran while one was open for 2% of the time, Pallas kernels for 12%

profile of v7, /device:TPU:0, one launch (start us, length us, event | category | flops | bytes accessed | tf_op | source)
XLA Modules:
  0.0 171.3 jit_solution(7666724514213683067)
XLA Ops:
  0.0 4.0 %key_part.1 = (f32[4,264,128]{2,1,0:T(8,128)}, f32[4,256,256]{2,1,0:T(8,128)}) custom-call(s32[1]{0:T(128)S(6)} %xor.23.first, f32[256,1024]{1,0:T(8,128)} %k_ref.3, f32[8,128,128]{2,1,0:T(8,128)} %k_map_ref.1, f32[256,1024]{1,0:T(8,128)} %v_ref.5), custom_call_target="tpu_custom_call" | custom-call | flops 603979776 | bytes 3145728 | tf_op jit(solution)/shard_map/key_part/pallas_call | solution.py:236
  4.1 3.0 %collective-permute-start = (f32[4,264,128]{2,1,0:T(8,128)}, f32[4,264,128]{2,1,0:T(8,128)}, u32[]{:S(2)}, u32[]{:S(2)}) collective-permute-start(f32[4,264,128]{2,1,0:T(8,128)} %get-tuple-element.76), channel_id=1, source_target_pairs={{0,4},{1,5},{2,6},{3,7},{4,0},{5,1},{6,2},{7,3},{8,12},{9,13},{10,... | collective-permute-start | bytes 1622024 | tf_op jit(solution)/shard_map/ppermute | solution.py:218
  7.6 2.7 %collective-permute-start.1 = (f32[512,128]{1,0:T(8,128)S(1)}, f32[512,128]{1,0:T(8,128)S(1)}, u32[]{:S(2)}, u32[]{:S(2)}) collective-permute-start(f32[512,128]{1,0:T(8,128)S(1)} %arrange.2), channel_id=1, source_target_pairs={{0,16},{1,17},{2,18},{3,19},{4,20},{5,21},{6,22},{7,23},{8,24},{9,... | collective-permute-start | bytes 786440 | tf_op jit(solution)/shard_map/ppermute | solution.py:218
  11.3 6.3 %own_part.1 = (f32[4,264,128]{2,1,0:T(8,128)S(1)}, f32[4,256,256]{2,1,0:T(8,128)S(1)}, f32[4,256,128]{2,1,0:T(8,128)S(1)}, f32[4,256,128]{2,1,0:T(8,128)S(1)}) custom-call(s32[1]{0:T(128)} %bitcast.first, f32[256,1024]{1,0:T(8,128)S(1)} %copy-done.1, f32[8,128,128]{2,1,0:T(8,128)S(1)} %copy-done.4, f32[256,1024]{1,0:T(8,128)S(1)} %copy-done.5, ...), custom_call_target="tpu_custom_call" | custom-call | flops 2013265920 | bytes 5767168 | tf_op jit(solution)/shard_map/own_part/pallas_call | solution.py:260
  18.7 3.3 %collective-permute-done.1.refs_9_ = f32[512,128]{1,0:T(8,128)S(1)} collective-permute-done((f32[512,128]{1,0:T(8,128)S(1)}, f32[512,128]{1,0:T(8,128)S(1)}, u32[]{:S(2)}, u32[]{:S(2)}) %collective-permute-start.1) | collective-permute-done | bytes 262176 | tf_op jit(solution)/shard_map/ppermute | solution.py:218
  25.1 2.7 %collective-permute-start.2 = (f32[4,264,128]{2,1,0:T(8,128)S(1)}, f32[4,264,128]{2,1,0:T(8,128)S(1)}, u32[]{:S(2)}, u32[]{:S(2)}) collective-permute-start(f32[4,264,128]{2,1,0:T(8,128)S(1)} %add.19), channel_id=1, source_target_pairs={{0,8},{1,9},{2,10},{3,11},{4,12},{5,13},{6,14},{7,15},{8,0},{9,1},... | collective-permute-start | bytes 1622024 | tf_op jit(solution)/shard_map/ppermute | solution.py:218
  28.0 19.0 %collective-permute-done.3.refs_16_.refs_8_ = f32[1024,128]{1,0:T(8,128)S(1)} collective-permute-done((f32[1024,128]{1,0:T(8,128)S(1)}, f32[1024,128]{1,0:T(8,128)S(1)}, u32[]{:S(2)}, u32[]{:S(2)}) %collective-permute-start.3) | collective-permute-done | bytes 524320 | tf_op jit(solution)/shard_map/ppermute | solution.py:218
  51.4 3.1 %collective-permute-start.8 = (f32[2,264,128]{2,1,0:T(8,128)S(1)}, f32[2,264,128]{2,1,0:T(8,128)S(1)}, u32[]{:S(2)}, u32[]{:S(2)}) collective-permute-start(f32[2,264,128]{2,1,0:T(8,128)S(1)} %select_add_fusion.3), channel_id=1, source_target_pairs={{0,16},{1,17},{2,18},{3,19},{4,20},{5,21},{6,22},{7,23},{8,24},{9,... | collective-permute-start | bytes 811016 | tf_op jit(solution)/shard_map/ppermute | solution.py:218
  54.6 5.4 %collective-permute-done.8 = f32[2,264,128]{2,1,0:T(8,128)S(1)} collective-permute-done((f32[2,264,128]{2,1,0:T(8,128)S(1)}, f32[2,264,128]{2,1,0:T(8,128)S(1)}, u32[]{:S(2)}, u32[]{:S(2)}) %collective-permute-start.8) | collective-permute-done | bytes 270368 | tf_op jit(solution)/shard_map/ppermute | solution.py:218
  61.4 11.8 %collective-permute-start.13 = (f32[512,128]{1,0:T(8,128)S(1)}, f32[512,128]{1,0:T(8,128)S(1)}, u32[]{:S(2)}, u32[]{:S(2)}) collective-permute-start(f32[512,128]{1,0:T(8,128)S(1)} %get-tuple-element.112), channel_id=1, source_target_pairs={{0,16},{1,17},{2,18},{3,19},{4,20},{5,21},{6,22},{7,23},{8,24},{9,... | collective-permute-start | bytes 786440 | tf_op jit(solution)/shard_map/ppermute | solution.py:218
  73.3 7.2 %collective-permute-done.11.refs_9_ = f32[512,128]{1,0:T(8,128)S(1)} collective-permute-done((f32[512,128]{1,0:T(8,128)S(1)}, f32[512,128]{1,0:T(8,128)S(1)}, u32[]{:S(2)}, u32[]{:S(2)}) %collective-permute-start.11) | collective-permute-done | bytes 262176 | tf_op jit(solution)/shard_map/ppermute | solution.py:218
  80.7 2.6 %collective-permute-start.12 = (f32[4,264,128]{2,1,0:T(8,128)S(1)}, f32[4,264,128]{2,1,0:T(8,128)S(1)}, u32[]{:S(2)}, u32[]{:S(2)}) collective-permute-start(f32[4,264,128]{2,1,0:T(8,128)S(1)} %get-tuple-element.144), channel_id=1, source_target_pairs={{0,4},{1,5},{2,6},{3,7},{4,0},{5,1},{6,2},{7,3},{8,12},{9,13},{10,... | collective-permute-start | bytes 1622024 | tf_op jit(solution)/shard_map/ppermute | solution.py:218
  86.3 3.2 %collective-permute-start.16 = (f32[1024,128]{1,0:T(8,128)S(1)}, f32[1024,128]{1,0:T(8,128)S(1)}, u32[]{:S(2)}, u32[]{:S(2)}) collective-permute-start(f32[1024,128]{1,0:T(8,128)S(1)} %collective-permute-done.6), channel_id=1, source_target_pairs={{0,16},{1,17},{2,18},{3,19},{4,20},{5,21},{6,22},{7,23},{8,24},{9,... | collective-permute-start | bytes 1572872 | tf_op jit(solution)/shard_map/ppermute | solution.py:218
  90.8 4.3 %query_part.1 = (f32[4,256,256]{2,1,0:T(8,128)S(1)}, f32[4,256,128]{2,1,0:T(8,128)S(1)}, f32[4,256,128]{2,1,0:T(8,128)S(1)}) custom-call(s32[1]{0:T(128)S(6)} %xor.23.first, f32[256,1024]{1,0:T(8,128)S(1)} %copy-done.5, f32[8,128,128]{2,1,0:T(8,128)S(1)} %copy-done.8, f32[256,1024]{1,0:T(8,128)S(1)} %copy-done.2, f32[4,256,256]{2,1,0:T(8,128)S(1)} %copy-done.6), custom_call_target="tpu_custom_call" | custom-call | flops 1409286144 | bytes 4194304 | tf_op jit(solution)/shard_map/query_part/pallas_call | solution.py:280
  95.1 11.6 %collective-permute-done.14.refs_0_.refs_1_ = f32[256,512]{1,0:T(8,128)S(1)} collective-permute-done((f32[256,512]{1,0:T(8,128)S(1)}, f32[256,512]{1,0:T(8,128)S(1)}, u32[]{:S(2)}, u32[]{:S(2)}) %collective-permute-start.14) | collective-permute-done | bytes 524320 | tf_op jit(solution)/shard_map/ppermute | solution.py:218
  108.1 3.1 %collective-permute-done.16.refs_6_.refs_13_ = f32[1024,128]{1,0:T(8,128)S(1)} collective-permute-done((f32[1024,128]{1,0:T(8,128)S(1)}, f32[1024,128]{1,0:T(8,128)S(1)}, u32[]{:S(2)}, u32[]{:S(2)}) %collective-permute-start.16) | collective-permute-done | bytes 524320 | tf_op jit(solution)/shard_map/ppermute | solution.py:218
  111.7 2.7 %collective-permute-start.20 = (f32[1024,128]{1,0:T(8,128)S(1)}, f32[1024,128]{1,0:T(8,128)S(1)}, u32[]{:S(2)}, u32[]{:S(2)}) collective-permute-start(f32[1024,128]{1,0:T(8,128)S(1)} %collective-permute-done.7), channel_id=1, source_target_pairs={{0,16},{1,17},{2,18},{3,19},{4,20},{5,21},{6,22},{7,23},{8,24},{9,... | collective-permute-start | bytes 1572872 | tf_op jit(solution)/shard_map/ppermute | solution.py:218
  117.8 13.2 %collective-permute-done.21.refs_17_ = f32[512,128]{1,0:T(8,128)S(1)} collective-permute-done((f32[512,128]{1,0:T(8,128)S(1)}, f32[512,128]{1,0:T(8,128)S(1)}, u32[]{:S(2)}, u32[]{:S(2)}) %collective-permute-start.21) | collective-permute-done | bytes 262176 | tf_op jit(solution)/shard_map/ppermute | solution.py:218
  131.0 2.6 %collective-permute-done.18.refs_1_ = f32[256,512]{1,0:T(8,128)S(1)} collective-permute-done((f32[256,512]{1,0:T(8,128)S(1)}, f32[256,512]{1,0:T(8,128)S(1)}, u32[]{:S(2)}, u32[]{:S(2)}) %collective-permute-start.18) | collective-permute-done | bytes 524320 | tf_op jit(solution)/shard_map/ppermute | solution.py:218
  138.0 3.5 %project.4.refs_10_ = f32[512,1024]{1,0:T(8,128)S(1)} custom-call(f32[256,512]{1,0:T(8,128)S(1)} %mix.2.refs_0_, f32[256,512]{1,0:T(8,128)S(1)} %collective-permute-done.14.refs_0_.refs_1_, f32[256,512]{1,0:T(8,128)S(1)} %collective-permute-done.15.refs_2_, f32[512,512]{1,0:T(8,128)S(1)} %collective-permute-done.19.refs_3_.refs_0_.refs_4_, ...), custom_call_target="tpu_custom_call" | custom-call | flops 2818572288 | bytes 5767168 | tf_op jit(solution)/shard_map/project/pallas_call | solution.py:468
  143.4 2.7 %collective-permute-done.23.refs_1_.refs_5_ = f32[256,512]{1,0:T(8,128)S(1)} collective-permute-done((f32[256,512]{1,0:T(8,128)S(1)}, f32[256,512]{1,0:T(8,128)S(1)}, u32[]{:S(2)}, u32[]{:S(2)}) %collective-permute-start.23) | collective-permute-done | bytes 524320 | tf_op jit(solution)/shard_map/ppermute | solution.py:218
  152.9 3.2 %collective-permute-start.27 = (f32[256,256]{1,0:T(8,128)S(1)}, f32[256,256]{1,0:T(8,128)S(1)}, u32[]{:S(2)}, u32[]{:S(2)}) collective-permute-start(f32[256,256]{1,0:T(8,128)S(1)} %get-tuple-element.140), channel_id=1, source_target_pairs={{0,2},{2,0},{3,10},{1,8},{4,6},{6,4},{7,14},{5,12},{8,3},{10,1},{1... | collective-permute-start | bytes 786440 | tf_op jit(solution)/shard_map/ppermute | solution.py:519
  156.1 2.6 %collective-permute-start.28 = (f32[256,256]{1,0:T(8,128)S(1)}, f32[256,256]{1,0:T(8,128)S(1)}, u32[]{:S(2)}, u32[]{:S(2)}) collective-permute-start(f32[256,256]{1,0:T(8,128)S(1)} %get-tuple-element.141), channel_id=1, source_target_pairs={{0,8},{2,10},{3,0},{1,2},{4,12},{6,14},{7,4},{5,6},{8,9},{10,11},{... | collective-permute-start | bytes 786440 | tf_op jit(solution)/shard_map/ppermute | solution.py:519
  159.5 8.2 %collective-permute-done.27.refs_1_ = f32[256,256]{1,0:T(8,128)S(1)} collective-permute-done((f32[256,256]{1,0:T(8,128)S(1)}, f32[256,256]{1,0:T(8,128)S(1)}, u32[]{:S(2)}, u32[]{:S(2)}) %collective-permute-start.27) | collective-permute-done | bytes 262176 | tf_op jit(solution)/shard_map/ppermute | solution.py:519
  (79 shorter events, 39.1 us)
Async XLA Ops:
  4.1 17.9 %collective-permute-start = (f32[4,264,128]{2,1,0:T(8,128)}, f32[4,264,128]{2,1,0:T(8,128)}, u32[]{:S(2)}, u32[]{:S(2)}) collective-permute-start(f32[4,264,128]{2,1,0:T(8,128)} %get-tuple-element.76), channel_id=1, source_target_pairs={{0,4},{1,5},{2,6},{3,7},{4,0},{5,1},{6,2},{7,3},{8,12},{9,13},{10,... | collective-permute-start | bytes 1622024 | tf_op jit(solution)/shard_map/ppermute | solution.py:218
  7.6 14.3 %collective-permute-start.1 = (f32[512,128]{1,0:T(8,128)S(1)}, f32[512,128]{1,0:T(8,128)S(1)}, u32[]{:S(2)}, u32[]{:S(2)}) collective-permute-start(f32[512,128]{1,0:T(8,128)S(1)} %arrange.2), channel_id=1, source_target_pairs={{0,16},{1,17},{2,18},{3,19},{4,20},{5,21},{6,22},{7,23},{8,24},{9,... | collective-permute-start | bytes 786440 | tf_op jit(solution)/shard_map/ppermute | solution.py:218
  22.0 25.0 %collective-permute-start.3 = (f32[1024,128]{1,0:T(8,128)S(1)}, f32[1024,128]{1,0:T(8,128)S(1)}, u32[]{:S(2)}, u32[]{:S(2)}) collective-permute-start(f32[1024,128]{1,0:T(8,128)S(1)} %get-tuple-element.88), channel_id=1, source_target_pairs={{0,16},{1,17},{2,18},{3,19},{4,20},{5,21},{6,22},{7,23},{8,24},{9,... | collective-permute-start | bytes 1572872 | tf_op jit(solution)/shard_map/ppermute | solution.py:218
  22.4 27.5 %collective-permute-start.4 = (f32[2048,128]{1,0:T(8,128)S(1)}, f32[2048,128]{1,0:T(8,128)S(1)}, u32[]{:S(2)}, u32[]{:S(2)}) collective-permute-start(f32[2048,128]{1,0:T(8,128)S(1)} %get-tuple-element.89.refs_7_.refs_14_.refs_6_.refs_2_), channel_id=1, source_target_pairs={{0,4},{1,5},{2,6},{3,7},{4,0},{5,1},{6,2},{7,3},{8,12},{9,13},{10,... | collective-permute-start | bytes 3145736 | tf_op jit(solution)/shard_map/ppermute | solution.py:218
  23.9 26.0 %collective-permute-start.5 = (f32[2048,128]{1,0:T(8,128)S(1)}, f32[2048,128]{1,0:T(8,128)S(1)}, u32[]{:S(2)}, u32[]{:S(2)}) collective-permute-start(f32[2048,128]{1,0:T(8,128)S(1)} %get-tuple-element.90), channel_id=1, source_target_pairs={{0,1},{1,0},{2,3},{3,2},{4,5},{5,4},{6,7},{7,6},{8,9},{9,8},{10,11... | collective-permute-start | bytes 3145736 | tf_op jit(solution)/shard_map/ppermute | solution.py:218
  25.1 24.9 %collective-permute-start.2 = (f32[4,264,128]{2,1,0:T(8,128)S(1)}, f32[4,264,128]{2,1,0:T(8,128)S(1)}, u32[]{:S(2)}, u32[]{:S(2)}) collective-permute-start(f32[4,264,128]{2,1,0:T(8,128)S(1)} %add.19), channel_id=1, source_target_pairs={{0,8},{1,9},{2,10},{3,11},{4,12},{5,13},{6,14},{7,15},{8,0},{9,1},... | collective-permute-start | bytes 1622024 | tf_op jit(solution)/shard_map/ppermute | solution.py:218
  27.8 19.3 %collective-permute-start.6 = (f32[1024,128]{1,0:T(8,128)S(1)}, f32[1024,128]{1,0:T(8,128)S(1)}, u32[]{:S(2)}, u32[]{:S(2)}) collective-permute-start(f32[1024,128]{1,0:T(8,128)S(1)} %get-tuple-element.91), channel_id=1, source_target_pairs={{0,1},{1,0},{2,3},{3,2},{4,5},{5,4},{6,7},{7,6},{8,9},{9,8},{10,11... | collective-permute-start | bytes 1572872 | tf_op jit(solution)/shard_map/ppermute | solution.py:218
  49.9 30.6 %collective-permute-start.10 = (f32[2048,128]{1,0:T(8,128)S(1)}, f32[2048,128]{1,0:T(8,128)S(1)}, u32[]{:S(2)}, u32[]{:S(2)}) collective-permute-start(f32[2048,128]{1,0:T(8,128)S(1)} %collective-permute-done.5.refs_4_.refs_11_.refs_2_.refs_6_), channel_id=1, source_target_pairs={{0,4},{1,5},{2,6},{3,7},{4,0},{5,1},{6,2},{7,3},{8,12},{9,13},{10,... | collective-permute-start | bytes 3145736 | tf_op jit(solution)/shard_map/ppermute | solution.py:218
  59.9 13.3 %collective-permute-start.9 = (f32[2,264,128]{2,1,0:T(8,128)S(1)}, f32[2,264,128]{2,1,0:T(8,128)S(1)}, u32[]{:S(2)}, u32[]{:S(2)}) collective-permute-start(f32[2,264,128]{2,1,0:T(8,128)S(1)} %collective-permute-done.8), channel_id=1, source_target_pairs={{16,24},{17,25},{18,26},{19,27},{20,28},{21,29},{22,30},{23,31},{2... | collective-permute-start | bytes 811016 | tf_op jit(solution)/shard_map/ppermute | solution.py:218
  60.8 19.7 %collective-permute-start.11 = (f32[512,128]{1,0:T(8,128)S(1)}, f32[512,128]{1,0:T(8,128)S(1)}, u32[]{:S(2)}, u32[]{:S(2)}) collective-permute-start(f32[512,128]{1,0:T(8,128)S(1)} %collective-permute-done.1.refs_9_), channel_id=1, source_target_pairs={{0,4},{1,5},{2,6},{3,7},{4,0},{5,1},{6,2},{7,3},{8,12},{9,13},{10,... | collective-permute-start | bytes 786440 | tf_op jit(solution)/shard_map/ppermute | solution.py:218
  61.4 23.4 %collective-permute-start.13 = (f32[512,128]{1,0:T(8,128)S(1)}, f32[512,128]{1,0:T(8,128)S(1)}, u32[]{:S(2)}, u32[]{:S(2)}) collective-permute-start(f32[512,128]{1,0:T(8,128)S(1)} %get-tuple-element.112), channel_id=1, source_target_pairs={{0,16},{1,17},{2,18},{3,19},{4,20},{5,21},{6,22},{7,23},{8,24},{9,... | collective-permute-start | bytes 786440 | tf_op jit(solution)/shard_map/ppermute | solution.py:218
  80.7 26.0 %collective-permute-start.12 = (f32[4,264,128]{2,1,0:T(8,128)S(1)}, f32[4,264,128]{2,1,0:T(8,128)S(1)}, u32[]{:S(2)}, u32[]{:S(2)}) collective-permute-start(f32[4,264,128]{2,1,0:T(8,128)S(1)} %get-tuple-element.144), channel_id=1, source_target_pairs={{0,4},{1,5},{2,6},{3,7},{4,0},{5,1},{6,2},{7,3},{8,12},{9,13},{10,... | collective-permute-start | bytes 1622024 | tf_op jit(solution)/shard_map/ppermute | solution.py:218
  84.8 21.9 %collective-permute-start.14 = (f32[256,512]{1,0:T(8,128)S(1)}, f32[256,512]{1,0:T(8,128)S(1)}, u32[]{:S(2)}, u32[]{:S(2)}) collective-permute-start(f32[256,512]{1,0:T(8,128)S(1)} %mix.2.refs_0_), channel_id=1, source_target_pairs={{0,8},{1,9},{2,10},{3,11},{4,12},{5,13},{6,14},{7,15},{8,0},{9,1},... | collective-permute-start | bytes 1572872 | tf_op jit(solution)/shard_map/ppermute | solution.py:218
  84.8 23.3 %collective-permute-start.15 = (f32[256,512]{1,0:T(8,128)S(1)}, f32[256,512]{1,0:T(8,128)S(1)}, u32[]{:S(2)}, u32[]{:S(2)}) collective-permute-start(f32[256,512]{1,0:T(8,128)S(1)} %mix.2.refs_0_), channel_id=1, source_target_pairs={{0,2},{1,3},{2,0},{3,1},{4,6},{5,7},{6,4},{7,5},{8,10},{9,11},{10,... | collective-permute-start | bytes 1572872 | tf_op jit(solution)/shard_map/ppermute | solution.py:218
  86.3 24.9 %collective-permute-start.16 = (f32[1024,128]{1,0:T(8,128)S(1)}, f32[1024,128]{1,0:T(8,128)S(1)}, u32[]{:S(2)}, u32[]{:S(2)}) collective-permute-start(f32[1024,128]{1,0:T(8,128)S(1)} %collective-permute-done.6), channel_id=1, source_target_pairs={{0,16},{1,17},{2,18},{3,19},{4,20},{5,21},{6,22},{7,23},{8,24},{9,... | collective-permute-start | bytes 1572872 | tf_op jit(solution)/shard_map/ppermute | solution.py:218
  89.6 21.7 %collective-permute-start.17 = (f32[1024,128]{1,0:T(8,128)S(1)}, f32[1024,128]{1,0:T(8,128)S(1)}, u32[]{:S(2)}, u32[]{:S(2)}) collective-permute-start(f32[1024,128]{1,0:T(8,128)S(1)} %collective-permute-done.3.refs_16_.refs_8_), channel_id=1, source_target_pairs={{0,4},{1,5},{2,6},{3,7},{4,0},{5,1},{6,2},{7,3},{8,12},{9,13},{10,... | collective-permute-start | bytes 1572872 | tf_op jit(solution)/shard_map/ppermute | solution.py:218
  111.2 24.0 %collective-permute-start.19 = (f32[512,512]{1,0:T(8,128)S(1)}, f32[512,512]{1,0:T(8,128)S(1)}, u32[]{:S(2)}, u32[]{:S(2)}) collective-permute-start(f32[512,512]{1,0:T(8,128)S(1)} %get-tuple-element.121), channel_id=1, source_target_pairs={{0,2},{1,3},{2,0},{3,1},{4,6},{5,7},{6,4},{7,5},{8,10},{9,11},{10,... | collective-permute-start | bytes 3145736 | tf_op jit(solution)/shard_map/ppermute | solution.py:218
  111.7 21.8 %collective-permute-start.18 = (f32[256,512]{1,0:T(8,128)S(1)}, f32[256,512]{1,0:T(8,128)S(1)}, u32[]{:S(2)}, u32[]{:S(2)}) collective-permute-start(f32[256,512]{1,0:T(8,128)S(1)} %get-tuple-element.120.refs_0_), channel_id=1, source_target_pairs={{0,8},{1,9},{2,10},{3,11},{4,12},{5,13},{6,14},{7,15},{8,0},{9,1},... | collective-permute-start | bytes 1572872 | tf_op jit(solution)/shard_map/ppermute | solution.py:218
  111.7 23.5 %collective-permute-start.20 = (f32[1024,128]{1,0:T(8,128)S(1)}, f32[1024,128]{1,0:T(8,128)S(1)}, u32[]{:S(2)}, u32[]{:S(2)}) collective-permute-start(f32[1024,128]{1,0:T(8,128)S(1)} %collective-permute-done.7), channel_id=1, source_target_pairs={{0,16},{1,17},{2,18},{3,19},{4,20},{5,21},{6,22},{7,23},{8,24},{9,... | collective-permute-start | bytes 1572872 | tf_op jit(solution)/shard_map/ppermute | solution.py:218
  114.4 20.8 %collective-permute-start.22 = (f32[1024,128]{1,0:T(8,128)S(1)}, f32[1024,128]{1,0:T(8,128)S(1)}, u32[]{:S(2)}, u32[]{:S(2)}) collective-permute-start(f32[1024,128]{1,0:T(8,128)S(1)} %collective-permute-done.16.refs_6_.refs_13_), channel_id=1, source_target_pairs={{0,4},{1,5},{2,6},{3,7},{4,0},{5,1},{6,2},{7,3},{8,12},{9,13},{10,... | collective-permute-start | bytes 1572872 | tf_op jit(solution)/shard_map/ppermute | solution.py:218
  115.9 15.1 %collective-permute-start.21 = (f32[512,128]{1,0:T(8,128)S(1)}, f32[512,128]{1,0:T(8,128)S(1)}, u32[]{:S(2)}, u32[]{:S(2)}) collective-permute-start(f32[512,128]{1,0:T(8,128)S(1)} %collective-permute-done.13.refs_4_), channel_id=1, source_target_pairs={{0,4},{1,5},{2,6},{3,7},{4,0},{5,1},{6,2},{7,3},{8,12},{9,13},{10,... | collective-permute-start | bytes 786440 | tf_op jit(solution)/shard_map/ppermute | solution.py:218
  135.6 11.3 %collective-permute-start.24 = (f32[1024,128]{1,0:T(8,128)S(1)}, f32[1024,128]{1,0:T(8,128)S(1)}, u32[]{:S(2)}, u32[]{:S(2)}) collective-permute-start(f32[1024,128]{1,0:T(8,128)S(1)} %collective-permute-done.20.refs_4_.refs_8_), channel_id=1, source_target_pairs={{0,4},{1,5},{2,6},{3,7},{4,0},{5,1},{6,2},{7,3},{8,12},{9,13},{10,... | collective-permute-start | bytes 1572872 | tf_op jit(solution)/shard_map/ppermute | solution.py:218
  152.9 14.8 %collective-permute-start.27 = (f32[256,256]{1,0:T(8,128)S(1)}, f32[256,256]{1,0:T(8,128)S(1)}, u32[]{:S(2)}, u32[]{:S(2)}) collective-permute-start(f32[256,256]{1,0:T(8,128)S(1)} %get-tuple-element.140), channel_id=1, source_target_pairs={{0,2},{2,0},{3,10},{1,8},{4,6},{6,4},{7,14},{5,12},{8,3},{10,1},{1... | collective-permute-start | bytes 786440 | tf_op jit(solution)/shard_map/ppermute | solution.py:519
  156.1 13.4 %collective-permute-start.28 = (f32[256,256]{1,0:T(8,128)S(1)}, f32[256,256]{1,0:T(8,128)S(1)}, u32[]{:S(2)}, u32[]{:S(2)}) collective-permute-start(f32[256,256]{1,0:T(8,128)S(1)} %get-tuple-element.141), channel_id=1, source_target_pairs={{0,8},{2,10},{3,0},{1,2},{4,12},{6,14},{7,4},{5,6},{8,9},{10,11},{... | collective-permute-start | bytes 786440 | tf_op jit(solution)/shard_map/ppermute | solution.py:519
  (17 other events, 130.9 us)

commit v8 on v7

--- a/solution.py
+++ b/solution.py
@@ -230,16 +230,16 @@
         return pl.BlockSpec((1, size, lanes), lambda i, *_: (i, 0, 0))
 
     def key_part(first):
-        columns = pl.BlockSpec((rows, wide), lambda i, first: (0, first[0]))
-        maps = pl.BlockSpec((half, head_size, feat_half), lambda i, first: (first[0], 0, 0))
+        columns = pl.BlockSpec((rows, wide // 2), lambda i, first: (0, 2 * first[0] + i))
+        maps = pl.BlockSpec((half // 2, head_size, feat_half), lambda i, first: (2 * first[0] + i, 0, 0))
         shapes = [of(half, feat_size + EXTRA, head_size), of(half, rows, feat_size)]
         return pl.pallas_call(
             key_kernel,
             grid_spec=pltpu.PrefetchScalarGridSpec(
                 num_scalar_prefetch=1,
-                grid=(1,),
+                grid=(2,),
                 in_specs=[columns, maps, columns],
-                out_specs=[pl.BlockSpec(s.shape, lambda i, first: (0, 0, 0)) for s in shapes],
+                out_specs=[pl.BlockSpec((half // 2, *s.shape[1:]), lambda i, first: (i, 0, 0)) for s in shapes],
             ),
             out_shape=shapes,
             compiler_params=params(60),

time: 172 us -> 172 us (level)
  no operation moved by 1% of the time
where the time goes in v8:
time: 172 us
  waiting for transfers between devices  85.4 us (50%)
  starting transfers between devices  52.3 us (30%)
  Pallas kernels  29.9 us (17%)
  local copies, waits for them, and re-layouts  2.46 us (1%)
    ppermute x26, waiting for transfers between devices, swap(): return lax.ppermute(x, AXES, pairs)  75.3 us
    ppermute x26, starting transfers between devices, swap(): return lax.ppermute(x, AXES, pairs)  45 us
    ppermute x4, waiting for transfers between devices, body(): lax.ppermute(part, AXES, perm)  10.1 us
    pallas_call x4, Pallas kernels, project(): pl.pallas_call(functools.partial(project_kernel, terms, len(used)), grid=...  8.27 us
    ppermute x4, starting transfers between devices, body(): lax.ppermute(part, AXES, perm)  7.27 us
    pallas_call x1, Pallas kernels, own_part(): pl.pallas_call(own_kernel, grid_spec=pltpu.PrefetchScalarGridSpec(num_sca...  6.27 us
    pallas_call x1, Pallas kernels, key_part(): pl.pallas_call(key_kernel, grid_spec=pltpu.PrefetchScalarGridSpec(num_sca...  4.43 us
    pallas_call x1, Pallas kernels, query_part(): pl.pallas_call(query_kernel, grid_spec=pltpu.PrefetchScalarGridSpec(num_s...  4.29 us
  transfers between devices with their start and end apart: 30, of which 17 were waited for; matrix products, arithmetic and copies ran while one was open for 2% of the time, Pallas kernels for 12%

profile of v8, /device:TPU:0, one launch (start us, length us, event | category | flops | bytes accessed | tf_op | source)
XLA Modules:
  0.0 171.7 jit_solution(11647659680564749326)
XLA Ops:
  0.0 4.4 %key_part.1 = (f32[4,264,128]{2,1,0:T(8,128)}, f32[4,256,256]{2,1,0:T(8,128)}) custom-call(s32[1]{0:T(128)S(6)} %xor.23.first, f32[256,1024]{1,0:T(8,128)} %k_ref.3, f32[8,128,128]{2,1,0:T(8,128)} %k_map_ref.1, f32[256,1024]{1,0:T(8,128)} %v_ref.5), custom_call_target="tpu_custom_call" | custom-call | flops 603979776 | bytes 3145728 | tf_op jit(solution)/shard_map/key_part/pallas_call | solution.py:236
  4.4 3.0 %collective-permute-start = (f32[4,264,128]{2,1,0:T(8,128)}, f32[4,264,128]{2,1,0:T(8,128)}, u32[]{:S(2)}, u32[]{:S(2)}) collective-permute-start(f32[4,264,128]{2,1,0:T(8,128)} %get-tuple-element.76), channel_id=1, source_target_pairs={{0,4},{1,5},{2,6},{3,7},{4,0},{5,1},{6,2},{7,3},{8,12},{9,13},{10,... | collective-permute-start | bytes 1622024 | tf_op jit(solution)/shard_map/ppermute | solution.py:218
  8.0 2.7 %collective-permute-start.1 = (f32[512,128]{1,0:T(8,128)S(1)}, f32[512,128]{1,0:T(8,128)S(1)}, u32[]{:S(2)}, u32[]{:S(2)}) collective-permute-start(f32[512,128]{1,0:T(8,128)S(1)} %arrange.2), channel_id=1, source_target_pairs={{0,16},{1,17},{2,18},{3,19},{4,20},{5,21},{6,22},{7,23},{8,24},{9,... | collective-permute-start | bytes 786440 | tf_op jit(solution)/shard_map/ppermute | solution.py:218
  11.7 6.3 %own_part.1 = (f32[4,264,128]{2,1,0:T(8,128)S(1)}, f32[4,256,256]{2,1,0:T(8,128)S(1)}, f32[4,256,128]{2,1,0:T(8,128)S(1)}, f32[4,256,128]{2,1,0:T(8,128)S(1)}) custom-call(s32[1]{0:T(128)} %bitcast.first, f32[256,1024]{1,0:T(8,128)S(1)} %copy-done.1, f32[8,128,128]{2,1,0:T(8,128)S(1)} %copy-done.4, f32[256,1024]{1,0:T(8,128)S(1)} %copy-done.5, ...), custom_call_target="tpu_custom_call" | custom-call | flops 2013265920 | bytes 5767168 | tf_op jit(solution)/shard_map/own_part/pallas_call | solution.py:260
  19.0 3.3 %collective-permute-done.1.refs_9_ = f32[512,128]{1,0:T(8,128)S(1)} collective-permute-done((f32[512,128]{1,0:T(8,128)S(1)}, f32[512,128]{1,0:T(8,128)S(1)}, u32[]{:S(2)}, u32[]{:S(2)}) %collective-permute-start.1) | collective-permute-done | bytes 262176 | tf_op jit(solution)/shard_map/ppermute | solution.py:218
  25.4 2.7 %collective-permute-start.2 = (f32[4,264,128]{2,1,0:T(8,128)S(1)}, f32[4,264,128]{2,1,0:T(8,128)S(1)}, u32[]{:S(2)}, u32[]{:S(2)}) collective-permute-start(f32[4,264,128]{2,1,0:T(8,128)S(1)} %add.19), channel_id=1, source_target_pairs={{0,8},{1,9},{2,10},{3,11},{4,12},{5,13},{6,14},{7,15},{8,0},{9,1},... | collective-permute-start | bytes 1622024 | tf_op jit(solution)/shard_map/ppermute | solution.py:218
  28.4 19.0 %collective-permute-done.3.refs_16_.refs_8_ = f32[1024,128]{1,0:T(8,128)S(1)} collective-permute-done((f32[1024,128]{1,0:T(8,128)S(1)}, f32[1024,128]{1,0:T(8,128)S(1)}, u32[]{:S(2)}, u32[]{:S(2)}) %collective-permute-start.3) | collective-permute-done | bytes 524320 | tf_op jit(solution)/shard_map/ppermute | solution.py:218
  51.8 3.1 %collective-permute-start.8 = (f32[2,264,128]{2,1,0:T(8,128)S(1)}, f32[2,264,128]{2,1,0:T(8,128)S(1)}, u32[]{:S(2)}, u32[]{:S(2)}) collective-permute-start(f32[2,264,128]{2,1,0:T(8,128)S(1)} %select_add_fusion.3), channel_id=1, source_target_pairs={{0,16},{1,17},{2,18},{3,19},{4,20},{5,21},{6,22},{7,23},{8,24},{9,... | collective-permute-start | bytes 811016 | tf_op jit(solution)/shard_map/ppermute | solution.py:218
  55.0 5.4 %collective-permute-done.8 = f32[2,264,128]{2,1,0:T(8,128)S(1)} collective-permute-done((f32[2,264,128]{2,1,0:T(8,128)S(1)}, f32[2,264,128]{2,1,0:T(8,128)S(1)}, u32[]{:S(2)}, u32[]{:S(2)}) %collective-permute-start.8) | collective-permute-done | bytes 270368 | tf_op jit(solution)/shard_map/ppermute | solution.py:218
  61.8 11.8 %collective-permute-start.13 = (f32[512,128]{1,0:T(8,128)S(1)}, f32[512,128]{1,0:T(8,128)S(1)}, u32[]{:S(2)}, u32[]{:S(2)}) collective-permute-start(f32[512,128]{1,0:T(8,128)S(1)} %get-tuple-element.112), channel_id=1, source_target_pairs={{0,16},{1,17},{2,18},{3,19},{4,20},{5,21},{6,22},{7,23},{8,24},{9,... | collective-permute-start | bytes 786440 | tf_op jit(solution)/shard_map/ppermute | solution.py:218
  73.7 7.2 %collective-permute-done.11.refs_9_ = f32[512,128]{1,0:T(8,128)S(1)} collective-permute-done((f32[512,128]{1,0:T(8,128)S(1)}, f32[512,128]{1,0:T(8,128)S(1)}, u32[]{:S(2)}, u32[]{:S(2)}) %collective-permute-start.11) | collective-permute-done | bytes 262176 | tf_op jit(solution)/shard_map/ppermute | solution.py:218
  81.1 2.6 %collective-permute-start.12 = (f32[4,264,128]{2,1,0:T(8,128)S(1)}, f32[4,264,128]{2,1,0:T(8,128)S(1)}, u32[]{:S(2)}, u32[]{:S(2)}) collective-permute-start(f32[4,264,128]{2,1,0:T(8,128)S(1)} %get-tuple-element.144), channel_id=1, source_target_pairs={{0,4},{1,5},{2,6},{3,7},{4,0},{5,1},{6,2},{7,3},{8,12},{9,13},{10,... | collective-permute-start | bytes 1622024 | tf_op jit(solution)/shard_map/ppermute | solution.py:218
  86.7 3.2 %collective-permute-start.16 = (f32[1024,128]{1,0:T(8,128)S(1)}, f32[1024,128]{1,0:T(8,128)S(1)}, u32[]{:S(2)}, u32[]{:S(2)}) collective-permute-start(f32[1024,128]{1,0:T(8,128)S(1)} %collective-permute-done.6), channel_id=1, source_target_pairs={{0,16},{1,17},{2,18},{3,19},{4,20},{5,21},{6,22},{7,23},{8,24},{9,... | collective-permute-start | bytes 1572872 | tf_op jit(solution)/shard_map/ppermute | solution.py:218
  91.1 4.3 %query_part.1 = (f32[4,256,256]{2,1,0:T(8,128)S(1)}, f32[4,256,128]{2,1,0:T(8,128)S(1)}, f32[4,256,128]{2,1,0:T(8,128)S(1)}) custom-call(s32[1]{0:T(128)S(6)} %xor.23.first, f32[256,1024]{1,0:T(8,128)S(1)} %copy-done.5, f32[8,128,128]{2,1,0:T(8,128)S(1)} %copy-done.8, f32[256,1024]{1,0:T(8,128)S(1)} %copy-done.2, f32[4,256,256]{2,1,0:T(8,128)S(1)} %copy-done.6), custom_call_target="tpu_custom_call" | custom-call | flops 1409286144 | bytes 4194304 | tf_op jit(solution)/shard_map/query_part/pallas_call | solution.py:280
  95.4 11.6 %collective-permute-done.14.refs_0_.refs_1_ = f32[256,512]{1,0:T(8,128)S(1)} collective-permute-done((f32[256,512]{1,0:T(8,128)S(1)}, f32[256,512]{1,0:T(8,128)S(1)}, u32[]{:S(2)}, u32[]{:S(2)}) %collective-permute-start.14) | collective-permute-done | bytes 524320 | tf_op jit(solution)/shard_map/ppermute | solution.py:218
  108.5 3.1 %collective-permute-done.16.refs_6_.refs_13_ = f32[1024,128]{1,0:T(8,128)S(1)} collective-permute-done((f32[1024,128]{1,0:T(8,128)S(1)}, f32[1024,128]{1,0:T(8,128)S(1)}, u32[]{:S(2)}, u32[]{:S(2)}) %collective-permute-start.16) | collective-permute-done | bytes 524320 | tf_op jit(solution)/shard_map/ppermute | solution.py:218
  112.1 2.7 %collective-permute-start.20 = (f32[1024,128]{1,0:T(8,128)S(1)}, f32[1024,128]{1,0:T(8,128)S(1)}, u32[]{:S(2)}, u32[]{:S(2)}) collective-permute-start(f32[1024,128]{1,0:T(8,128)S(1)} %collective-permute-done.7), channel_id=1, source_target_pairs={{0,16},{1,17},{2,18},{3,19},{4,20},{5,21},{6,22},{7,23},{8,24},{9,... | collective-permute-start | bytes 1572872 | tf_op jit(solution)/shard_map/ppermute | solution.py:218
  118.2 13.1 %collective-permute-done.21.refs_17_ = f32[512,128]{1,0:T(8,128)S(1)} collective-permute-done((f32[512,128]{1,0:T(8,128)S(1)}, f32[512,128]{1,0:T(8,128)S(1)}, u32[]{:S(2)}, u32[]{:S(2)}) %collective-permute-start.21) | collective-permute-done | bytes 262176 | tf_op jit(solution)/shard_map/ppermute | solution.py:218
  131.4 2.6 %collective-permute-done.18.refs_1_ = f32[256,512]{1,0:T(8,128)S(1)} collective-permute-done((f32[256,512]{1,0:T(8,128)S(1)}, f32[256,512]{1,0:T(8,128)S(1)}, u32[]{:S(2)}, u32[]{:S(2)}) %collective-permute-start.18) | collective-permute-done | bytes 524320 | tf_op jit(solution)/shard_map/ppermute | solution.py:218
  138.4 3.5 %project.4.refs_10_ = f32[512,1024]{1,0:T(8,128)S(1)} custom-call(f32[256,512]{1,0:T(8,128)S(1)} %mix.2.refs_0_, f32[256,512]{1,0:T(8,128)S(1)} %collective-permute-done.14.refs_0_.refs_1_, f32[256,512]{1,0:T(8,128)S(1)} %collective-permute-done.15.refs_2_, f32[512,512]{1,0:T(8,128)S(1)} %collective-permute-done.19.refs_3_.refs_0_.refs_4_, ...), custom_call_target="tpu_custom_call" | custom-call | flops 2818572288 | bytes 5767168 | tf_op jit(solution)/shard_map/project/pallas_call | solution.py:468
  143.8 2.7 %collective-permute-done.23.refs_1_.refs_5_ = f32[256,512]{1,0:T(8,128)S(1)} collective-permute-done((f32[256,512]{1,0:T(8,128)S(1)}, f32[256,512]{1,0:T(8,128)S(1)}, u32[]{:S(2)}, u32[]{:S(2)}) %collective-permute-start.23) | collective-permute-done | bytes 524320 | tf_op jit(solution)/shard_map/ppermute | solution.py:218
  153.2 3.2 %collective-permute-start.27 = (f32[256,256]{1,0:T(8,128)S(1)}, f32[256,256]{1,0:T(8,128)S(1)}, u32[]{:S(2)}, u32[]{:S(2)}) collective-permute-start(f32[256,256]{1,0:T(8,128)S(1)} %get-tuple-element.140), channel_id=1, source_target_pairs={{0,2},{2,0},{3,10},{1,8},{4,6},{6,4},{7,14},{5,12},{8,3},{10,1},{1... | collective-permute-start | bytes 786440 | tf_op jit(solution)/shard_map/ppermute | solution.py:519
  156.5 2.7 %collective-permute-start.28 = (f32[256,256]{1,0:T(8,128)S(1)}, f32[256,256]{1,0:T(8,128)S(1)}, u32[]{:S(2)}, u32[]{:S(2)}) collective-permute-start(f32[256,256]{1,0:T(8,128)S(1)} %get-tuple-element.141), channel_id=1, source_target_pairs={{0,8},{2,10},{3,0},{1,2},{4,12},{6,14},{7,4},{5,6},{8,9},{10,11},{... | collective-permute-start | bytes 786440 | tf_op jit(solution)/shard_map/ppermute | solution.py:519
  159.8 8.2 %collective-permute-done.27.refs_1_ = f32[256,256]{1,0:T(8,128)S(1)} collective-permute-done((f32[256,256]{1,0:T(8,128)S(1)}, f32[256,256]{1,0:T(8,128)S(1)}, u32[]{:S(2)}, u32[]{:S(2)}) %collective-permute-start.27) | collective-permute-done | bytes 262176 | tf_op jit(solution)/shard_map/ppermute | solution.py:519
  (79 shorter events, 39.0 us)
Async XLA Ops:
  4.4 17.9 %collective-permute-start = (f32[4,264,128]{2,1,0:T(8,128)}, f32[4,264,128]{2,1,0:T(8,128)}, u32[]{:S(2)}, u32[]{:S(2)}) collective-permute-start(f32[4,264,128]{2,1,0:T(8,128)} %get-tuple-element.76), channel_id=1, source_target_pairs={{0,4},{1,5},{2,6},{3,7},{4,0},{5,1},{6,2},{7,3},{8,12},{9,13},{10,... | collective-permute-start | bytes 1622024 | tf_op jit(solution)/shard_map/ppermute | solution.py:218
  8.0 14.3 %collective-permute-start.1 = (f32[512,128]{1,0:T(8,128)S(1)}, f32[512,128]{1,0:T(8,128)S(1)}, u32[]{:S(2)}, u32[]{:S(2)}) collective-permute-start(f32[512,128]{1,0:T(8,128)S(1)} %arrange.2), channel_id=1, source_target_pairs={{0,16},{1,17},{2,18},{3,19},{4,20},{5,21},{6,22},{7,23},{8,24},{9,... | collective-permute-start | bytes 786440 | tf_op jit(solution)/shard_map/ppermute | solution.py:218
  22.4 25.0 %collective-permute-start.3 = (f32[1024,128]{1,0:T(8,128)S(1)}, f32[1024,128]{1,0:T(8,128)S(1)}, u32[]{:S(2)}, u32[]{:S(2)}) collective-permute-start(f32[1024,128]{1,0:T(8,128)S(1)} %get-tuple-element.88), channel_id=1, source_target_pairs={{0,16},{1,17},{2,18},{3,19},{4,20},{5,21},{6,22},{7,23},{8,24},{9,... | collective-permute-start | bytes 1572872 | tf_op jit(solution)/shard_map/ppermute | solution.py:218
  22.8 27.5 %collective-permute-start.4 = (f32[2048,128]{1,0:T(8,128)S(1)}, f32[2048,128]{1,0:T(8,128)S(1)}, u32[]{:S(2)}, u32[]{:S(2)}) collective-permute-start(f32[2048,128]{1,0:T(8,128)S(1)} %get-tuple-element.89.refs_7_.refs_14_.refs_6_.refs_2_), channel_id=1, source_target_pairs={{0,4},{1,5},{2,6},{3,7},{4,0},{5,1},{6,2},{7,3},{8,12},{9,13},{10,... | collective-permute-start | bytes 3145736 | tf_op jit(solution)/shard_map/ppermute | solution.py:218
  24.3 26.0 %collective-permute-start.5 = (f32[2048,128]{1,0:T(8,128)S(1)}, f32[2048,128]{1,0:T(8,128)S(1)}, u32[]{:S(2)}, u32[]{:S(2)}) collective-permute-start(f32[2048,128]{1,0:T(8,128)S(1)} %get-tuple-element.90), channel_id=1, source_target_pairs={{0,1},{1,0},{2,3},{3,2},{4,5},{5,4},{6,7},{7,6},{8,9},{9,8},{10,11... | collective-permute-start | bytes 3145736 | tf_op jit(solution)/shard_map/ppermute | solution.py:218
  25.4 24.9 %collective-permute-start.2 = (f32[4,264,128]{2,1,0:T(8,128)S(1)}, f32[4,264,128]{2,1,0:T(8,128)S(1)}, u32[]{:S(2)}, u32[]{:S(2)}) collective-permute-start(f32[4,264,128]{2,1,0:T(8,128)S(1)} %add.19), channel_id=1, source_target_pairs={{0,8},{1,9},{2,10},{3,11},{4,12},{5,13},{6,14},{7,15},{8,0},{9,1},... | collective-permute-start | bytes 1622024 | tf_op jit(solution)/shard_map/ppermute | solution.py:218
  28.1 19.3 %collective-permute-start.6 = (f32[1024,128]{1,0:T(8,128)S(1)}, f32[1024,128]{1,0:T(8,128)S(1)}, u32[]{:S(2)}, u32[]{:S(2)}) collective-permute-start(f32[1024,128]{1,0:T(8,128)S(1)} %get-tuple-element.91), channel_id=1, source_target_pairs={{0,1},{1,0},{2,3},{3,2},{4,5},{5,4},{6,7},{7,6},{8,9},{9,8},{10,11... | collective-permute-start | bytes 1572872 | tf_op jit(solution)/shard_map/ppermute | solution.py:218
  50.3 30.6 %collective-permute-start.10 = (f32[2048,128]{1,0:T(8,128)S(1)}, f32[2048,128]{1,0:T(8,128)S(1)}, u32[]{:S(2)}, u32[]{:S(2)}) collective-permute-start(f32[2048,128]{1,0:T(8,128)S(1)} %collective-permute-done.5.refs_4_.refs_11_.refs_2_.refs_6_), channel_id=1, source_target_pairs={{0,4},{1,5},{2,6},{3,7},{4,0},{5,1},{6,2},{7,3},{8,12},{9,13},{10,... | collective-permute-start | bytes 3145736 | tf_op jit(solution)/shard_map/ppermute | solution.py:218
  60.3 13.3 %collective-permute-start.9 = (f32[2,264,128]{2,1,0:T(8,128)S(1)}, f32[2,264,128]{2,1,0:T(8,128)S(1)}, u32[]{:S(2)}, u32[]{:S(2)}) collective-permute-start(f32[2,264,128]{2,1,0:T(8,128)S(1)} %collective-permute-done.8), channel_id=1, source_target_pairs={{16,24},{17,25},{18,26},{19,27},{20,28},{21,29},{22,30},{23,31},{2... | collective-permute-start | bytes 811016 | tf_op jit(solution)/shard_map/ppermute | solution.py:218
  61.2 19.7 %collective-permute-start.11 = (f32[512,128]{1,0:T(8,128)S(1)}, f32[512,128]{1,0:T(8,128)S(1)}, u32[]{:S(2)}, u32[]{:S(2)}) collective-permute-start(f32[512,128]{1,0:T(8,128)S(1)} %collective-permute-done.1.refs_9_), channel_id=1, source_target_pairs={{0,4},{1,5},{2,6},{3,7},{4,0},{5,1},{6,2},{7,3},{8,12},{9,13},{10,... | collective-permute-start | bytes 786440 | tf_op jit(solution)/shard_map/ppermute | solution.py:218
  61.8 23.4 %collective-permute-start.13 = (f32[512,128]{1,0:T(8,128)S(1)}, f32[512,128]{1,0:T(8,128)S(1)}, u32[]{:S(2)}, u32[]{:S(2)}) collective-permute-start(f32[512,128]{1,0:T(8,128)S(1)} %get-tuple-element.112), channel_id=1, source_target_pairs={{0,16},{1,17},{2,18},{3,19},{4,20},{5,21},{6,22},{7,23},{8,24},{9,... | collective-permute-start | bytes 786440 | tf_op jit(solution)/shard_map/ppermute | solution.py:218
  81.1 26.0 %collective-permute-start.12 = (f32[4,264,128]{2,1,0:T(8,128)S(1)}, f32[4,264,128]{2,1,0:T(8,128)S(1)}, u32[]{:S(2)}, u32[]{:S(2)}) collective-permute-start(f32[4,264,128]{2,1,0:T(8,128)S(1)} %get-tuple-element.144), channel_id=1, source_target_pairs={{0,4},{1,5},{2,6},{3,7},{4,0},{5,1},{6,2},{7,3},{8,12},{9,13},{10,... | collective-permute-start | bytes 1622024 | tf_op jit(solution)/shard_map/ppermute | solution.py:218
  85.2 21.9 %collective-permute-start.14 = (f32[256,512]{1,0:T(8,128)S(1)}, f32[256,512]{1,0:T(8,128)S(1)}, u32[]{:S(2)}, u32[]{:S(2)}) collective-permute-start(f32[256,512]{1,0:T(8,128)S(1)} %mix.2.refs_0_), channel_id=1, source_target_pairs={{0,8},{1,9},{2,10},{3,11},{4,12},{5,13},{6,14},{7,15},{8,0},{9,1},... | collective-permute-start | bytes 1572872 | tf_op jit(solution)/shard_map/ppermute | solution.py:218
  85.2 23.3 %collective-permute-start.15 = (f32[256,512]{1,0:T(8,128)S(1)}, f32[256,512]{1,0:T(8,128)S(1)}, u32[]{:S(2)}, u32[]{:S(2)}) collective-permute-start(f32[256,512]{1,0:T(8,128)S(1)} %mix.2.refs_0_), channel_id=1, source_target_pairs={{0,2},{1,3},{2,0},{3,1},{4,6},{5,7},{6,4},{7,5},{8,10},{9,11},{10,... | collective-permute-start | bytes 1572872 | tf_op jit(solution)/shard_map/ppermute | solution.py:218
  86.7 24.9 %collective-permute-start.16 = (f32[1024,128]{1,0:T(8,128)S(1)}, f32[1024,128]{1,0:T(8,128)S(1)}, u32[]{:S(2)}, u32[]{:S(2)}) collective-permute-start(f32[1024,128]{1,0:T(8,128)S(1)} %collective-permute-done.6), channel_id=1, source_target_pairs={{0,16},{1,17},{2,18},{3,19},{4,20},{5,21},{6,22},{7,23},{8,24},{9,... | collective-permute-start | bytes 1572872 | tf_op jit(solution)/shard_map/ppermute | solution.py:218
  89.9 21.7 %collective-permute-start.17 = (f32[1024,128]{1,0:T(8,128)S(1)}, f32[1024,128]{1,0:T(8,128)S(1)}, u32[]{:S(2)}, u32[]{:S(2)}) collective-permute-start(f32[1024,128]{1,0:T(8,128)S(1)} %collective-permute-done.3.refs_16_.refs_8_), channel_id=1, source_target_pairs={{0,4},{1,5},{2,6},{3,7},{4,0},{5,1},{6,2},{7,3},{8,12},{9,13},{10,... | collective-permute-start | bytes 1572872 | tf_op jit(solution)/shard_map/ppermute | solution.py:218
  111.6 24.0 %collective-permute-start.19 = (f32[512,512]{1,0:T(8,128)S(1)}, f32[512,512]{1,0:T(8,128)S(1)}, u32[]{:S(2)}, u32[]{:S(2)}) collective-permute-start(f32[512,512]{1,0:T(8,128)S(1)} %get-tuple-element.121), channel_id=1, source_target_pairs={{0,2},{1,3},{2,0},{3,1},{4,6},{5,7},{6,4},{7,5},{8,10},{9,11},{10,... | collective-permute-start | bytes 3145736 | tf_op jit(solution)/shard_map/ppermute | solution.py:218
  112.1 21.8 %collective-permute-start.18 = (f32[256,512]{1,0:T(8,128)S(1)}, f32[256,512]{1,0:T(8,128)S(1)}, u32[]{:S(2)}, u32[]{:S(2)}) collective-permute-start(f32[256,512]{1,0:T(8,128)S(1)} %get-tuple-element.120.refs_0_), channel_id=1, source_target_pairs={{0,8},{1,9},{2,10},{3,11},{4,12},{5,13},{6,14},{7,15},{8,0},{9,1},... | collective-permute-start | bytes 1572872 | tf_op jit(solution)/shard_map/ppermute | solution.py:218
  112.1 23.5 %collective-permute-start.20 = (f32[1024,128]{1,0:T(8,128)S(1)}, f32[1024,128]{1,0:T(8,128)S(1)}, u32[]{:S(2)}, u32[]{:S(2)}) collective-permute-start(f32[1024,128]{1,0:T(8,128)S(1)} %collective-permute-done.7), channel_id=1, source_target_pairs={{0,16},{1,17},{2,18},{3,19},{4,20},{5,21},{6,22},{7,23},{8,24},{9,... | collective-permute-start | bytes 1572872 | tf_op jit(solution)/shard_map/ppermute | solution.py:218
  114.8 20.8 %collective-permute-start.22 = (f32[1024,128]{1,0:T(8,128)S(1)}, f32[1024,128]{1,0:T(8,128)S(1)}, u32[]{:S(2)}, u32[]{:S(2)}) collective-permute-start(f32[1024,128]{1,0:T(8,128)S(1)} %collective-permute-done.16.refs_6_.refs_13_), channel_id=1, source_target_pairs={{0,4},{1,5},{2,6},{3,7},{4,0},{5,1},{6,2},{7,3},{8,12},{9,13},{10,... | collective-permute-start | bytes 1572872 | tf_op jit(solution)/shard_map/ppermute | solution.py:218
  116.3 15.1 %collective-permute-start.21 = (f32[512,128]{1,0:T(8,128)S(1)}, f32[512,128]{1,0:T(8,128)S(1)}, u32[]{:S(2)}, u32[]{:S(2)}) collective-permute-start(f32[512,128]{1,0:T(8,128)S(1)} %collective-permute-done.13.refs_4_), channel_id=1, source_target_pairs={{0,4},{1,5},{2,6},{3,7},{4,0},{5,1},{6,2},{7,3},{8,12},{9,13},{10,... | collective-permute-start | bytes 786440 | tf_op jit(solution)/shard_map/ppermute | solution.py:218
  135.9 11.3 %collective-permute-start.24 = (f32[1024,128]{1,0:T(8,128)S(1)}, f32[1024,128]{1,0:T(8,128)S(1)}, u32[]{:S(2)}, u32[]{:S(2)}) collective-permute-start(f32[1024,128]{1,0:T(8,128)S(1)} %collective-permute-done.20.refs_4_.refs_8_), channel_id=1, source_target_pairs={{0,4},{1,5},{2,6},{3,7},{4,0},{5,1},{6,2},{7,3},{8,12},{9,13},{10,... | collective-permute-start | bytes 1572872 | tf_op jit(solution)/shard_map/ppermute | solution.py:218
  153.2 14.8 %collective-permute-start.27 = (f32[256,256]{1,0:T(8,128)S(1)}, f32[256,256]{1,0:T(8,128)S(1)}, u32[]{:S(2)}, u32[]{:S(2)}) collective-permute-start(f32[256,256]{1,0:T(8,128)S(1)} %get-tuple-element.140), channel_id=1, source_target_pairs={{0,2},{2,0},{3,10},{1,8},{4,6},{6,4},{7,14},{5,12},{8,3},{10,1},{1... | collective-permute-start | bytes 786440 | tf_op jit(solution)/shard_map/ppermute | solution.py:519
  156.5 13.4 %collective-permute-start.28 = (f32[256,256]{1,0:T(8,128)S(1)}, f32[256,256]{1,0:T(8,128)S(1)}, u32[]{:S(2)}, u32[]{:S(2)}) collective-permute-start(f32[256,256]{1,0:T(8,128)S(1)} %get-tuple-element.141), channel_id=1, source_target_pairs={{0,8},{2,10},{3,0},{1,2},{4,12},{6,14},{7,4},{5,6},{8,9},{10,11},{... | collective-permute-start | bytes 786440 | tf_op jit(solution)/shard_map/ppermute | solution.py:519
  (17 other events, 132.4 us)
